TPU v7x, 128 devices: a whole 4x4x4 slice. The times are simulated.
128 devices in a mesh: img: 8 (over y, x_lo), seq: 16 (over z, x_hi, core).
Axes of the slice: x: 4 (x_hi: 2, x_lo: 2; x = x_hi * 2 + x_lo), y: 4, z: 4, core: 2. Of those that a mesh axis runs over, the one named last changes fastest.
Arguments:
- image_query: bfloat16 [8, 2048, 1280], P('img', 'seq'), may hold values from -7 to 7
- image_key: bfloat16 [8, 2048, 1280], P('img', 'seq'), may hold values from -7 to 7
- image_value: bfloat16 [8, 2048, 1280], P('img', 'seq'), may hold values from -3 to 3
- image_output: bfloat16 [8, 2048, 1280], P('img', 'seq'), may hold values from -0.875 to 0.875
- output_grad: bfloat16 [8, 2048, 2432], P('img', 'seq'), may hold values from -48 to 48
- image_logsum: float32 [8, 2048, 20], P('img', 'seq'), may hold values from 8 to 9
- text_query: bfloat16 [8, 333, 1280], P('img'), may hold values from -7 to 7
- text_key: bfloat16 [8, 333, 1280], P('img'), may hold values from -7 to 7
- text_value: bfloat16 [8, 333, 1280], P('img'), may hold values from -3 to 3
- text_output: bfloat16 [8, 333, 1280], P('img'), may hold values from -0.875 to 0.875
- text_grad: bfloat16 [8, 333, 1280], P('img'), may hold values from -48 to 48
- text_logsum: float32 [8, 333, 20], P('img'), may hold values from 8 to 9
- out_weight: bfloat16 [2432, 1280], replicated, may hold values from -0.125 to 0.125
Outputs:
- query_grad: bfloat16 [8, 2048, 1280], P('img', 'seq')
- key_grad: bfloat16 [8, 2048, 1280], P('img', 'seq')
- value_grad: bfloat16 [8, 2048, 1280], P('img', 'seq')
- text_query_grad: bfloat16 [8, 333, 1280], P('img')
- text_key_grad: bfloat16 [8, 333, 1280], P('img')
- text_value_grad: bfloat16 [8, 333, 1280], P('img')
- weight_grad: float32 [2432, 1280], P('seq')
All inputs are finite; a program needn't handle non-finite values.
Results may differ from a plain program's by a relative error of at most 0.017.
Values may be sent and summed in bfloat16 or wider, within the bound.
No kernel may reach another device: no remote copies, remote signals or barrier semaphores. Data moves between devices by JAX's collectives and lax.ppermute only.
A program may use at most 192 MiB of HBM per device.

v0:
```python
import math

import jax
import jax.numpy as jnp
from jax import lax
from jax.sharding import Mesh
from jax.sharding import PartitionSpec as P

SEQ = ("seq_0", "seq_1", "seq_2")


def in_one_piece(arrays, axis, dim, along):
    widths = [a.shape[along] for a in arrays]
    both = jnp.concatenate(arrays, axis=along)
    out = lax.all_gather(both, axis, axis=dim, tiled=True)
    return tuple(jnp.split(out, [sum(widths[:k]) for k in range(1, len(widths))], axis=along))


def in_one_piece_2(arrays, axis, dim, along):
    widths = [a.shape[along] for a in arrays]
    both = jnp.concatenate(arrays, axis=along)
    out = lax.psum_scatter(both, axis, scatter_dimension=dim, tiled=True)
    return tuple(jnp.split(out, [sum(widths[:k]) for k in range(1, len(widths))], axis=along))


def cut_along(array, dim, devices):
    before, after = (array.shape[:dim], array.shape[dim + 1 :])
    return jnp.moveaxis(array.reshape(*before, devices, -1, *after), dim, 0)


def sum_by_chip(array, chips, core, dim):
    sizes = (lax.axis_size(chips), lax.axis_size(core))
    blocks = cut_along(array, dim, sizes[0] * sizes[1])
    inside = blocks.shape[1:]
    blocks = blocks.reshape(*sizes, *inside).swapaxes(0, 1).reshape(-1, *inside)
    blocks = lax.psum_scatter(blocks, core, scatter_dimension=0, tiled=True)
    return lax.psum_scatter(blocks, chips, scatter_dimension=0, tiled=True)[0]


def from_everyone(array, axis):
    devices = lax.axis_size(axis)
    return lax.all_to_all(
        jnp.broadcast_to(array[None], (devices, *array.shape)), axis, 0, 0, tiled=True
    )


def of_everyone(array, axis):
    return from_everyone(array, axis).astype(jnp.float32).sum(axis=0)


def row_dot(grads_out, outputs, head_count):
    product = grads_out.astype(jnp.float32) * outputs.astype(jnp.float32)
    return product.reshape(product.shape[0], head_count, -1).sum(axis=-1)


def score_parts(queries, grads_out, log_sum, row_dots, key_rows, value_rows):
    head_count = log_sum.shape[1]
    query_count = queries.shape[0]
    key_count = key_rows.shape[0]
    head_width = queries.shape[1] // head_count
    scaling = head_width ** (-0.5)
    query_heads = queries.reshape(query_count, head_count, head_width)
    grad_heads = grads_out.reshape(query_count, head_count, head_width)
    key_heads = key_rows.reshape(key_count, head_count, head_width)
    value_heads = value_rows.reshape(key_count, head_count, head_width)
    scores = (
        jnp.einsum("qhe,khe->hqk", query_heads, key_heads, preferred_element_type=jnp.float32)
        * scaling
    )
    weights = jnp.exp(scores - log_sum.T[:, :, None])
    grad_weights = jnp.einsum(
        "qhe,khe->hqk", grad_heads, value_heads, preferred_element_type=jnp.float32
    )
    grad_scores = weights * (grad_weights - row_dots.T[:, :, None])
    return (
        query_heads,
        grad_heads,
        key_heads,
        weights.astype(jnp.bfloat16),
        grad_scores.astype(jnp.bfloat16),
        scaling,
    )


def pair_grads(queries, grads_out, log_sum, row_dots, key_rows, value_rows):
    query_heads, grad_heads, key_heads, weights_low, scores_low, scaling = score_parts(
        queries, grads_out, log_sum, row_dots, key_rows, value_rows
    )
    query_part = (
        jnp.einsum("hqk,khe->qhe", scores_low, key_heads, preferred_element_type=jnp.float32)
        * scaling
    )
    key_part = (
        jnp.einsum("hqk,qhe->khe", scores_low, query_heads, preferred_element_type=jnp.float32)
        * scaling
    )
    value_part = jnp.einsum(
        "hqk,qhe->khe", weights_low, grad_heads, preferred_element_type=jnp.float32
    )
    return (
        query_part.reshape(queries.shape[0], -1),
        key_part.reshape(key_rows.shape[0], -1),
        value_part.reshape(key_rows.shape[0], -1),
    )


def shards(
    image_query,
    image_key,
    image_value,
    image_output,
    output_grad,
    image_logsum,
    text_query,
    text_key,
    text_value,
    text_output,
    text_grad,
    text_logsum,
    out_weight,
):
    head_count = image_logsum.shape[-1]
    collected = ([], [], [], [], [], [])
    number = 0
    queries = image_query[number]
    key_rows = image_key[number]
    value_rows = image_value[number]
    log_sum = image_logsum[number]
    image_dout = jnp.dot(
        output_grad[number], out_weight, preferred_element_type=jnp.float32
    ).astype(jnp.bfloat16)
    image_dots = row_dot(image_dout, image_output[number], head_count)
    text_queries = text_query[number]
    text_keys = text_key[number]
    text_values = text_value[number]
    text_dout = text_grad[number]
    text_lsum = text_logsum[number]
    text_dots = row_dot(text_dout, text_output[number], head_count)
    query_from_text, tkey_image, tvalue_image = pair_grads(
        queries, image_dout, log_sum, image_dots, text_keys, text_values
    )
    tquery_image, key_from_text, value_from_text = pair_grads(
        text_queries, text_dout, text_lsum, text_dots, key_rows, value_rows
    )
    tquery_self, tkey_self, tvalue_self = pair_grads(
        text_queries, text_dout, text_lsum, text_dots, text_keys, text_values
    )
    text_sums = (
        lax.psum(tquery_image.astype(jnp.bfloat16), SEQ).astype(jnp.float32),
        lax.psum(tkey_image.astype(jnp.bfloat16), SEQ).astype(jnp.float32),
        lax.psum(tvalue_image.astype(jnp.bfloat16), SEQ).astype(jnp.float32),
    )
    local_rows, feature = queries.shape
    query_acc = jnp.zeros((local_rows, feature), jnp.float32)
    key_piece, value_piece = in_one_piece((key_rows, value_rows), SEQ, 0, 1)
    row_span = key_piece.shape[0]
    block_rows = math.gcd(row_span, 512)
    block_count = row_span // block_rows

    def key_step(running, section):
        key_block, value_block = section
        query_part, key_part, value_part = pair_grads(
            queries, image_dout, log_sum, image_dots, key_block, value_block
        )
        return (running + query_part, (key_part, value_part))

    query_acc, (key_blocks, value_blocks) = lax.scan(
        key_step,
        query_acc,
        (
            key_piece.reshape(block_count, block_rows, feature),
            value_piece.reshape(block_count, block_rows, feature),
        ),
    )
    key_all = key_blocks.reshape(row_span, feature)
    value_all = value_blocks.reshape(row_span, feature)
    query_image, key_all, value_all = (query_acc, key_all, value_all)
    key_image, value_image = tuple(
        (
            part.astype(jnp.float32)
            for part in in_one_piece_2(
                (key_all.astype(jnp.bfloat16), value_all.astype(jnp.bfloat16)), SEQ, 0, 1
            )
        )
    )
    collected[0].append((query_image + query_from_text).astype(jnp.bfloat16))
    collected[1].append((key_image + key_from_text).astype(jnp.bfloat16))
    collected[2].append((value_image + value_from_text).astype(jnp.bfloat16))
    collected[3].append((text_sums[0] + tquery_self).astype(jnp.bfloat16))
    collected[4].append((text_sums[1] + tkey_self).astype(jnp.bfloat16))
    collected[5].append((text_sums[2] + tvalue_self).astype(jnp.bfloat16))
    feature = image_output.shape[2]
    shard_rows = out_weight.shape[0] // lax.axis_size(SEQ)
    running = jnp.zeros(
        (shard_rows * lax.axis_size(("seq_0", "seq_1")) * lax.axis_size("seq_2"), feature),
        jnp.float32,
    )
    number = 0
    grad_part = output_grad[number]
    running = lax.dot_general(
        grad_part,
        image_output[number],
        (((0,), (0,)), ((), ())),
        preferred_element_type=jnp.float32,
    )
    weight_shard = sum_by_chip(running.astype(jnp.bfloat16), ("seq_0", "seq_1"), "seq_2", 0).astype(
        jnp.float32
    )
    weight_grad = of_everyone(weight_shard.astype(jnp.bfloat16), "img").astype(jnp.float32)
    return (
        jnp.stack(collected[0], 0),
        jnp.stack(collected[1], 0),
        jnp.stack(collected[2], 0),
        jnp.stack(collected[3], 0),
        jnp.stack(collected[4], 0),
        jnp.stack(collected[5], 0),
        weight_grad,
    )


def solution(mesh):
    finer = Mesh(
        mesh.devices.reshape(mesh.shape["img"], 4, 2, 2), ("img", "seq_0", "seq_1", "seq_2")
    )
    return jax.shard_map(
        shards,
        mesh=finer,
        in_specs=(
            P("img", SEQ, None),
            P("img", SEQ, None),
            P("img", SEQ, None),
            P("img", SEQ, None),
            P("img", SEQ, None),
            P("img", SEQ, None),
            P("img", None, None),
            P("img", None, None),
            P("img", None, None),
            P("img", None, None),
            P("img", None, None),
            P("img", None, None),
            P(),
        ),
        out_specs=(
            P("img", SEQ, None),
            P("img", SEQ, None),
            P("img", SEQ, None),
            P("img", None, None),
            P("img", None, None),
            P("img", None, None),
            P(SEQ, None),
        ),
        check_vma=False,
    )
```

profile of v0, /device:TPU:1, one launch (start us, length us, event | category | flops | bytes accessed | tf_op | source)
XLA Modules:
  0.0 377.7 jit_solution(16087514064878817874)
XLA Ops:
  9.1 2.8 convolution_convert_fusion
  11.9 3.0 copy.108
  16.9 18.8 %reduce-scatter.6.cloned.1.call-done = bf16[8,152,1280]{2,1,0:T(8,128)(2,1)} async-done(((bf16[16,152,1280]{2,1,0:T(8,128)(2,1)}), bf16[8,152,1280]{2,1,0:T(8,128)(2,1)}) %reduce-scatter.6.cloned.1.call-update) | async-done | bytes 3112976 | tf_op jit(solution)/shard_map/reduce_scatter | solution.py:36
  37.2 3.8 %convert_multiply_fusion.1 = (f32[128,1280]{1,0:T(8,128)S(1)}, bf16[128,1280]{1,0:T(8,128)(2,1)S(1)}) fusion(bf16[1,128,1280]{2,1,0:T(8,128)(2,1)S(1)} %copy-done.23, bf16[2432,1280]{1,0:T(8,128)(2,1)} %param.27, bf16[1,128,2432]{2,1,0:T(8,128)(2,1)S(1)} %copy-done), kind=kOutput, calls=%fused_computation.55 | convolution fusion | flops 797573120 | bytes 8159232 | tf_op jit(solution)/shard_map/dot_general | solution.py:129
  42.3 2.3 copy.88
  44.6 2.2 copy.90
  50.3 2.6 copy.99
  55.2 2.8 multiply_convert_fusion.2
  60.8 2.3 copy.102
  69.3 2.7 fusion.22
  73.6 30.8 %all-gather.2.cloned.1.call-done = bf16[2048,2560]{1,0:T(8,128)(2,1)} async-done(((bf16[128,2560]{1,0:T(8,128)(2,1)}), bf16[2048,2560]{1,0:T(8,128)(2,1)}) %all-gather.2.cloned.1.call-update) | async-done | bytes 10485776 | tf_op jit(solution)/shard_map/all_gather | solution.py:15
  104.4 9.0 %fusion.37 = (bf16[2048,1280]{1,0:T(8,128)(2,1)}, bf16[2048,1280]{1,0:T(8,128)(2,1)}) fusion(bf16[2048,2560]{1,0:T(8,128)(2,1)} %all-gather.2.cloned.1.call-done), kind=kLoop, calls=%fused_computation.68 | loop fusion | bytes 20971520 | tf_op jit(solution)/shard_map/split | solution.py:16
  113.3 103.2 %while.15 = (s32[]{:T(128)}, f32[128,1280]{0,1:T(8,128)}, bf16[4,512,1280]{1,2,0:T(8,128)(2,1)}, bf16[4,512,1280]{1,2,0:T(8,128)(2,1)}, bf16[4,512,1280]{2,1,0:T...) while((s32[]{:T(128)}, f32[128,1280]{0,1:T(8,128)}, ...), condition=%wide.region_2.0_spmd.clone, body=%wide.region_1.0_spmd.clone.sunk | while | flops 851148800 | bytes 62945536 | solution.py:167
  116.1 4.4 %fusion.101 = f32[20,512,128]{2,1,0:T(8,128)} fusion(bf16[512,20,64]{0,2,1:T(8,128)(2,1)S(1)} %bitcast.175, bf16[128,20,64]{0,2,1:T(8,128)(2,1)} %bitcast.186), kind=kOutput, calls=%fused_computation.69.clone.1 | convolution fusion | flops 167772160 | bytes 6881280 | tf_op jit(solution)/shard_map/while/body/eval_jaxpr/qhe,khe->hqk/dot_general | solution.py:67
  123.4 4.6 %multiply_convert_fusion.7 = bf16[20,512,128]{2,1,0:T(8,128)(2,1)S(1)} fusion(f32[20,512,128]{2,1,0:T(8,128)} %fusion.101, f32[20,128]{1,0:T(8,128)S(1)} %bitcast.235, f32[20,128]{1,0:T(8,128)S(1)} %bitcast.225, bf16[512,20,64]{0,2,1:T(8,128)(2,1)} %bitcast.179, bf16[128,20,64]{0,2,1:T(8,128)(2,1)S(1)} %bitcast.182), kind=kOutput, calls=%fused_computation.clone.1 | convolution fusion | flops 174325760 | bytes 9523200 | tf_op jit(solution)/shard_map/while/body/eval_jaxpr/qhe,khe->hqk/dot_general | solution.py:71
  131.6 3.6 fusion.102
  141.7 4.4 %fusion.101 = f32[20,512,128]{2,1,0:T(8,128)} fusion(bf16[512,20,64]{0,2,1:T(8,128)(2,1)S(1)} %bitcast.175, bf16[128,20,64]{0,2,1:T(8,128)(2,1)} %bitcast.186), kind=kOutput, calls=%fused_computation.69.clone.1 | convolution fusion | flops 167772160 | bytes 6881280 | tf_op jit(solution)/shard_map/while/body/eval_jaxpr/qhe,khe->hqk/dot_general | solution.py:67
  149.0 4.7 %multiply_convert_fusion.7 = bf16[20,512,128]{2,1,0:T(8,128)(2,1)S(1)} fusion(f32[20,512,128]{2,1,0:T(8,128)} %fusion.101, f32[20,128]{1,0:T(8,128)S(1)} %bitcast.235, f32[20,128]{1,0:T(8,128)S(1)} %bitcast.225, bf16[512,20,64]{0,2,1:T(8,128)(2,1)} %bitcast.179, bf16[128,20,64]{0,2,1:T(8,128)(2,1)S(1)} %bitcast.182), kind=kOutput, calls=%fused_computation.clone.1 | convolution fusion | flops 174325760 | bytes 9523200 | tf_op jit(solution)/shard_map/while/body/eval_jaxpr/qhe,khe->hqk/dot_general | solution.py:71
  155.2 2.2 bitcast_add_fusion.2
  157.4 3.7 fusion.102
  167.6 4.4 %fusion.101 = f32[20,512,128]{2,1,0:T(8,128)} fusion(bf16[512,20,64]{0,2,1:T(8,128)(2,1)S(1)} %bitcast.175, bf16[128,20,64]{0,2,1:T(8,128)(2,1)} %bitcast.186), kind=kOutput, calls=%fused_computation.69.clone.1 | convolution fusion | flops 167772160 | bytes 6881280 | tf_op jit(solution)/shard_map/while/body/eval_jaxpr/qhe,khe->hqk/dot_general | solution.py:67
  174.8 4.7 %multiply_convert_fusion.7 = bf16[20,512,128]{2,1,0:T(8,128)(2,1)S(1)} fusion(f32[20,512,128]{2,1,0:T(8,128)} %fusion.101, f32[20,128]{1,0:T(8,128)S(1)} %bitcast.235, f32[20,128]{1,0:T(8,128)S(1)} %bitcast.225, bf16[512,20,64]{0,2,1:T(8,128)(2,1)} %bitcast.179, bf16[128,20,64]{0,2,1:T(8,128)(2,1)S(1)} %bitcast.182), kind=kOutput, calls=%fused_computation.clone.1 | convolution fusion | flops 174325760 | bytes 9523200 | tf_op jit(solution)/shard_map/while/body/eval_jaxpr/qhe,khe->hqk/dot_general | solution.py:71
  181.0 2.2 bitcast_add_fusion.2
  183.2 3.6 fusion.102
  193.5 4.4 %fusion.101 = f32[20,512,128]{2,1,0:T(8,128)} fusion(bf16[512,20,64]{0,2,1:T(8,128)(2,1)S(1)} %bitcast.175, bf16[128,20,64]{0,2,1:T(8,128)(2,1)} %bitcast.186), kind=kOutput, calls=%fused_computation.69.clone.1 | convolution fusion | flops 167772160 | bytes 6881280 | tf_op jit(solution)/shard_map/while/body/eval_jaxpr/qhe,khe->hqk/dot_general | solution.py:67
  200.8 4.7 %multiply_convert_fusion.7 = bf16[20,512,128]{2,1,0:T(8,128)(2,1)S(1)} fusion(f32[20,512,128]{2,1,0:T(8,128)} %fusion.101, f32[20,128]{1,0:T(8,128)S(1)} %bitcast.235, f32[20,128]{1,0:T(8,128)S(1)} %bitcast.225, bf16[512,20,64]{0,2,1:T(8,128)(2,1)} %bitcast.179, bf16[128,20,64]{0,2,1:T(8,128)(2,1)S(1)} %bitcast.182), kind=kOutput, calls=%fused_computation.clone.1 | convolution fusion | flops 174325760 | bytes 9523200 | tf_op jit(solution)/shard_map/while/body/eval_jaxpr/qhe,khe->hqk/dot_general | solution.py:71
  206.9 2.2 bitcast_add_fusion.2
  209.1 3.7 fusion.102
  216.5 7.9 %copy.94 = bf16[4,512,1280]{2,1,0:T(8,128)(2,1)} copy(bf16[4,512,1280]{1,2,0:T(8,128)(2,1)} %get-tuple-element.63) | data formatting | bytes 10485760 | tf_op jit(solution)/shard_map/convert_element_type | solution.py:182
  224.4 7.8 %copy.93 = bf16[4,512,1280]{2,1,0:T(8,128)(2,1)} copy(bf16[4,512,1280]{1,2,0:T(8,128)(2,1)} %get-tuple-element.62) | data formatting | bytes 10485760 | tf_op jit(solution)/shard_map/convert_element_type | solution.py:182
  232.2 9.6 %pad_maximum_fusion = bf16[2048,2560]{1,0:T(8,128)(2,1)} fusion(bf16[2048,1280]{1,0:T(8,128)(2,1)} %bitcast.205, bf16[2048,1280]{1,0:T(8,128)(2,1)} %bitcast.206), kind=kLoop, calls=%fused_computation.15 | loop fusion | flops 20971520 | bytes 20971520 | tf_op jit(solution)/shard_map/concatenate | solution.py:21
  246.2 4.4 %fusion.14 = f32[20,128,64]{1,2,0:T(8,128)} fusion(bf16[333,20,64]{0,2,1:T(8,128)(2,1)S(1)} %bitcast.191, f32[20,333,128]{2,1,0:T(8,128)} %copy-done.9, f32[20,333]{1,0:T(8,128)S(1)} %bitcast.231), kind=kOutput, calls=%fused_computation.34 | convolution fusion | flops 111674880 | bytes 4944400 | tf_op jit(solution)/shard_map/hqk,qhe->khe/dot_general | solution.py:97
  252.1 3.0 fusion.41
  255.1 4.2 %multiply_convert_fusion.1 = bf16[20,333,333]{2,1,0:T(8,128)(2,1)S(1)} fusion(f32[20,333,333]{2,1,0:T(8,128)S(1)} %fusion.41, f32[20,333]{1,0:T(8,128)S(1)} %bitcast.238, f32[20,333]{1,0:T(8,128)S(1)} %bitcast.232, bf16[333,20,64]{0,2,1:T(8,128)(2,1)S(1)} %bitcast.192, bf16[333,20,64]{0,2,1:T(8,128)(2,1)S(1)} %bitcast.208), kind=kOutput, calls=%fused_computation.16 | convolution fusion | flops 294964768 | bytes 15064920 | tf_op jit(solution)/shard_map/qhe,khe->hqk/dot_general | solution.py:71
  259.8 2.4 convolution_multiply_fusion.2
  262.3 3.0 convolution_multiply_fusion.3
  265.2 2.8 broadcast_in_dim.28
  268.1 4.5 %all-to-all-start = ((bf16[8,152,1280]{2,1,0:T(8,128)(2,1)}), bf16[8,152,1280]{2,1,0:T(8,128)(2,1)}, u32[]{:S(2)}, u32[]{:S(2)}) async-start(bf16[8,152,1280]{2,1,0:T(8,128)(2,1)} %broadcast_in_dim.28), calls=%async_computation.3 | async-start | bytes 6225920 | tf_op jit(solution)/shard_map/all_to_all | solution.py:42
  272.6 2.7 convolution_multiply_fusion.4
  275.3 2.2 copy.100
  277.5 3.3 copy.103
  280.8 2.8 copy.105
  283.7 6.1 %fusion.7 = f32[20,333,64]{1,2,0:T(8,128)} fusion(bf16[333,20,64]{0,2,1:T(8,128)(2,1)S(1)} %bitcast.193, f32[20,333,333]{2,1,0:T(8,128)} %copy-done.4, f32[20,333]{1,0:T(8,128)S(1)} %bitcast.233), kind=kOutput, calls=%fused_computation.20 | convolution fusion | flops 290529184 | bytes 11455200 | tf_op jit(solution)/shard_map/hqk,qhe->khe/dot_general | solution.py:97
  291.7 2.4 fusion.27
  294.1 3.7 fusion.25
  300.8 25.8 %all-to-all-done = bf16[8,152,1280]{2,1,0:T(8,128)(2,1)} async-done(((bf16[8,152,1280]{2,1,0:T(8,128)(2,1)}), bf16[8,152,1280]{2,1,0:T(8,128)(2,1)}, u32[]{:S(2)}, u32[]{:S(2)}) %all-to-all-start) | async-done | bytes 3112992 | tf_op jit(solution)/shard_map/all_to_all | solution.py:42
  326.6 3.2 convert_reduce_fusion
  329.8 38.8 %reduce-scatter.4.cloned.1.call-done = bf16[128,2560]{1,0:T(8,128)(2,1)} async-done(((bf16[2048,2560]{1,0:T(8,128)(2,1)}), bf16[128,2560]{1,0:T(8,128)(2,1)}) %reduce-scatter.4.cloned.1.call-update) | async-done | bytes 655376 | tf_op jit(solution)/shard_map/reduce_scatter | solution.py:22
  (158 shorter events, 80.6 us)
Async XLA Ops:
  8.0 1.1 copy-start
  8.0 27.7 %reduce-scatter.6.cloned.1.call-start = ((), (), s32[]{:S(2)}) async-start(), calls=%async_computation.6 | async-start | bytes 9338880 | tf_op jit(solution)/shard_map/reduce_scatter | solution.py:36
  14.9 1.0 copy-start.25
  14.9 1.1 copy-start.26
  14.9 22.0 %copy-start.29 = (bf16[1,128,1280]{2,1,0:T(8,128)(2,1)S(1)}, bf16[1,128,1280]{2,1,0:T(8,128)(2,1)}, u32[]{:S(2)}) copy-start(bf16[1,128,1280]{2,1,0:T(8,128)(2,1)} %param.15) | copy-start | bytes 983044
  14.9 89.4 %all-gather.2.cloned.1.call-start = ((), (), s32[]{:S(2)}) async-start(), calls=%async_computation.4 | async-start | bytes 11141120 | tf_op jit(solution)/shard_map/all_gather | solution.py:15
  16.0 21.2 %copy-start.31 = (f32[1,128,20]{1,0,2:T(1,128)S(1)}, f32[1,128,20]{1,0,2:T(1,128)}, u32[]{:S(2)}) copy-start(f32[1,128,20]{1,0,2:T(1,128)} %param.20) | copy-start | bytes 30724
  16.0 21.2 %copy-start.23 = (bf16[1,128,1280]{2,1,0:T(8,128)(2,1)S(1)}, bf16[1,128,1280]{2,1,0:T(8,128)(2,1)}, u32[]{:S(2)}) copy-start(bf16[1,128,1280]{2,1,0:T(8,128)(2,1)} %param.18) | copy-start | bytes 983044
  16.9 248.4 %reduce-scatter.8.cloned.1.call-start = ((), (), s32[]{:S(2)}) async-start(), calls=%async_computation.7 | async-start | bytes 3502080 | tf_op jit(solution)/shard_map/reduce_scatter | solution.py:37
  35.8 255.9 %all-reduce.3.cloned.1.call-start = ((), (), s32[]{:S(2)}) async-start(), calls=%async_computation.8 | async-start | bytes 5160960 | tf_op jit(solution)/shard_map/psum | solution.py:149
  42.3 8.0 %copy-start.30 = (f32[1,333,20]{1,0,2:T(1,128)S(1)}, f32[1,333,20]{1,0,2:T(1,128)}, u32[]{:S(2)}) copy-start(f32[1,333,20]{1,0,2:T(1,128)} %param.26) | copy-start | bytes 79924
  48.3 6.8 %copy-start.7 = (bf16[1,333,1280]{1,2,0:T(8,128)(2,1)}, bf16[1,333,1280]{1,2,0:T(8,128)(2,1)S(1)}, u32[]{:S(2)}) copy-start(bf16[1,333,1280]{1,2,0:T(8,128)(2,1)S(1)} %copy.97) | copy-start | bytes 2557444
  50.2 4.9 %copy-start.11 = (bf16[1,333,1280]{1,2,0:T(8,128)(2,1)}, bf16[1,333,1280]{1,2,0:T(8,128)(2,1)S(1)}, u32[]{:S(2)}) copy-start(bf16[1,333,1280]{1,2,0:T(8,128)(2,1)S(1)} %copy.95) | copy-start | bytes 2557444
  52.8 2.3 copy-start.24
  55.1 5.6 %copy-start.9 = (f32[20,333,128]{2,1,0:T(8,128)}, f32[20,333,128]{2,1,0:T(8,128)S(1)}, u32[]{:S(2)}) copy-start(f32[20,333,128]{2,1,0:T(8,128)S(1)} %fusion.40) | copy-start | bytes 10229764
  58.0 1.2 copy-start.17
  59.2 5.1 %copy-start.13 = (bf16[1,333,1280]{1,2,0:T(8,128)(2,1)S(1)}, bf16[1,333,1280]{1,2,0:T(8,128)(2,1)}, u32[]{:S(2)}) copy-start(bf16[1,333,1280]{1,2,0:T(8,128)(2,1)} %copy.88) | copy-start | bytes 2557444
  60.8 4.2 %copy-start.19 = (bf16[1,333,1280]{1,2,0:T(8,128)(2,1)S(1)}, bf16[1,333,1280]{1,2,0:T(8,128)(2,1)}, u32[]{:S(2)}) copy-start(bf16[1,333,1280]{1,2,0:T(8,128)(2,1)} %copy.90) | copy-start | bytes 2557444
  64.9 3.1 copy-start.10
  66.2 1.2 copy-start.18
  73.3 295.3 %reduce-scatter.4.cloned.1.call-start = ((), (), s32[]{:S(2)}) async-start(), calls=%async_computation.5 | async-start | bytes 11141120 | tf_op jit(solution)/shard_map/reduce_scatter | solution.py:22
  116.1 4.4 %copy-start.2 = (bf16[1,512,1280]{1,2,0:T(8,128)(2,1)}, bf16[1,512,1280]{1,2,0:T(8,128)(2,1)S(1)}, u32[]{:S(2)}) copy-start(bf16[1,512,1280]{1,2,0:T(8,128)(2,1)S(1)} %copy.120) | copy-start | bytes 3932164 | tf_op jit(solution)/shard_map/while
  123.4 4.7 %copy-start.3 = (bf16[1,512,1280]{1,2,0:T(8,128)(2,1)S(1)}, bf16[1,512,1280]{1,2,0:T(8,128)(2,1)}, u32[]{:S(2)}) copy-start(bf16[1,512,1280]{1,2,0:T(8,128)(2,1)} %copy-done.2) | copy-start | bytes 3932164 | tf_op jit(solution)/shard_map/while
  137.2 1.7 copy-start.6
  138.9 0.7 copy-start.5
  141.7 4.4 %copy-start.2 = (bf16[1,512,1280]{1,2,0:T(8,128)(2,1)}, bf16[1,512,1280]{1,2,0:T(8,128)(2,1)S(1)}, u32[]{:S(2)}) copy-start(bf16[1,512,1280]{1,2,0:T(8,128)(2,1)S(1)} %copy.120) | copy-start | bytes 3932164 | tf_op jit(solution)/shard_map/while
  149.0 4.7 %copy-start.3 = (bf16[1,512,1280]{1,2,0:T(8,128)(2,1)S(1)}, bf16[1,512,1280]{1,2,0:T(8,128)(2,1)}, u32[]{:S(2)}) copy-start(bf16[1,512,1280]{1,2,0:T(8,128)(2,1)} %copy-done.2) | copy-start | bytes 3932164 | tf_op jit(solution)/shard_map/while
  163.0 1.7 copy-start.6
  164.8 0.7 copy-start.5
  167.5 4.4 %copy-start.2 = (bf16[1,512,1280]{1,2,0:T(8,128)(2,1)}, bf16[1,512,1280]{1,2,0:T(8,128)(2,1)S(1)}, u32[]{:S(2)}) copy-start(bf16[1,512,1280]{1,2,0:T(8,128)(2,1)S(1)} %copy.120) | copy-start | bytes 3932164 | tf_op jit(solution)/shard_map/while
  174.8 4.7 %copy-start.3 = (bf16[1,512,1280]{1,2,0:T(8,128)(2,1)S(1)}, bf16[1,512,1280]{1,2,0:T(8,128)(2,1)}, u32[]{:S(2)}) copy-start(bf16[1,512,1280]{1,2,0:T(8,128)(2,1)} %copy-done.2) | copy-start | bytes 3932164 | tf_op jit(solution)/shard_map/while
  188.8 1.8 copy-start.6
  193.5 4.4 %copy-start.2 = (bf16[1,512,1280]{1,2,0:T(8,128)(2,1)}, bf16[1,512,1280]{1,2,0:T(8,128)(2,1)S(1)}, u32[]{:S(2)}) copy-start(bf16[1,512,1280]{1,2,0:T(8,128)(2,1)S(1)} %copy.120) | copy-start | bytes 3932164 | tf_op jit(solution)/shard_map/while
  200.8 4.7 %copy-start.3 = (bf16[1,512,1280]{1,2,0:T(8,128)(2,1)S(1)}, bf16[1,512,1280]{1,2,0:T(8,128)(2,1)}, u32[]{:S(2)}) copy-start(bf16[1,512,1280]{1,2,0:T(8,128)(2,1)} %copy-done.2) | copy-start | bytes 3932164 | tf_op jit(solution)/shard_map/while
  214.8 1.7 copy-start.6
  241.9 1.2 copy-start.14
  243.1 3.1 copy-start.8
  246.2 5.8 %copy-start.12 = (bf16[1,333,1280]{1,2,0:T(8,128)(2,1)S(1)}, bf16[1,333,1280]{1,2,0:T(8,128)(2,1)}, u32[]{:S(2)}) copy-start(bf16[1,333,1280]{1,2,0:T(8,128)(2,1)} %copy-done.11) | copy-start | bytes 2557444
  252.1 3.0 copy-start.20
  255.0 4.8 %copy-start.4 = (f32[20,333,333]{2,1,0:T(8,128)}, f32[20,333,333]{2,1,0:T(8,128)S(1)}, u32[]{:S(2)}) copy-start(f32[20,333,333]{2,1,0:T(8,128)S(1)} %fusion.41) | copy-start | bytes 26613364
  259.8 2.4 copy-start.15
  268.1 58.5 %all-to-all-start = ((bf16[8,152,1280]{2,1,0:T(8,128)(2,1)}), bf16[8,152,1280]{2,1,0:T(8,128)(2,1)}, u32[]{:S(2)}, u32[]{:S(2)}) async-start(bf16[8,152,1280]{2,1,0:T(8,128)(2,1)} %broadcast_in_dim.28), calls=%async_computation.3 | async-start | bytes 6225920 | tf_op jit(solution)/shard_map/all_to_all | solution.py:42
  291.7 2.4 copy-start.27
  291.7 2.4 copy-start.28
  294.0 3.7 copy-start.16
  294.0 4.8 %copy-start.21 = (f32[128,1280]{1,0:T(8,128)S(1)}, f32[128,1280]{1,0:T(8,128)}, u32[]{:S(2)}) copy-start(f32[128,1280]{1,0:T(8,128)} %copy.92) | copy-start | bytes 1966084
  297.8 70.8 %copy-start.22 = (f32[128,1280]{1,0:T(8,128)S(1)}, f32[128,1280]{1,0:T(8,128)}, u32[]{:S(2)}) copy-start(f32[128,1280]{1,0:T(8,128)} %copy.100) | copy-start | bytes 1966084
  298.9 71.8 %copy-start.1 = (bf16[1,128,2432]{2,1,0:T(8,128)(2,1)S(1)}, bf16[1,128,2432]{2,1,0:T(8,128)(2,1)}, u32[]{:S(2)}) copy-start(bf16[1,128,2432]{2,1,0:T(8,128)(2,1)} %param.19) | copy-start | bytes 1867780
  (2 other events, 1.4 us)
Sparse Core Ops, SparseCore 0:
  15.1 20.6 reduce-scatter.5
  39.4 106.9 reduce-scatter.7
  242.0 126.5 reduce-scatter.3
Sparse Core Ops, SparseCore 1:
  17.9 86.4 all-gather.1
  107.5 148.2 all-reduce.2
where the time goes:
time: 380 us; the launch traced here: 378 us
  waiting for transfers between devices  114 us (30%)
  matrix products  110 us (29%)
  local copies, waits for them, and re-layouts  98 us (26%)
  other arithmetic  35.1 us (9%)
  between operations  15.6 us (4%)
  starting transfers between devices  4.9 us (1%)
    reduce_scatter x1, waiting for transfers between devices, in_one_piece_2(): out = lax.psum_scatter(both, axis, scatter_dimension=dim, tiled=True)  38.8 us
    all_gather x1, waiting for transfers between devices, in_one_piece(): out = lax.all_gather(both, axis, axis=dim, tiled=True)  30.8 us
    dot_general x7, matrix products, pair_grads(): jnp.einsum('hqk,qhe->khe', weights_low, grad_heads, preferred_element_typ...  27.8 us
    dot_general x7, matrix products, score_parts(): jnp.einsum('qhe,khe->hqk', grad_heads, value_heads, preferred_element_typ...  26.9 us
    all_to_all x1, waiting for transfers between devices, from_everyone(): lax.all_to_all(jnp.broadcast_to(array[None], (devices, *array.shape)), ax...  25.8 us
    dot_general x7, matrix products, score_parts(): jnp.einsum('qhe,khe->hqk', query_heads, key_heads, preferred_element_type...  22 us
    dynamic_slice x16, local copies, waits for them, and re-layouts, shards(): lax.scan(key_step, query_acc, (key_piece.reshape(block_count, block_rows,...  19.7 us
    reduce_scatter x1, waiting for transfers between devices, sum_by_chip(): blocks = lax.psum_scatter(blocks, core, scatter_dimension=0, tiled=True)  18.8 us
  transfers between devices with their start and end apart: 6, of which 4 were waited for; matrix products, arithmetic and copies ran while one was open for 60% of the time, Pallas kernels for 0%

commit v1 on v0

v1 whole, which is shorter than its diff:
```python
import jax
import jax.numpy as jnp
from jax import lax
from jax.experimental import pallas as pl
from jax.experimental.pallas import tpu as pltpu
from jax.sharding import Mesh
from jax.sharding import PartitionSpec as P

SEQ = ("z", "xh", "core")
CHIPS = ("z", "xh")
IMG = ("y", "xl")
BF = jnp.bfloat16
F32 = jnp.float32
NT = (((1,), (1,)), ((), ()))

N = 16
TOK = 128
S = N * TOK
TXT = 333
TXT_Q = 384
TXT_K = 336
HALF = 176
HALF_Q = 256
SH = N * TOK // 2
W_ROWS = S + TXT_Q
L_ROWS = SH + HALF_Q
SCALE = 0.125
MSG = 400
OUT = 288
TOUT = TXT_K + HALF + TXT_K
VMEM_LIMIT = 56 * 2**20


def iota(shape, dim):
    return lax.broadcasted_iota(jnp.int32, shape, dim)


def thirds(x):
    high = x.astype(BF).astype(F32)
    rest = x - high
    middle = rest.astype(BF).astype(F32)
    return high, middle, rest - middle


def dot(a, b):
    return jnp.dot(a, b, preferred_element_type=F32)


def dot_nt(a, b):
    return lax.dot_general(a, b, NT, preferred_element_type=F32)


def swap_halves(x):
    return pltpu.roll(x, 64, 1)


def picked_sum(pick, x):
    a, b, c = thirds(x)
    pick = pick.astype(BF)
    return dot_nt(pick, a.astype(BF)) + dot_nt(pick, b.astype(BF)) + dot_nt(pick, c.astype(BF))


def stat_rows(lsum, delta, base, row):
    width = lsum.shape[1]
    rows = iota((16, width), 0)
    tile = jnp.zeros((16, width), F32)
    for k, part in enumerate(thirds(lsum)):
        tile = jnp.where(rows == base + k, part[row : row + 1, :], tile)
    for k, part in enumerate(thirds(delta)):
        tile = jnp.where(rows == 8 + base + k, part[row : row + 1, :], tile)
    return tile


def pack_kernel(index, og, w, q, k, v, o, l, send):
    j = pl.program_id(0)
    g = dot(og[...], w[...]).astype(BF).astype(F32)
    qf, kf, vf = q[...].astype(F32), k[...].astype(F32), v[...].astype(F32)
    delta = picked_sum(
        jnp.where(iota((8, 256), 1) // 64 == iota((8, 256), 0), 1.0, 0.0),
        g * o[...].astype(F32),
    )
    lsum = picked_sum(
        jnp.where(iota((8, 20), 1) == 4 * j + iota((8, 20), 0), 1.0, 0.0), l[...]
    )
    low = iota((TOK, 128), 1) < 64

    def packed(a, b, r):
        t = 128 * (r // 2)
        a, b = a[:, t : t + 128], b[:, t : t + 128]
        if r % 2 == 0:
            return jnp.where(low, a, swap_halves(b)).astype(BF)
        return jnp.where(low, swap_halves(a), b).astype(BF)

    @pl.when(j < 4)
    def whole():
        for r in range(4):
            d = 4 * j + r
            send[d, 0:128, :] = packed(qf, g, r)
            send[d, 128:256, :] = packed(kf, vf, r)
            send[d, 384:400, :] = stat_rows(lsum, delta, 0, r).astype(BF)

    @pl.when(j == 4)
    def shared():
        parity = index[0] % 2
        here = iota((16, 128), 1) // 64 == parity
        for r in range(4):
            qg, kv = packed(qf, g, r), packed(kf, vf, r)
            stat = stat_rows(lsum, delta, 4, r)
            moved = swap_halves(stat)
            for qi in range(2):
                mine = jnp.where(here, jnp.where(parity == qi, stat, moved), 0.0)
                for ki in range(2):
                    d = 4 * r + 2 * qi + ki
                    send[d, 256:320, :] = qg[64 * qi : 64 * qi + 64]
                    send[d, 320:384, :] = kv[64 * ki : 64 * ki + 64]
                    send[d, 384:400, :] = (send[d, 384:400, :].astype(F32) + mine).astype(BF)


def pack(index, og, w, q, k, v, o, l):
    depth = og.shape[1]
    column = pl.BlockSpec((TOK, 256), lambda j, s: (0, j))
    return pl.pallas_call(
        pack_kernel,
        grid_spec=pltpu.PrefetchScalarGridSpec(
            num_scalar_prefetch=1,
            grid=(5,),
            in_specs=[
                pl.BlockSpec((TOK, depth), lambda j, s: (0, 0)),
                pl.BlockSpec((depth, 256), lambda j, s: (0, j)),
                column,
                column,
                column,
                column,
                pl.BlockSpec((TOK, 20), lambda j, s: (0, 0)),
            ],
            out_specs=pl.BlockSpec((N, MSG, 128), lambda j, s: (0, 0, 0)),
        ),
        out_shape=jax.ShapeDtypeStruct((N, MSG, 128), BF),
        compiler_params=pltpu.CompilerParams(vmem_limit_bytes=VMEM_LIMIT),
        name="pack",
    )(index, og, w, q, k, v, o, l)


def text_kernel(
    index, wq, wk, wv, wo, wg, lq, lk, lv, lo, lg, l, wqg, wkv, wst, lqg, lkv, lst, buf, lbuf
):
    d = index[0]
    for n, ref in enumerate((wq, wk, wv, wo, wg, lq, lk, lv, lo, lg)):
        buf[n] = jnp.zeros(buf.shape[1:], F32)
        buf[n, 0:TXT, :] = ref[...].astype(F32)
    lbuf[...] = jnp.zeros(lbuf.shape, F32)
    lbuf[0:TXT, :] = l[...]

    def gather(first, odd, q_rows, k_rows):
        q, k, v = buf[first, q_rows, :], buf[first + 1, k_rows, :], buf[first + 2, k_rows, :]
        o, g = buf[first + 3, q_rows, :], buf[first + 4, q_rows, :]

        def pair(a, b):
            low = iota(a.shape, 1) < 64
            left = jnp.where(odd, swap_halves(a), a)
            right = jnp.where(odd, b, swap_halves(b))
            return jnp.where(low, left, right)

        product = o * g
        mine = (iota(product.shape, 1) >= 64) == odd
        return pair(q, g), pair(k, v), jnp.where(mine, product, 0.0)

    qg, kv, product = gather(0, d % 2 == 1, slice(0, TXT_Q), slice(0, TXT_Q))
    ones = jnp.ones((8, 128), F32)
    pick = jnp.where(iota((8, 20), 1) == d, 1.0, 0.0)
    wqg[...] = qg.astype(BF)
    wkv[...] = kv.astype(BF)
    wst[...] = stat_rows(
        picked_sum(pick, lbuf[0:TXT_Q, :]), picked_sum(ones, product), 0, 0
    ).astype(BF)

    head = 16 + d // 4
    q_rows = pl.ds(pl.multiple_of(HALF * ((d % 4) // 2), 16), HALF_Q)
    k_rows = pl.ds(pl.multiple_of(HALF * (d % 2), 16), HALF_Q)
    qg, kv, product = gather(5, head % 2 == 1, q_rows, k_rows)
    inside = iota((HALF_Q, 128), 0) < HALF
    pick = jnp.where(iota((8, 20), 1) == head, 1.0, 0.0)
    lqg[...] = jnp.where(inside, qg, 0.0).astype(BF)
    lkv[...] = jnp.where(inside, kv, 0.0).astype(BF)
    lst[...] = stat_rows(
        picked_sum(pick, lbuf[q_rows, :]),
        picked_sum(ones, jnp.where(inside, product, 0.0)),
        4,
        0,
    ).astype(BF)


def text_prep(index, q, k, v, o, g, l):
    whole = pl.BlockSpec((TXT, 128), lambda i, s: (0, s[0] // 2))
    shared = pl.BlockSpec((TXT, 128), lambda i, s: (0, 8 + s[0] // 8))
    shapes = [
        (TXT_Q, 128), (TXT_Q, 128), (16, TXT_Q), (HALF_Q, 128), (HALF_Q, 128), (16, HALF_Q)
    ]
    return pl.pallas_call(
        text_kernel,
        grid_spec=pltpu.PrefetchScalarGridSpec(
            num_scalar_prefetch=1,
            grid=(1,),
            in_specs=[whole] * 5 + [shared] * 5 + [pl.BlockSpec((TXT, 20), lambda i, s: (0, 0))],
            out_specs=[pl.BlockSpec(s, lambda i, s_: (0, 0)) for s in shapes],
            scratch_shapes=[
                pltpu.VMEM((10, HALF + HALF_Q, 128), F32),
                pltpu.VMEM((HALF + HALF_Q, 20), F32),
            ],
        ),
        out_shape=[jax.ShapeDtypeStruct(s, BF) for s in shapes],
        compiler_params=pltpu.CompilerParams(vmem_limit_bytes=VMEM_LIMIT),
        name="text_prep",
    )(index, q, k, v, o, g, q, k, v, o, g, l)


def transposed(x):
    return x.astype(F32).T.astype(BF)


class Head:
    def __init__(self, refs):
        self.ka, self.va, self.b0, self.b1, self.qta, self.gta, self.kt, self.dkv, self.dqt = refs

    @staticmethod
    def scratch(rows):
        return [pltpu.VMEM((rows, 128), BF)] * 4 + [
            pltpu.VMEM((128, rows), BF),
            pltpu.VMEM((128, rows), BF),
            pltpu.VMEM((64, rows), BF),
            pltpu.VMEM((rows, 128), F32),
            pltpu.VMEM((64, rows), F32),
        ]

    def fill(self, at, qg, kv, stat, base):
        rows = qg.shape[0]
        lane = iota((rows, 128), 1)
        low = lane < 64
        zero = jnp.zeros((rows, 128), BF)
        here = pl.ds(at, rows)
        kf = kv.astype(F32)
        off = lane - 64 - base
        ka = jnp.where(low, kf * SCALE, jnp.where((off >= 0) & (off < 3), -1.0, 0.0))
        off = lane - 8 - base
        va = jnp.where(low, jnp.where((off >= 0) & (off < 3), -1.0, 0.0), kf)
        self.ka[here, :] = ka.astype(BF)
        self.va[here, :] = va.astype(BF)
        self.b0[here, :] = jnp.where(low, zero, qg)
        self.b1[here, :] = jnp.where(low, qg, zero)
        qgt = transposed(qg)
        self.qta[0:64, here] = qgt[0:64]
        self.qta[64:80, here] = stat
        self.qta[80:128, here] = jnp.zeros((48, rows), BF)
        self.gta[0:16, here] = stat
        self.gta[16:64, here] = jnp.zeros((48, rows), BF)
        self.gta[64:128, here] = qgt[64:128]
        self.kt[:, here] = transposed(kv)[0:64]

    def zero(self):
        self.dkv[...] = jnp.zeros(self.dkv.shape, F32)
        self.dqt[...] = jnp.zeros(self.dqt.shape, F32)

    def block(self, k0, kb, q0, qb):
        ks, qs = pl.ds(k0, kb), pl.ds(q0, qb)
        p = jnp.exp(dot(self.ka[ks, :], self.qta[:, qs]))
        ds = p * dot(self.va[ks, :], self.gta[:, qs])
        p, ds = p.astype(BF), ds.astype(BF)
        self.dkv[ks, :] += dot(p, self.b0[qs, :]) + dot(ds, self.b1[qs, :])
        self.dqt[:, qs] += dot(self.kt[:, ks], ds)

    def blocks(self, k_all, kb, q_all, qb):
        def q_step(i, _):
            q0 = pl.multiple_of(i * qb, 128)

            def k_step(n, _):
                self.block(pl.multiple_of(n * kb, 128), kb, q0, qb)
                return 0

            return lax.fori_loop(0, k_all // kb, k_step, 0)

        lax.fori_loop(0, q_all // qb, q_step, 0)


def attend_kernel(recv, wqg, wkv, wst, lqg, lkv, lst, out, tout, *refs):
    w, h = Head(refs[:9]), Head(refs[9:])
    for s in range(N):
        w.fill(TOK * s, recv[s, 0:128, :], recv[s, 128:256, :], recv[s, 384:400, :], 0)
    for m in range(N // 2):
        a, b = 2 * m, 2 * m + 1
        stat = jnp.where(
            iota((16, 128), 1) < 64, recv[a, 384:400, :], recv[b, 384:400, :]
        )
        h.fill(
            128 * m,
            jnp.concatenate([recv[a, 256:320, :], recv[b, 256:320, :]], 0),
            jnp.concatenate([recv[a, 320:384, :], recv[b, 320:384, :]], 0),
            stat,
            4,
        )
    for m in range(TXT_Q // 128):
        t = slice(128 * m, 128 * m + 128)
        w.fill(S + 128 * m, wqg[t, :], wkv[t, :], wst[:, t], 0)
    for m in range(HALF_Q // 128):
        t = slice(128 * m, 128 * m + 128)
        h.fill(SH + 128 * m, lqg[t, :], lkv[t, :], lst[:, t], 4)
    w.zero()
    h.zero()

    w.block(S, TXT_K, S, TXT_Q)

    def whole_text(n, _):
        at = pl.multiple_of(n * 512, 512)
        w.block(at, 512, S, TXT_Q)
        w.block(S, TXT_K, at, 512)
        return 0

    lax.fori_loop(0, S // 512, whole_text, 0)
    h.block(SH, HALF, SH, HALF_Q)

    def shared_text(n, _):
        at = pl.multiple_of(n * 512, 512)
        h.block(at, 512, SH, HALF_Q)
        h.block(SH, HALF, at, 512)
        return 0

    lax.fori_loop(0, SH // 512, shared_text, 0)

    h.blocks(SH, 256, SH, 512)
    w.blocks(S, 256, S, 512)

    factor = jnp.where(iota((128, 128), 1) < 64, SCALE, 1.0)
    for m in range(TXT_Q // 128):
        rows = min(128, TXT_K - 128 * m)
        tout[128 * m : 128 * m + rows, :] = (
            w.dkv[S + 128 * m : S + 128 * m + rows, :] * factor[:rows]
        ).astype(BF)
        lower = h.dqt[:, SH + 128 * m : SH + 128 * m + 128] if m < 2 else jnp.zeros((64, 128), F32)
        both = jnp.concatenate([w.dqt[:, S + 128 * m : S + 128 * m + 128], lower], 0)
        at = TXT_K + HALF + 128 * m
        tout[at : at + rows, :] = (both * SCALE).T[:rows].astype(BF)
    tout[TXT_K : TXT_K + 128, :] = (h.dkv[SH : SH + 128, :] * factor).astype(BF)
    tout[TXT_K + 128 : TXT_K + HALF, :] = (
        h.dkv[SH + 128 : SH + HALF, :] * factor[: HALF - 128]
    ).astype(BF)

    for s in range(N):
        out[s, 0:128, :] = (w.dkv[128 * s : 128 * s + 128, :] * factor).astype(BF)
        out[s, 128:192, :] = (h.dkv[64 * s : 64 * s + 64, :] * factor[:64]).astype(BF)
        a = w.dqt[:, 128 * s : 128 * s + 128] * SCALE
        both = jnp.concatenate([a, swap_halves(a)], 0).T
        out[s, 192:256, :] = both[0:64].astype(BF)
    for m in range(N // 2):
        a = h.dqt[:, 128 * m : 128 * m + 128] * SCALE
        both = jnp.concatenate([a, pltpu.roll(a, 96, 1)], 0).T
        out[2 * m, 256:288, :] = both[0:32].astype(BF)
        out[2 * m + 1, 256:288, :] = both[64:96].astype(BF)


def attend(recv, texts):
    full = pl.BlockSpec(memory_space=pltpu.VMEM)
    return pl.pallas_call(
        attend_kernel,
        in_specs=[full] * 7,
        out_specs=[full] * 2,
        out_shape=[
            jax.ShapeDtypeStruct((N, OUT, 128), BF),
            jax.ShapeDtypeStruct((TOUT, 128), BF),
        ],
        scratch_shapes=Head.scratch(W_ROWS) + Head.scratch(L_ROWS),
        compiler_params=pltpu.CompilerParams(vmem_limit_bytes=VMEM_LIMIT),
        name="attend",
    )(recv, *texts)


def lane_pair(even, odd):
    low = iota(even.shape, 1) < 64
    return (
        jnp.where(low, even, swap_halves(odd)),
        jnp.where(low, swap_halves(even), odd),
    )


def unpack_kernel(recv, dq, dk, dv):
    def part(d, rows):
        return recv[d, rows, :].astype(F32)

    for t in range(N // 2):
        lanes = slice(128 * t, 128 * t + 128)
        keys, values = lane_pair(part(2 * t, slice(0, 128)), part(2 * t + 1, slice(0, 128)))
        dk[:, lanes] = keys.astype(BF)
        dv[:, lanes] = values.astype(BF)
        first, second = lane_pair(part(2 * t, slice(192, 256)), part(2 * t + 1, slice(192, 256)))
        dq[0:64, lanes] = first.astype(BF)
        dq[64:128, lanes] = second.astype(BF)
    for t in range(2):
        lanes = slice(1024 + 128 * t, 1024 + 128 * t + 128)
        for half in range(2):
            rows = slice(64 * half, 64 * half + 64)
            keys, values = lane_pair(
                *(
                    part(4 * r + half, slice(128, 192)) + part(4 * r + 2 + half, slice(128, 192))
                    for r in (2 * t, 2 * t + 1)
                )
            )
            dk[rows, lanes] = keys.astype(BF)
            dv[rows, lanes] = values.astype(BF)
            first, second = lane_pair(
                *(
                    part(4 * r + 2 * half, slice(256, 288))
                    + part(4 * r + 2 * half + 1, slice(256, 288))
                    for r in (2 * t, 2 * t + 1)
                )
            )
            dq[64 * half : 64 * half + 32, lanes] = first.astype(BF)
            dq[64 * half + 32 : 64 * half + 64, lanes] = second.astype(BF)


def unpack(recv):
    full = pl.BlockSpec(memory_space=pltpu.VMEM)
    return pl.pallas_call(
        unpack_kernel,
        in_specs=[full],
        out_specs=[full] * 3,
        out_shape=[jax.ShapeDtypeStruct((TOK, 1280), BF)] * 3,
        compiler_params=pltpu.CompilerParams(vmem_limit_bytes=VMEM_LIMIT),
        name="unpack",
    )(recv)


def unpack_text_kernel(core, mine, other, dq, dk, dv):
    odd_core = core[0] == 1

    def part(d, rows):
        a, b = mine[d // 2, rows, :].astype(F32), other[d // 2, rows, :].astype(F32)
        return jnp.where(odd_core, b, a) if d % 2 == 0 else jnp.where(odd_core, a, b)

    at = TXT_K + HALF
    for t in range(N // 2):
        lanes = slice(128 * t, 128 * t + 128)
        keys, values = lane_pair(part(2 * t, slice(0, TXT_K)), part(2 * t + 1, slice(0, TXT_K)))
        dk[:, lanes] = keys[:TXT].astype(BF)
        dv[:, lanes] = values[:TXT].astype(BF)
        queries, _ = lane_pair(part(2 * t, slice(at, TOUT)), part(2 * t + 1, slice(at, TOUT)))
        dq[:, lanes] = queries[:TXT].astype(BF)
    shared = slice(TXT_K, TXT_K + HALF)
    shared_q = slice(at, at + HALF)
    for t in range(2):
        lanes = slice(1024 + 128 * t, 1024 + 128 * t + 128)
        for half in range(2):
            size = min(HALF, TXT - HALF * half)
            rows = slice(HALF * half, HALF * half + size)
            keys, values = lane_pair(
                *(
                    part(4 * r + half, shared) + part(4 * r + 2 + half, shared)
                    for r in (2 * t, 2 * t + 1)
                )
            )
            dk[rows, lanes] = keys[:size].astype(BF)
            dv[rows, lanes] = values[:size].astype(BF)
            _, queries = lane_pair(
                *(
                    part(4 * r + 2 * half, shared_q) + part(4 * r + 2 * half + 1, shared_q)
                    for r in (2 * t, 2 * t + 1)
                )
            )
            dq[rows, lanes] = queries[:size].astype(BF)


def unpack_text(core, mine, other):
    full = pl.BlockSpec(memory_space=pltpu.VMEM)
    return pl.pallas_call(
        unpack_text_kernel,
        in_specs=[pl.BlockSpec(memory_space=pltpu.SMEM), full, full],
        out_specs=[full] * 3,
        out_shape=[jax.ShapeDtypeStruct((TXT, 1280), BF)] * 3,
        compiler_params=pltpu.CompilerParams(vmem_limit_bytes=VMEM_LIMIT),
        name="unpack_text",
    )(core, mine, other)


def exchange(x, axes):
    return lax.all_to_all(x, axes, 0, 0, tiled=True)


def other_core(x):
    return lax.ppermute(x, "core", [(0, 1), (1, 0)])


def spread(x, axes):
    return exchange(jnp.broadcast_to(x[None], (lax.axis_size(axes), *x.shape)), axes)


def weight_gradient(og, o):
    chips = lax.axis_size(CHIPS)
    quarters = lax.axis_size("y")
    core = lax.axis_index("core")
    blocks = og.T.reshape(chips, 2, -1, og.shape[0])
    rows = blocks.shape[2]
    mine = lax.dynamic_index_in_dim(blocks, core, 1, False)
    theirs = lax.dynamic_index_in_dim(blocks, 1 - core, 1, False)
    left = jnp.concatenate([mine, other_core(theirs)], 2)
    right = jnp.concatenate([o, other_core(o)], 0)
    term = jnp.einsum("prt,tc->prc", left, right, preferred_element_type=F32).astype(BF)
    padded = -(-rows // (8 * quarters)) * 8 * quarters
    term = jnp.pad(term, ((0, 0), (0, padded - rows), (0, 0)))
    term = term.reshape(chips, quarters, padded // quarters, -1).swapaxes(0, 1)
    part = exchange(term, "y").astype(F32).sum(0).astype(BF)
    part = exchange(part, CHIPS).astype(F32).sum(0).astype(BF)
    part = spread(part, IMG).reshape(quarters, -1, *part.shape).astype(F32).sum(1)
    return part.reshape(padded, -1)[:rows]


def shards(
    image_query,
    image_key,
    image_value,
    image_output,
    output_grad,
    image_logsum,
    text_query,
    text_key,
    text_value,
    text_output,
    text_grad,
    text_logsum,
    out_weight,
):
    device = lax.axis_index(SEQ).astype(jnp.int32).reshape(1)
    core = lax.axis_index("core").astype(jnp.int32).reshape(1)
    send = pack(
        device,
        output_grad[0],
        out_weight,
        image_query[0],
        image_key[0],
        image_value[0],
        image_output[0],
        image_logsum[0],
    )
    recv = exchange(send, SEQ)
    texts = text_prep(
        device,
        text_query[0],
        text_key[0],
        text_value[0],
        text_output[0],
        text_grad[0],
        text_logsum[0],
    )
    out, text_out = attend(recv, texts)
    mine = spread(text_out, CHIPS)
    text_grads = unpack_text(core, mine, other_core(mine))
    grads = unpack(exchange(out, SEQ))
    weight_grad = weight_gradient(output_grad[0], image_output[0])
    return (*(g[None] for g in grads), *(g[None] for g in text_grads), weight_grad)


def solution(mesh):
    pairs = 2 if mesh.shape["img"] > 1 else 1
    finer = Mesh(
        mesh.devices.reshape(mesh.shape["img"] // pairs, pairs, 4, 2, 2),
        ("y", "xl", "z", "xh", "core"),
    )
    image = P(IMG, SEQ, None)
    text = P(IMG, None, None)
    return jax.shard_map(
        shards,
        mesh=finer,
        in_specs=(image,) * 6 + (text,) * 6 + (P(),),
        out_specs=(image,) * 3 + (text,) * 3 + (P(SEQ, None),),
        check_vma=False,
    )
```

time: 380 us -> 183 us (0.48)
  matrix products: 110 us -> 0.97 us
  local copies, waits for them, and re-layouts: 98 us -> 10.3 us
  Pallas kernels: 0 us -> 49.6 us
  waiting for transfers between devices: 114 us -> 70.8 us
  other arithmetic: 35.1 us -> 1.83 us
  starting transfers between devices: 4.9 us -> 28.6 us
  blocking collectives: 0 us -> 18.3 us
  between operations: 15.6 us -> 0.72 us
    dot_general x37 -> x1, matrix products: 110 us -> 0.97 us  [weight_gradient(): jnp.einsum('prt,tc->prc', left, right, preferred_element_type=F32)]
    reduce_scatter x3 -> x0, waiting for transfers between devices: 57.6 us -> none  [the longest x1 38.8 us: in_one_piece_2(): out = lax.psum_scatter(both, axis, scatter_dimension=dim, tiled=True)]
    pallas_call x0 -> x5, Pallas kernels: none -> 49.6 us  [the longest x1 31.4 us: attend(): pl.pallas_call(attend_kernel, in_specs=[full] * 7, out_specs=[full] * 2,...]
    all_to_all x1 -> x5, waiting for transfers between devices: 25.8 us -> 69.5 us  [exchange(): return lax.all_to_all(x, axes, 0, 0, tiled=True)]
    all_gather x1 -> x0, waiting for transfers between devices: 30.8 us -> none  [in_one_piece(): out = lax.all_gather(both, axis, axis=dim, tiled=True)]
    all_to_all x1 -> x5, starting transfers between devices: 4.51 us -> 27.7 us  [exchange(): return lax.all_to_all(x, axes, 0, 0, tiled=True)]
    convert_element_type x5 -> x0, local copies, waits for them, and re-layouts: 20.6 us -> none  [the longest x1 7.93 us: shards(): value_all.astype(jnp.bfloat16)]
    dynamic_slice x16 -> x0, local copies, waits for them, and re-layouts: 19.7 us -> none  [shards(): lax.scan(key_step, query_acc, (key_piece.reshape(block_count, block_rows,...]
  transfers between devices with their start and end apart: 6 -> 8, of which waited for: 4 -> 6; matrix products, arithmetic and copies ran while one was open for 60% -> 4% of each run, Pallas kernels for 0% -> 20%
where the time goes in v1:
time: 183 us; the launch traced here: 181 us
  waiting for transfers between devices  70.8 us (39%)
  Pallas kernels  49.6 us (27%)
  starting transfers between devices  28.6 us (16%)
  blocking collectives  18.3 us (10%)
  local copies, waits for them, and re-layouts  10.3 us (6%)
  other arithmetic  1.83 us (1%)
    all_to_all x5, waiting for transfers between devices, exchange(): return lax.all_to_all(x, axes, 0, 0, tiled=True)  69.5 us
    pallas_call x1, Pallas kernels, attend(): pl.pallas_call(attend_kernel, in_specs=[full] * 7, out_specs=[full] * 2,...  31.4 us
    all_to_all x5, starting transfers between devices, exchange(): return lax.all_to_all(x, axes, 0, 0, tiled=True)  27.7 us
    all_to_all x1, blocking collectives, exchange(): return lax.all_to_all(x, axes, 0, 0, tiled=True)  18.3 us
    pallas_call x1, Pallas kernels, pack(): pl.pallas_call(pack_kernel, grid_spec=pltpu.PrefetchScalarGridSpec(num_sc...  8.25 us
    pallas_call x1, Pallas kernels, unpack_text(): pl.pallas_call(unpack_text_kernel, in_specs=[pl.BlockSpec(memory_space=pl...  4.83 us
  transfers between devices with their start and end apart: 8, of which 6 were waited for; matrix products, arithmetic and copies ran while one was open for 4% of the time, Pallas kernels for 20%

profile of v1, /device:TPU:1, one launch (start us, length us, event | category | flops | bytes accessed | tf_op | source)
XLA Modules:
  0.0 181.1 jit_solution(5961703710199811227)
XLA Ops:
  0.6 1.4 copy.31
  2.1 8.2 %pack.1 = bf16[16,400,128]{2,1,0:T(8,128)(2,1)} custom-call(s32[1]{0:T(128)} %bitcast.index, bf16[128,2432]{1,0:T(8,128)(2,1)} %bitcast.51, bf16[2432,1280]{1,0:T(8,128)(2,1)} %w.1, bf16[128,1280]{1,0:T(8,128)(2,1)} %bitcast.58, bf16[128,1280]{1,0:T(8,128)(2,1)} %bitcast.59, bf16[128,1280]{1,0:T(8,128)(2,1)} %bitcast.60, bf16[128,1280]{1,0:T(8,128)(2,1)} %bitcast.54, ...), custom_call_target="tpu_custom_call" | custom-call | tf_op jit(solution)/shard_map/pack/pallas_call | solution.py:122
  10.3 0.0 copy-start.3
  10.3 0.0 copy-start.2
  10.3 9.4 %all-to-all-start = ((bf16[16,400,128]{2,1,0:T(8,128)(2,1)}), bf16[16,400,128]{2,1,0:T(8,128)(2,1)S(1)}, u32[]{:S(2)}, u32[]{:S(2)}) async-start(bf16[16,400,128]{2,1,0:T(8,128)(2,1)} %pack.1), calls=%async_computation | async-start | bytes 3276800 | tf_op jit(solution)/shard_map/all_to_all | solution.py:482
  19.8 0.0 copy-done.3
  19.8 0.2 collective-permute-start.2
  19.9 0.0 copy-done.2
  20.0 0.3 copy.33
  20.3 0.1 dynamic-slice_bitcast_fusion.1
  20.4 0.5 collective-permute-start.1
  20.8 1.2 collective-permute-done.1
  22.1 0.0 collective-permute-done.2
  22.1 1.0 convolution_convert_fusion
  23.0 0.2 pad.4
  23.3 1.9 %copy.36 = bf16[8,4,40,1280]{3,2,0,1:T(8,128)(2,1)} copy(bf16[8,4,40,1280]{3,2,1,0:T(8,128)(2,1)S(1)} %bitcast.39) | data formatting | bytes 6553600 | tf_op jit(solution)/shard_map/reshape | solution.py:506
  25.2 18.1 %all-to-all-done.recv = bf16[16,400,128]{2,1,0:T(8,128)(2,1)S(1)} async-done(((bf16[16,400,128]{2,1,0:T(8,128)(2,1)}), bf16[16,400,128]{2,1,0:T(8,128)(2,1)S(1)}, u32[]{:S(2)}, u32[]{:S(2)}) %all-to-all-start) | async-done | bytes 1638432 | tf_op jit(solution)/shard_map/all_to_all | solution.py:482
  43.3 0.0 copy-start
  43.3 0.0 copy-start.4
  43.3 1.2 copy-done
  44.5 4.2 %all-to-all-start.3 = ((bf16[4,8,40,1280]{3,2,1,0:T(8,128)(2,1)}), bf16[4,8,40,1280]{3,2,1,0:T(8,128)(2,1)S(1)}, u32[]{:S(2)}, u32[]{:S(2)}) async-start(bf16[4,8,40,1280]{3,2,1,0:T(8,128)(2,1)} %bitcast.38), calls=%async_computation.3 | async-start | bytes 6553600 | tf_op jit(solution)/shard_map/all_to_all | solution.py:482
  48.7 0.0 copy-done.4
  48.7 0.8 copy.32
  49.5 2.5 %text_prep.1 = (bf16[384,128]{1,0:T(8,128)(2,1)}, bf16[384,128]{1,0:T(8,128)(2,1)}, bf16[16,384]{1,0:T(8,128)(2,1)}, bf16[256,128]{1,0:T(8,128)(2,1)}, bf16[256,...) custom-call(s32[1]{0:T(128)} %bitcast.index, bf16[333,1280]{1,0:T(8,128)(2,1)} %bitcast.40, bf16[333,1280]{1,0:T(8,128)(2,1)} %bitcast.42, ...), custom_call_target="tpu_custom_call" | custom-call | tf_op jit(solution)/shard_map/text_prep/pallas_call | solution.py:199
  52.0 31.4 %attend.1 = (bf16[16,288,128]{2,1,0:T(8,128)(2,1)}, bf16[848,128]{1,0:T(8,128)(2,1)}) custom-call(bf16[16,400,128]{2,1,0:T(8,128)(2,1)} %copy-done, bf16[384,128]{1,0:T(8,128)(2,1)} %get-tuple-element.21.wqg, bf16[384,128]{1,0:T(8,128)(2,1)} %get-tuple-element.22.wkv, bf16[16,384]{1,0:T(8,128)(2,1)} %get-tuple-element.23.wst, ...), custom_call_target="tpu_custom_call" | custom-call | tf_op jit(solution)/shard_map/attend/pallas_call | solution.py:361
  83.4 3.1 %all-to-all-done.3 = bf16[4,8,40,1280]{3,2,1,0:T(8,128)(2,1)S(1)} async-done(((bf16[4,8,40,1280]{3,2,1,0:T(8,128)(2,1)}), bf16[4,8,40,1280]{3,2,1,0:T(8,128)(2,1)S(1)}, u32[]{:S(2)}, u32[]{:S(2)}) %all-to-all-start.3) | async-done | bytes 3276832 | tf_op jit(solution)/shard_map/all_to_all | solution.py:482
  86.5 2.4 %broadcast_in_dim.33 = bf16[8,848,128]{2,1,0:T(8,128)(2,1)} broadcast(bf16[848,128]{1,0:T(8,128)(2,1)} %get-tuple-element.31), dimensions={1,2} | broadcast | bytes 1953792 | tf_op jit(solution)/shard_map/broadcast_in_dim | solution.py:490
  88.9 4.3 %all-to-all-start.2 = ((bf16[8,848,128]{2,1,0:T(8,128)(2,1)}), bf16[8,848,128]{2,1,0:T(8,128)(2,1)}, u32[]{:S(2)}, u32[]{:S(2)}) async-start(bf16[8,848,128]{2,1,0:T(8,128)(2,1)} %broadcast_in_dim.33), calls=%async_computation.2 | async-start | bytes 3473408 | tf_op jit(solution)/shard_map/all_to_all | solution.py:482
  93.2 1.6 reduce_sum.33
  94.8 20.6 %all-to-all-done.2.mine = bf16[8,848,128]{2,1,0:T(8,128)(2,1)} async-done(((bf16[8,848,128]{2,1,0:T(8,128)(2,1)}), bf16[8,848,128]{2,1,0:T(8,128)(2,1)}, u32[]{:S(2)}, u32[]{:S(2)}) %all-to-all-start.2) | async-done | bytes 1736736 | tf_op jit(solution)/shard_map/all_to_all | solution.py:482
  115.4 18.3 %all_to_all.30 = bf16[8,40,1280]{2,1,0:T(8,128)(2,1)S(1)} all-to-all(bf16[8,40,1280]{2,1,0:T(8,128)(2,1)} %reduce_sum.33), channel_id=1, replica_groups=mesh['y'=4,'xl'=2,'z'=4,'xh'=2,'core'=2] {'z','xh'}, dimensions={0} | all-to-all | bytes 1638400 | tf_op jit(solution)/shard_map/all_to_all | solution.py:482
  133.7 6.2 %all-to-all-start.1 = ((bf16[16,288,128]{2,1,0:T(8,128)(2,1)}), bf16[16,288,128]{2,1,0:T(8,128)(2,1)S(1)}, u32[]{:S(2)}, u32[]{:S(2)}) async-start(bf16[16,288,128]{2,1,0:T(8,128)(2,1)} %get-tuple-element.27), calls=%async_computation.1 | async-start | bytes 2359296 | tf_op jit(solution)/shard_map/all_to_all | solution.py:482
  139.9 0.3 collective-permute-start
  140.2 0.1 reduce_sum.34
  140.3 18.3 %all-to-all-done.1.recv = bf16[16,288,128]{2,1,0:T(8,128)(2,1)S(1)} async-done(((bf16[16,288,128]{2,1,0:T(8,128)(2,1)}), bf16[16,288,128]{2,1,0:T(8,128)(2,1)S(1)}, u32[]{:S(2)}, u32[]{:S(2)}) %all-to-all-start.1) | async-done | bytes 1179680 | tf_op jit(solution)/shard_map/all_to_all | solution.py:482
  158.6 0.0 copy-start.1
  158.6 1.0 broadcast_in_dim.37
  159.6 3.5 %all-to-all-start.5 = ((bf16[8,40,1280]{2,1,0:T(8,128)(2,1)}), bf16[8,40,1280]{2,1,0:T(8,128)(2,1)S(1)}, u32[]{:S(2)}, u32[]{:S(2)}) async-start(bf16[8,40,1280]{2,1,0:T(8,128)(2,1)} %broadcast_in_dim.37), calls=%async_computation.5 | async-start | bytes 1638400 | tf_op jit(solution)/shard_map/all_to_all | solution.py:482
  163.2 0.0 copy-done.1
  163.2 2.6 %unpack.1 = (bf16[128,1280]{1,0:T(8,128)(2,1)}, bf16[128,1280]{1,0:T(8,128)(2,1)}, bf16[128,1280]{1,0:T(8,128)(2,1)}) custom-call(bf16[16,288,128]{2,1,0:T(8,128)(2,1)} %copy-done.1), custom_call_target="tpu_custom_call" | custom-call | tf_op jit(solution)/shard_map/unpack/pallas_call | solution.py:420
  165.8 9.4 %all-to-all-done.5 = bf16[8,40,1280]{2,1,0:T(8,128)(2,1)S(1)} async-done(((bf16[8,40,1280]{2,1,0:T(8,128)(2,1)}), bf16[8,40,1280]{2,1,0:T(8,128)(2,1)S(1)}, u32[]{:S(2)}, u32[]{:S(2)}) %all-to-all-start.5) | async-done | bytes 819232 | tf_op jit(solution)/shard_map/all_to_all | solution.py:482
  175.2 0.1 convert_reduce_fusion
  175.3 0.9 slice.4
  176.2 0.0 collective-permute-done.other
  176.3 4.8 %unpack_text.1 = (bf16[333,1280]{1,0:T(8,128)(2,1)}, bf16[333,1280]{1,0:T(8,128)(2,1)}, bf16[333,1280]{1,0:T(8,128)(2,1)}) custom-call(s32[1]{0:T(128)} %bitcast.16.core, bf16[8,848,128]{2,1,0:T(8,128)(2,1)} %all-to-all-done.2.mine, bf16[8,848,128]{2,1,0:T(8,128)(2,1)} %collective-permute-done.other), custom_call_target="tpu_custom_call" | custom-call | tf_op jit(solution)/shard_map/unpack_text/pallas_call | solution.py:471
Async XLA Ops:
  10.3 9.4 %copy-start.3 = (bf16[1,128,1280]{2,1,0:T(8,128)(2,1)S(1)}, bf16[1,128,1280]{2,1,0:T(8,128)(2,1)}, u32[]{:S(2)}) copy-start(bf16[1,128,1280]{2,1,0:T(8,128)(2,1)} %param.16) | copy-start | bytes 983044
  10.3 9.6 %copy-start.2 = (bf16[1,128,2432]{2,1,0:T(8,128)(2,1)S(1)}, bf16[1,128,2432]{2,1,0:T(8,128)(2,1)}, u32[]{:S(2)}) copy-start(bf16[1,128,2432]{2,1,0:T(8,128)(2,1)} %param.17) | copy-start | bytes 1867780
  10.3 33.0 %all-to-all-start = ((bf16[16,400,128]{2,1,0:T(8,128)(2,1)}), bf16[16,400,128]{2,1,0:T(8,128)(2,1)S(1)}, u32[]{:S(2)}, u32[]{:S(2)}) async-start(bf16[16,400,128]{2,1,0:T(8,128)(2,1)} %pack.1), calls=%async_computation | async-start | bytes 3276800 | tf_op jit(solution)/shard_map/all_to_all | solution.py:482
  19.8 2.3 %collective-permute-start.2 = (bf16[128,1280]{1,0:T(8,128)(2,1)S(1)}, bf16[128,1280]{1,0:T(8,128)(2,1)S(1)}, u32[]{:S(2)}, u32[]{:S(2)}) collective-permute-start(bf16[128,1280]{1,0:T(8,128)(2,1)S(1)} %bitcast.55), channel_id=1, source_target_pairs={{0,1},{1,0},{2,3},{3,2},{4,5},{5,4},{6,7},{7,6},{8,9},{9,8},{10,11... | collective-permute-start | bytes 983048 | tf_op jit(solution)/shard_map/ppermute | solution.py:486
  20.4 1.7 collective-permute-start.1
  43.3 1.2 copy-start
  43.3 5.4 %copy-start.4 = (f32[1,333,20]{1,0,2:T(1,128)S(1)}, f32[1,333,20]{1,0,2:T(1,128)}, u32[]{:S(2)}) copy-start(f32[1,333,20]{1,0,2:T(1,128)} %param.24) | copy-start | bytes 79924
  44.5 42.0 %all-to-all-start.3 = ((bf16[4,8,40,1280]{3,2,1,0:T(8,128)(2,1)}), bf16[4,8,40,1280]{3,2,1,0:T(8,128)(2,1)S(1)}, u32[]{:S(2)}, u32[]{:S(2)}) async-start(bf16[4,8,40,1280]{3,2,1,0:T(8,128)(2,1)} %bitcast.38), calls=%async_computation.3 | async-start | bytes 6553600 | tf_op jit(solution)/shard_map/all_to_all | solution.py:482
  88.9 26.5 %all-to-all-start.2 = ((bf16[8,848,128]{2,1,0:T(8,128)(2,1)}), bf16[8,848,128]{2,1,0:T(8,128)(2,1)}, u32[]{:S(2)}, u32[]{:S(2)}) async-start(bf16[8,848,128]{2,1,0:T(8,128)(2,1)} %broadcast_in_dim.33), calls=%async_computation.2 | async-start | bytes 3473408 | tf_op jit(solution)/shard_map/all_to_all | solution.py:482
  133.7 24.9 %all-to-all-start.1 = ((bf16[16,288,128]{2,1,0:T(8,128)(2,1)}), bf16[16,288,128]{2,1,0:T(8,128)(2,1)S(1)}, u32[]{:S(2)}, u32[]{:S(2)}) async-start(bf16[16,288,128]{2,1,0:T(8,128)(2,1)} %get-tuple-element.27), calls=%async_computation.1 | async-start | bytes 2359296 | tf_op jit(solution)/shard_map/all_to_all | solution.py:482
  139.9 36.4 %collective-permute-start = (bf16[8,848,128]{2,1,0:T(8,128)(2,1)}, bf16[8,848,128]{2,1,0:T(8,128)(2,1)}, u32[]{:S(2)}, u32[]{:S(2)}) collective-permute-start(bf16[8,848,128]{2,1,0:T(8,128)(2,1)} %all-to-all-done.2.mine), channel_id=1, source_target_pairs={{0,1},{1,0},{2,3},{3,2},{4,5},{5,4},{6,7},{7,6},{8,9},{9,8},{10,11... | collective-permute-start | bytes 5210120 | tf_op jit(solution)/shard_map/ppermute | solution.py:486
  158.6 4.6 %copy-start.1 = (bf16[16,288,128]{2,1,0:T(8,128)(2,1)}, bf16[16,288,128]{2,1,0:T(8,128)(2,1)S(1)}, u32[]{:S(2)}) copy-start(bf16[16,288,128]{2,1,0:T(8,128)(2,1)S(1)} %all-to-all-done.1.recv) | copy-start | bytes 3538948
  159.6 15.6 %all-to-all-start.5 = ((bf16[8,40,1280]{2,1,0:T(8,128)(2,1)}), bf16[8,40,1280]{2,1,0:T(8,128)(2,1)S(1)}, u32[]{:S(2)}, u32[]{:S(2)}) async-start(bf16[8,40,1280]{2,1,0:T(8,128)(2,1)} %broadcast_in_dim.37), calls=%async_computation.5 | async-start | bytes 1638400 | tf_op jit(solution)/shard_map/all_to_all | solution.py:482

commit v2 on v1

--- a/solution.py
+++ b/solution.py
@@ -60,6 +60,12 @@
     return dot_nt(pick, a.astype(BF)) + dot_nt(pick, b.astype(BF)) + dot_nt(pick, c.astype(BF))
 
 
+def picked_rows(pick, x):
+    a, b, c = thirds(x)
+    pick = pick.astype(BF)
+    return dot(pick, a.astype(BF)) + dot(pick, b.astype(BF)) + dot(pick, c.astype(BF))
+
+
 def stat_rows(lsum, delta, base, row):
     width = lsum.shape[1]
     rows = iota((16, width), 0)
@@ -79,7 +85,7 @@
         jnp.where(iota((8, 256), 1) // 64 == iota((8, 256), 0), 1.0, 0.0),
         g * o[...].astype(F32),
     )
-    lsum = picked_sum(
+    lsum = picked_rows(
         jnp.where(iota((8, 20), 1) == 4 * j + iota((8, 20), 0), 1.0, 0.0), l[...]
     )
     low = iota((TOK, 128), 1) < 64
@@ -131,7 +137,7 @@
                 column,
                 column,
                 column,
-                pl.BlockSpec((TOK, 20), lambda j, s: (0, 0)),
+                pl.BlockSpec((20, TOK), lambda j, s: (0, 0)),
             ],
             out_specs=pl.BlockSpec((N, MSG, 128), lambda j, s: (0, 0, 0)),
         ),
@@ -149,7 +155,7 @@
         buf[n] = jnp.zeros(buf.shape[1:], F32)
         buf[n, 0:TXT, :] = ref[...].astype(F32)
     lbuf[...] = jnp.zeros(lbuf.shape, F32)
-    lbuf[0:TXT, :] = l[...]
+    lbuf[:, 0:TXT] = l[...]
 
     def gather(first, odd, q_rows, k_rows):
         q, k, v = buf[first, q_rows, :], buf[first + 1, k_rows, :], buf[first + 2, k_rows, :]
@@ -171,7 +177,7 @@
     wqg[...] = qg.astype(BF)
     wkv[...] = kv.astype(BF)
     wst[...] = stat_rows(
-        picked_sum(pick, lbuf[0:TXT_Q, :]), picked_sum(ones, product), 0, 0
+        picked_rows(pick, lbuf[:, 0:TXT_Q]), picked_sum(ones, product), 0, 0
     ).astype(BF)
 
     head = 16 + d // 4
@@ -182,8 +188,11 @@
     pick = jnp.where(iota((8, 20), 1) == head, 1.0, 0.0)
     lqg[...] = jnp.where(inside, qg, 0.0).astype(BF)
     lkv[...] = jnp.where(inside, kv, 0.0).astype(BF)
+    lsum = picked_rows(pick, lbuf[...])
     lst[...] = stat_rows(
-        picked_sum(pick, lbuf[q_rows, :]),
+        jnp.where(
+            d % 4 < 2, lsum[:, 0:HALF_Q], pltpu.roll(lsum, lsum.shape[1] - HALF, 1)[:, 0:HALF_Q]
+        ),
         picked_sum(ones, jnp.where(inside, product, 0.0)),
         4,
         0,
@@ -201,11 +210,11 @@
         grid_spec=pltpu.PrefetchScalarGridSpec(
             num_scalar_prefetch=1,
             grid=(1,),
-            in_specs=[whole] * 5 + [shared] * 5 + [pl.BlockSpec((TXT, 20), lambda i, s: (0, 0))],
+            in_specs=[whole] * 5 + [shared] * 5 + [pl.BlockSpec((20, TXT), lambda i, s: (0, 0))],
             out_specs=[pl.BlockSpec(s, lambda i, s_: (0, 0)) for s in shapes],
             scratch_shapes=[
                 pltpu.VMEM((10, HALF + HALF_Q, 128), F32),
-                pltpu.VMEM((HALF + HALF_Q, 20), F32),
+                pltpu.VMEM((20, 512), F32),
             ],
         ),
         out_shape=[jax.ShapeDtypeStruct(s, BF) for s in shapes],
@@ -281,15 +290,15 @@
         lax.fori_loop(0, q_all // qb, q_step, 0)
 
 
-def attend_kernel(recv, wqg, wkv, wst, lqg, lkv, lst, out, tout, *refs):
-    w, h = Head(refs[:9]), Head(refs[9:])
+def fill_whole(w, recv):
     for s in range(N):
         w.fill(TOK * s, recv[s, 0:128, :], recv[s, 128:256, :], recv[s, 384:400, :], 0)
+
+
+def fill_shared(h, recv):
     for m in range(N // 2):
         a, b = 2 * m, 2 * m + 1
-        stat = jnp.where(
-            iota((16, 128), 1) < 64, recv[a, 384:400, :], recv[b, 384:400, :]
-        )
+        stat = jnp.where(iota((16, 128), 1) < 64, recv[a, 384:400, :], recv[b, 384:400, :])
         h.fill(
             128 * m,
             jnp.concatenate([recv[a, 256:320, :], recv[b, 256:320, :]], 0),
@@ -297,6 +306,14 @@
             stat,
             4,
         )
+
+
+def text_pairs_kernel(
+    recv, wqg, wkv, wst, lqg, lkv, lst, tout, w_dkv, w_dqt, h_dkv, h_dqt, *refs
+):
+    w, h = Head(refs[:9]), Head(refs[9:])
+    fill_whole(w, recv)
+    fill_shared(h, recv)
     for m in range(TXT_Q // 128):
         t = slice(128 * m, 128 * m + 128)
         w.fill(S + 128 * m, wqg[t, :], wkv[t, :], wst[:, t], 0)
@@ -309,67 +326,92 @@
     w.block(S, TXT_K, S, TXT_Q)
 
     def whole_text(n, _):
-        at = pl.multiple_of(n * 512, 512)
-        w.block(at, 512, S, TXT_Q)
-        w.block(S, TXT_K, at, 512)
+        at = pl.multiple_of(n * 1024, 1024)
+        w.block(at, 1024, S, TXT_Q)
+        w.block(S, TXT_K, at, 1024)
         return 0
 
-    lax.fori_loop(0, S // 512, whole_text, 0)
+    lax.fori_loop(0, S // 1024, whole_text, 0)
     h.block(SH, HALF, SH, HALF_Q)
-
-    def shared_text(n, _):
-        at = pl.multiple_of(n * 512, 512)
-        h.block(at, 512, SH, HALF_Q)
-        h.block(SH, HALF, at, 512)
-        return 0
-
-    lax.fori_loop(0, SH // 512, shared_text, 0)
-
-    h.blocks(SH, 256, SH, 512)
-    w.blocks(S, 256, S, 512)
+    h.block(0, SH, SH, HALF_Q)
+    h.block(SH, HALF, 0, SH)
+
+    w_dkv[...] = w.dkv[0:S, :]
+    w_dqt[...] = w.dqt[:, 0:S]
+    h_dkv[...] = h.dkv[0:SH, :]
+    h_dqt[...] = h.dqt[:, 0:SH]
 
     factor = jnp.where(iota((128, 128), 1) < 64, SCALE, 1.0)
+
+    def put(at, value):
+        value = value.astype(BF)
+        for n in range(N // 2):
+            tout[n, at : at + value.shape[0], :] = value
+
     for m in range(TXT_Q // 128):
         rows = min(128, TXT_K - 128 * m)
-        tout[128 * m : 128 * m + rows, :] = (
-            w.dkv[S + 128 * m : S + 128 * m + rows, :] * factor[:rows]
-        ).astype(BF)
+        put(128 * m, w.dkv[S + 128 * m : S + 128 * m + rows, :] * factor[:rows])
         lower = h.dqt[:, SH + 128 * m : SH + 128 * m + 128] if m < 2 else jnp.zeros((64, 128), F32)
         both = jnp.concatenate([w.dqt[:, S + 128 * m : S + 128 * m + 128], lower], 0)
-        at = TXT_K + HALF + 128 * m
-        tout[at : at + rows, :] = (both * SCALE).T[:rows].astype(BF)
-    tout[TXT_K : TXT_K + 128, :] = (h.dkv[SH : SH + 128, :] * factor).astype(BF)
-    tout[TXT_K + 128 : TXT_K + HALF, :] = (
-        h.dkv[SH + 128 : SH + HALF, :] * factor[: HALF - 128]
-    ).astype(BF)
-
+        put(TXT_K + HALF + 128 * m, (both * SCALE).T[:rows])
+    put(TXT_K, h.dkv[SH : SH + 128, :] * factor)
+    put(TXT_K + 128, h.dkv[SH + 128 : SH + HALF, :] * factor[: HALF - 128])
+
+
+STATE = [(S, 128), (64, S), (SH, 128), (64, SH)]
+
+
+def text_pairs(recv, texts):
+    full = pl.BlockSpec(memory_space=pltpu.VMEM)
+    return pl.pallas_call(
+        text_pairs_kernel,
+        in_specs=[full] * 7,
+        out_specs=[full] * 5,
+        out_shape=[jax.ShapeDtypeStruct((N // 2, TOUT, 128), BF)]
+        + [jax.ShapeDtypeStruct(s, F32) for s in STATE],
+        scratch_shapes=Head.scratch(W_ROWS) + Head.scratch(L_ROWS),
+        compiler_params=pltpu.CompilerParams(vmem_limit_bytes=VMEM_LIMIT),
+        name="text_pairs",
+    )(recv, *texts)
+
+
+def scales():
+    return jnp.where(iota((128, 128), 1) < 64, SCALE, 1.0)
+
+
+def image_pairs_kernel(recv, a, b, c, d, out, *refs):
+    w, h = Head(refs[:9]), Head(refs[9:])
+    fill_whole(w, recv)
+    fill_shared(h, recv)
+    for source, target in ((a, w.dkv), (b, w.dqt), (c, h.dkv), (d, h.dqt)):
+        target[...] = source[...]
+    h.blocks(SH, 1024, SH, 512)
+    w.blocks(S, 1024, S, 512)
+    factor = scales()
     for s in range(N):
         out[s, 0:128, :] = (w.dkv[128 * s : 128 * s + 128, :] * factor).astype(BF)
-        out[s, 128:192, :] = (h.dkv[64 * s : 64 * s + 64, :] * factor[:64]).astype(BF)
-        a = w.dqt[:, 128 * s : 128 * s + 128] * SCALE
-        both = jnp.concatenate([a, swap_halves(a)], 0).T
-        out[s, 192:256, :] = both[0:64].astype(BF)
+        part = w.dqt[:, 128 * s : 128 * s + 128] * SCALE
+        both = jnp.concatenate([part, swap_halves(part)], 0).T
+        out[s, 128:192, :] = both[0:64].astype(BF)
+        out[s, 192:256, :] = (h.dkv[64 * s : 64 * s + 64, :] * factor[:64]).astype(BF)
     for m in range(N // 2):
-        a = h.dqt[:, 128 * m : 128 * m + 128] * SCALE
-        both = jnp.concatenate([a, pltpu.roll(a, 96, 1)], 0).T
+        part = h.dqt[:, 128 * m : 128 * m + 128] * SCALE
+        both = jnp.concatenate([part, pltpu.roll(part, 96, 1)], 0).T
         out[2 * m, 256:288, :] = both[0:32].astype(BF)
         out[2 * m + 1, 256:288, :] = both[64:96].astype(BF)
 
 
-def attend(recv, texts):
+def image_pairs(recv, state):
     full = pl.BlockSpec(memory_space=pltpu.VMEM)
     return pl.pallas_call(
-        attend_kernel,
-        in_specs=[full] * 7,
-        out_specs=[full] * 2,
-        out_shape=[
-            jax.ShapeDtypeStruct((N, OUT, 128), BF),
-            jax.ShapeDtypeStruct((TOUT, 128), BF),
-        ],
-        scratch_shapes=Head.scratch(W_ROWS) + Head.scratch(L_ROWS),
+        image_pairs_kernel,
+        in_specs=[full] * 5,
+        out_specs=full,
+        out_shape=jax.ShapeDtypeStruct((N, OUT, 128), BF),
+        scratch_shapes=Head.scratch(S) + Head.scratch(SH),
         compiler_params=pltpu.CompilerParams(vmem_limit_bytes=VMEM_LIMIT),
-        name="attend",
-    )(recv, *texts)
+        name="image_pairs",
+    )(recv, *state)
 
 
 def lane_pair(even, odd):
@@ -389,7 +431,7 @@
         keys, values = lane_pair(part(2 * t, slice(0, 128)), part(2 * t + 1, slice(0, 128)))
         dk[:, lanes] = keys.astype(BF)
         dv[:, lanes] = values.astype(BF)
-        first, second = lane_pair(part(2 * t, slice(192, 256)), part(2 * t + 1, slice(192, 256)))
+        first, second = lane_pair(part(2 * t, slice(128, 192)), part(2 * t + 1, slice(128, 192)))
         dq[0:64, lanes] = first.astype(BF)
         dq[64:128, lanes] = second.astype(BF)
     for t in range(2):
@@ -398,7 +440,7 @@
             rows = slice(64 * half, 64 * half + 64)
             keys, values = lane_pair(
                 *(
-                    part(4 * r + half, slice(128, 192)) + part(4 * r + 2 + half, slice(128, 192))
+                    part(4 * r + half, slice(192, 256)) + part(4 * r + 2 + half, slice(192, 256))
                     for r in (2 * t, 2 * t + 1)
                 )
             )
@@ -486,27 +528,55 @@
     return lax.ppermute(x, "core", [(0, 1), (1, 0)])
 
 
-def spread(x, axes):
-    return exchange(jnp.broadcast_to(x[None], (lax.axis_size(axes), *x.shape)), axes)
-
-
-def weight_gradient(og, o):
-    chips = lax.axis_size(CHIPS)
-    quarters = lax.axis_size("y")
+def shifted(x, axis, by):
+    size = lax.axis_size(axis)
+    return lax.ppermute(x, axis, [(i, (i + by) % size) for i in range(size)])
+
+
+def scattered_sum(x, axis, after=()):
+    size, me = lax.axis_size(axis), lax.axis_index(axis)
+    pieces = [
+        shifted(lax.dynamic_index_in_dim(x, (me + by) % size, 0, False), axis, by)
+        for by in range(1, size)
+    ]
+    pieces, _ = lax.optimization_barrier((pieces, after))
+    own = lax.dynamic_index_in_dim(x, me, 0, False).astype(F32)
+    for piece in pieces:
+        own = own + piece.astype(F32)
+    return own.astype(BF)
+
+
+def gathered(x, axis):
+    size, me = lax.axis_size(axis), lax.axis_index(axis)
+    out = jnp.zeros((size, *x.shape), x.dtype)
+    for by in range(size):
+        piece = shifted(x, axis, by) if by else x
+        out = lax.dynamic_update_index_in_dim(out, piece, (me - by) % size, 0)
+    return out
+
+
+def weight_gradient(og, o, before, after):
+    z, xh, y = (lax.axis_size(a) for a in ("z", "xh", "y"))
     core = lax.axis_index("core")
-    blocks = og.T.reshape(chips, 2, -1, og.shape[0])
-    rows = blocks.shape[2]
-    mine = lax.dynamic_index_in_dim(blocks, core, 1, False)
-    theirs = lax.dynamic_index_in_dim(blocks, 1 - core, 1, False)
-    left = jnp.concatenate([mine, other_core(theirs)], 2)
+    tokens = og.shape[0]
+    rows = og.shape[1] // (2 * z * xh)
+    padded = -(-rows // (8 * y)) * 8 * y
+    blocks = og.T.reshape(z, xh, 2, rows, tokens)
+    blocks = jnp.pad(blocks, ((0, 0),) * 3 + ((0, padded - rows), (0, 0)))
+    blocks = blocks.reshape(z, xh, 2, y, padded // y, tokens).transpose(2, 3, 1, 0, 4, 5)
+    mine = lax.dynamic_index_in_dim(blocks, core, 0, False)
+    theirs = lax.dynamic_index_in_dim(blocks, 1 - core, 0, False)
+    left = jnp.concatenate([mine, other_core(theirs)], 4)
     right = jnp.concatenate([o, other_core(o)], 0)
-    term = jnp.einsum("prt,tc->prc", left, right, preferred_element_type=F32).astype(BF)
-    padded = -(-rows // (8 * quarters)) * 8 * quarters
-    term = jnp.pad(term, ((0, 0), (0, padded - rows), (0, 0)))
-    term = term.reshape(chips, quarters, padded // quarters, -1).swapaxes(0, 1)
-    part = exchange(term, "y").astype(F32).sum(0).astype(BF)
-    part = exchange(part, CHIPS).astype(F32).sum(0).astype(BF)
-    part = spread(part, IMG).reshape(quarters, -1, *part.shape).astype(F32).sum(1)
+    part = jnp.dot(left.reshape(-1, 2 * tokens), right, preferred_element_type=F32).astype(BF)
+    part = part.reshape(y, xh, z, padded // y, -1)
+    part, _ = lax.optimization_barrier((part, before))
+    part = scattered_sum(part, "y", after)
+    for axis in ("xh", "z"):
+        part = scattered_sum(part, axis)
+    if lax.axis_size("xl") > 1:
+        part = (part.astype(F32) + shifted(part, "xl", 1).astype(F32)).astype(BF)
+    part = gathered(part, "y").astype(F32)
     return part.reshape(padded, -1)[:rows]
 
 
@@ -535,8 +605,9 @@
         image_key[0],
         image_value[0],
         image_output[0],
-        image_logsum[0],
+        image_logsum[0].T,
     )
+    send, upstream, outputs = lax.optimization_barrier((send, output_grad[0], image_output[0]))
     recv = exchange(send, SEQ)
     texts = text_prep(
         device,
@@ -545,13 +616,14 @@
         text_value[0],
         text_output[0],
         text_grad[0],
-        text_logsum[0],
+        text_logsum[0].T,
     )
-    out, text_out = attend(recv, texts)
-    mine = spread(text_out, CHIPS)
+    text_out, *state = text_pairs(recv, texts)
+    mine = exchange(text_out, CHIPS)
     text_grads = unpack_text(core, mine, other_core(mine))
+    out = image_pairs(recv, state)
     grads = unpack(exchange(out, SEQ))
-    weight_grad = weight_gradient(output_grad[0], image_output[0])
+    weight_grad = weight_gradient(upstream, outputs, texts, (out, mine))
     return (*(g[None] for g in grads), *(g[None] for g in text_grads), weight_grad)
 
 

time: 183 us -> 170 us (0.929)
  blocking collectives: 18.3 us -> 0 us
  starting transfers between devices: 28.6 us -> 42 us
  waiting for transfers between devices: 70.8 us -> 63.9 us
  Pallas kernels: 49.6 us -> 46.1 us
  other arithmetic: 1.83 us -> 4.16 us
    all_to_all x5 -> x3, waiting for transfers between devices: 69.5 us -> 19.2 us  [exchange(): return lax.all_to_all(x, axes, 0, 0, tiled=True)]
    ppermute x0 -> x11, waiting for transfers between devices: none -> 44.7 us  [shifted(): return lax.ppermute(x, axis, [(i, (i + by) % size) for i in range(size)])]
    ppermute x0 -> x11, starting transfers between devices: none -> 18.3 us  [shifted(): return lax.ppermute(x, axis, [(i, (i + by) % size) for i in range(size)])]
    all_to_all x1 -> x0, blocking collectives: 18.3 us -> none  [exchange(): return lax.all_to_all(x, axes, 0, 0, tiled=True)]
    all_to_all x5 -> x3, starting transfers between devices: 27.7 us -> 21.9 us  [exchange(): return lax.all_to_all(x, axes, 0, 0, tiled=True)]
    unnamed x12 -> x18, local copies, waits for them, and re-layouts: 3.46 us -> 6.94 us
    broadcast_in_dim x2 -> x1, local copies, waits for them, and re-layouts: 3.37 us -> 0.03 us  [gathered(): out = jnp.zeros((size, *x.shape), x.dtype)]
    convert_element_type x0 -> x3, other arithmetic: none -> 3.2 us  [scattered_sum(): return own.astype(BF)]
  transfers between devices with their start and end apart: 8 -> 17, of which waited for: 6 -> 7; matrix products, arithmetic and copies ran while one was open for 4% -> 4% of each run, Pallas kernels for 20% -> 20%
where the time goes in v2:
time: 170 us
  waiting for transfers between devices  63.9 us (38%)
  Pallas kernels  46.1 us (27%)
  starting transfers between devices  42 us (25%)
  local copies, waits for them, and re-layouts  10.5 us (6%)
  other arithmetic  4.16 us (2%)
  matrix products  2.19 us (1%)
    ppermute x11, waiting for transfers between devices, shifted(): return lax.ppermute(x, axis, [(i, (i + by) % size) for i in range(size)])  44.7 us
    all_to_all x3, starting transfers between devices, exchange(): return lax.all_to_all(x, axes, 0, 0, tiled=True)  21.9 us
    all_to_all x3, waiting for transfers between devices, exchange(): return lax.all_to_all(x, axes, 0, 0, tiled=True)  19.2 us
    pallas_call x1, Pallas kernels, image_pairs(): pl.pallas_call(image_pairs_kernel, in_specs=[full] * 5, out_specs=full, o...  18.6 us
    ppermute x11, starting transfers between devices, shifted(): return lax.ppermute(x, axis, [(i, (i + by) % size) for i in range(size)])  18.3 us
    pallas_call x1, Pallas kernels, text_pairs(): pl.pallas_call(text_pairs_kernel, in_specs=[full] * 7, out_specs=[full] *...  10 us
    pallas_call x1, Pallas kernels, pack(): pl.pallas_call(pack_kernel, grid_spec=pltpu.PrefetchScalarGridSpec(num_sc...  7.75 us
    unnamed x18, local copies, waits for them, and re-layouts  6.94 us
  transfers between devices with their start and end apart: 17, of which 7 were waited for; matrix products, arithmetic and copies ran while one was open for 4% of the time, Pallas kernels for 20%

profile of v2, /device:TPU:1, one launch (start us, length us, event | category | flops | bytes accessed | tf_op | source)
XLA Modules:
  0.0 169.8 jit_solution(2582510410297182042)
XLA Ops:
  0.6 1.3 copy.28
  1.9 7.8 %pack.1 = bf16[16,400,128]{2,1,0:T(8,128)(2,1)} custom-call(s32[1]{0:T(128)} %bitcast.index, bf16[128,2432]{1,0:T(8,128)(2,1)} %bitcast.86, bf16[2432,1280]{1,0:T(8,128)(2,1)} %w.1, bf16[128,1280]{1,0:T(8,128)(2,1)} %bitcast.94, bf16[128,1280]{1,0:T(8,128)(2,1)} %bitcast.95, bf16[128,1280]{1,0:T(8,128)(2,1)} %bitcast.96, bf16[128,1280]{1,0:T(8,128)(2,1)} %bitcast.91, ...), custom_call_target="tpu_custom_call" | custom-call | tf_op jit(solution)/shard_map/pack/pallas_call | solution.py:128
  9.7 9.4 %all-to-all-start = ((bf16[16,400,128]{2,1,0:T(8,128)(2,1)}), bf16[16,400,128]{2,1,0:T(8,128)(2,1)S(1)}, u32[]{:S(2)}, u32[]{:S(2)}) async-start(bf16[16,400,128]{2,1,0:T(8,128)(2,1)} %pack.1), calls=%async_computation | async-start | bytes 3276800 | tf_op jit(solution)/shard_map/all_to_all | solution.py:524
  19.2 0.3 copy.20
  19.5 0.1 pad.4
  19.5 0.8 dynamic-slice_bitcast_fusion.5
  20.4 0.1 collective-permute-start.1
  20.5 0.4 collective-permute-start.2
  20.9 0.6 copy.27
  21.5 2.3 %text_prep.1 = (bf16[384,128]{1,0:T(8,128)(2,1)}, bf16[384,128]{1,0:T(8,128)(2,1)}, bf16[16,384]{1,0:T(8,128)(2,1)}, bf16[256,128]{1,0:T(8,128)(2,1)}, bf16[256,...) custom-call(s32[1]{0:T(128)} %bitcast.index, bf16[333,1280]{1,0:T(8,128)(2,1)} %bitcast.74, bf16[333,1280]{1,0:T(8,128)(2,1)} %bitcast.76, ...), custom_call_target="tpu_custom_call" | custom-call | tf_op jit(solution)/shard_map/text_prep/pallas_call | solution.py:208
  23.8 18.8 %all-to-all-done.recv = bf16[16,400,128]{2,1,0:T(8,128)(2,1)S(1)} async-done(((bf16[16,400,128]{2,1,0:T(8,128)(2,1)}), bf16[16,400,128]{2,1,0:T(8,128)(2,1)S(1)}, u32[]{:S(2)}, u32[]{:S(2)}) %all-to-all-start) | async-done | bytes 1638432 | tf_op jit(solution)/shard_map/all_to_all | solution.py:524
  42.7 1.2 copy-done
  43.9 10.0 %text_pairs.1 = (bf16[8,848,128]{2,1,0:T(8,128)(2,1)}, f32[2048,128]{1,0:T(8,128)}, f32[64,2048]{1,0:T(8,128)}, f32[1024,128]{1,0:T(8,128)}, f32[64,1024]{1,0:T(8,128)}) custom-call(bf16[16,400,128]{2,1,0:T(8,128)(2,1)} %copy-done, bf16[384,128]{1,0:T(8,128)(2,1)} %get-tuple-element.35.wqg, bf16[384,128]{1,0:T(8,128)(2,1)} %get-tuple-element.36.wkv, ...), custom_call_target="tpu_custom_call" | custom-call | tf_op jit(solution)/shard_map/text_pairs/pallas_call | solution.py:366
  53.9 4.3 %all-to-all-start.2 = ((bf16[8,848,128]{2,1,0:T(8,128)(2,1)}), bf16[8,848,128]{2,1,0:T(8,128)(2,1)}, u32[]{:S(2)}, u32[]{:S(2)}) async-start(bf16[8,848,128]{2,1,0:T(8,128)(2,1)} %get-tuple-element.48), calls=%async_computation.2 | async-start | bytes 3473408 | tf_op jit(solution)/shard_map/all_to_all | solution.py:524
  58.2 0.8 copy.21
  59.1 0.7 copy-done.6
  59.8 2.2 %convolution_convert_fusion = bf16[1280,1280]{1,0:T(8,128)(2,1)S(1)} fusion(bf16[1280,128]{1,0:T(8,128)(2,1)S(1)} %bitcast.90, bf16[1280,128]{1,0:T(8,128)(2,1)} %bitcast.89, bf16[128,1280]{1,0:T(8,128)(2,1)} %copy-done.6, bf16[128,1280]{1,0:T(8,128)(2,1)} %bitcast.92), kind=kOutput, calls=%fused_computation | convolution fusion | flops 843120640 | bytes 4587520 | tf_op jit(solution)/shard_map/dot_general | solution.py:571
  62.0 1.5 dynamic-slice_bitcast_fusion
  63.5 1.3 collective-permute-start.3
  64.8 2.6 %collective-permute-start.4 = (bf16[2,4,40,1280]{3,2,1,0:T(8,128)(2,1)}, bf16[2,4,40,1280]{3,2,1,0:T(8,128)(2,1)}, u32[]{:S(2)}, u32[]{:S(2)}) collective-permute-start(bf16[2,4,40,1280]{3,2,1,0:T(8,128)(2,1)} %get-tuple-element.64), channel_id=1, source_target_pairs={{0,64},{32,96},{64,0},{96,32},{1,65},{33,97},{65,1},{97,33},{2,66}... | collective-permute-start | bytes 2457608 | tf_op jit(solution)/shard_map/ppermute | solution.py:533
  67.4 1.1 collective-permute-start.5
  68.4 18.6 %image_pairs.1 = bf16[16,288,128]{2,1,0:T(8,128)(2,1)} custom-call(bf16[16,400,128]{2,1,0:T(8,128)(2,1)} %copy-done, f32[2048,128]{1,0:T(8,128)} %get-tuple-element.41.a, f32[64,2048]{1,0:T(8,128)} %get-tuple-element.42.b, f32[1024,128]{1,0:T(8,128)} %get-tuple-element.43.c, f32[64,1024]{1,0:T(8,128)} %get-tuple-element.44.d), custom_call_target="tpu_custom_call" | custom-call | tf_op jit(solution)/shard_map/image_pairs/pallas_call | solution.py:406
  87.0 15.6 %collective-permute-done.4 = bf16[2,4,40,1280]{3,2,1,0:T(8,128)(2,1)} collective-permute-done((bf16[2,4,40,1280]{3,2,1,0:T(8,128)(2,1)}, bf16[2,4,40,1280]{3,2,1,0:T(8,128)(2,1)}, u32[]{:S(2)}, u32[]{:S(2)}) %collective-permute-start.4) | collective-permute-done | bytes 819232 | tf_op jit(solution)/shard_map/ppermute | solution.py:533
  102.6 2.0 %fusion.2 = bf16[2,4,40,1280]{3,2,1,0:T(8,128)(2,1)S(1)} fusion(bf16[2,4,40,1280]{3,2,1,0:T(8,128)(2,1)} %collective-permute-done.5, bf16[2,4,40,1280]{3,2,1,0:T(8,128)(2,1)} %collective-permute-done.4, bf16[2,4,40,1280]{3,2,1,0:T(8,128)(2,1)} %collective-permute-done.3, bf16[4,2,4,40,1280]{4,3,2,1,0:T(8,128)(2,1)S(1)} %bitcast.73, s32[]{:T(128)S(6)} %select_n.102), kind=kLoop, calls=%fused_computation.4 | loop fusion | flops 3276800 | bytes 4096004 | tf_op jit(solution)/shard_map/convert_element_type | solution.py:546
  104.6 0.0 copy-start.2
  104.6 0.9 copy-done.2
  105.5 2.6 %collective-permute-start.6 = (bf16[4,40,1280]{2,1,0:T(8,128)(2,1)S(1)}, bf16[4,40,1280]{2,1,0:T(8,128)(2,1)S(1)}, u32[]{:S(2)}, u32[]{:S(2)}) collective-permute-start(bf16[4,40,1280]{2,1,0:T(8,128)(2,1)S(1)} %dynamic-slice_bitcast_fusion.3), channel_id=1, source_target_pairs={{0,2},{2,0},{1,3},{3,1},{4,6},{6,4},{5,7},{7,5},{8,10},{10,8},{9,1... | collective-permute-start | bytes 1228808 | tf_op jit(solution)/shard_map/ppermute | solution.py:533
  108.2 8.1 %collective-permute-done.6 = bf16[4,40,1280]{2,1,0:T(8,128)(2,1)S(1)} collective-permute-done((bf16[4,40,1280]{2,1,0:T(8,128)(2,1)S(1)}, bf16[4,40,1280]{2,1,0:T(8,128)(2,1)S(1)}, u32[]{:S(2)}, u32[]{:S(2)}) %collective-permute-start.6) | collective-permute-done | bytes 409632 | tf_op jit(solution)/shard_map/ppermute | solution.py:533
  116.2 1.1 fusion.3
  117.4 0.9 collective-permute-start.7
  118.2 2.4 %collective-permute-start.8 = (bf16[40,1280]{1,0:T(8,128)(2,1)S(1)}, bf16[40,1280]{1,0:T(8,128)(2,1)S(1)}, u32[]{:S(2)}, u32[]{:S(2)}) collective-permute-start(bf16[40,1280]{1,0:T(8,128)(2,1)S(1)} %get-tuple-element.69), channel_id=1, source_target_pairs={{0,8},{4,12},{8,0},{12,4},{1,9},{5,13},{9,1},{13,5},{2,10},{6,14},... | collective-permute-start | bytes 307208 | tf_op jit(solution)/shard_map/ppermute | solution.py:533
  120.6 1.2 collective-permute-start.9
  121.8 8.2 %all-to-all-start.1 = ((bf16[16,288,128]{2,1,0:T(8,128)(2,1)}), bf16[16,288,128]{2,1,0:T(8,128)(2,1)S(1)}, u32[]{:S(2)}, u32[]{:S(2)}) async-start(bf16[16,288,128]{2,1,0:T(8,128)(2,1)} %image_pairs.1), calls=%async_computation.1 | async-start | bytes 2359296 | tf_op jit(solution)/shard_map/all_to_all | solution.py:524
  130.0 0.1 fusion.12
  130.1 0.5 collective-permute-start.10
  130.6 15.9 %collective-permute-done.10 = bf16[40,1280]{1,0:T(8,128)(2,1)S(1)} collective-permute-done((bf16[40,1280]{1,0:T(8,128)(2,1)S(1)}, bf16[40,1280]{1,0:T(8,128)(2,1)S(1)}, u32[]{:S(2)}, u32[]{:S(2)}) %collective-permute-start.10) | collective-permute-done | bytes 102432 | tf_op jit(solution)/shard_map/ppermute | solution.py:533
  146.5 1.7 %collective-permute-start.11 = (bf16[40,1280]{1,0:T(8,128)(2,1)S(1)}, bf16[40,1280]{1,0:T(8,128)(2,1)S(1)}, u32[]{:S(2)}, u32[]{:S(2)}) collective-permute-start(bf16[40,1280]{1,0:T(8,128)(2,1)S(1)} %get-tuple-element.62), channel_id=1, source_target_pairs={{0,32},{32,64},{64,96},{96,0},{1,33},{33,65},{65,97},{97,1},{2,34}... | collective-permute-start | bytes 307208 | tf_op jit(solution)/shard_map/ppermute | solution.py:533
  148.2 0.4 all-to-all-done.1.recv
  148.6 1.0 copy-done.1
  149.6 2.6 %unpack.1 = (bf16[128,1280]{1,0:T(8,128)(2,1)}, bf16[128,1280]{1,0:T(8,128)(2,1)}, bf16[128,1280]{1,0:T(8,128)(2,1)}) custom-call(bf16[16,288,128]{2,1,0:T(8,128)(2,1)} %copy-done.1), custom_call_target="tpu_custom_call" | custom-call | tf_op jit(solution)/shard_map/unpack/pallas_call | solution.py:462
  152.2 1.3 collective-permute-start
  153.6 2.1 %collective-permute-start.12 = (bf16[40,1280]{1,0:T(8,128)(2,1)S(1)}, bf16[40,1280]{1,0:T(8,128)(2,1)S(1)}, u32[]{:S(2)}, u32[]{:S(2)}) collective-permute-start(bf16[40,1280]{1,0:T(8,128)(2,1)S(1)} %get-tuple-element.62), channel_id=1, source_target_pairs={{0,64},{32,96},{64,0},{96,32},{1,65},{33,97},{65,1},{97,33},{2,66}... | collective-permute-start | bytes 307208 | tf_op jit(solution)/shard_map/ppermute | solution.py:533
  155.7 1.9 %collective-permute-start.13 = (bf16[40,1280]{1,0:T(8,128)(2,1)S(1)}, bf16[40,1280]{1,0:T(8,128)(2,1)S(1)}, u32[]{:S(2)}, u32[]{:S(2)}) collective-permute-start(bf16[40,1280]{1,0:T(8,128)(2,1)S(1)} %get-tuple-element.62), channel_id=1, source_target_pairs={{0,96},{32,0},{64,32},{96,64},{1,97},{33,1},{65,33},{97,65},{2,98}... | collective-permute-start | bytes 307208 | tf_op jit(solution)/shard_map/ppermute | solution.py:533
  157.6 2.0 %collective-permute-done.12 = bf16[40,1280]{1,0:T(8,128)(2,1)S(1)} collective-permute-done((bf16[40,1280]{1,0:T(8,128)(2,1)S(1)}, bf16[40,1280]{1,0:T(8,128)(2,1)S(1)}, u32[]{:S(2)}, u32[]{:S(2)}) %collective-permute-start.12) | collective-permute-done | bytes 102432 | tf_op jit(solution)/shard_map/ppermute | solution.py:533
  159.6 3.2 %collective-permute-done.13 = bf16[40,1280]{1,0:T(8,128)(2,1)S(1)} collective-permute-done((bf16[40,1280]{1,0:T(8,128)(2,1)S(1)}, bf16[40,1280]{1,0:T(8,128)(2,1)S(1)}, u32[]{:S(2)}, u32[]{:S(2)}) %collective-permute-start.13) | collective-permute-done | bytes 102432 | tf_op jit(solution)/shard_map/ppermute | solution.py:533
  162.8 0.9 slice_convert_fusion
  163.7 1.2 copy-done.4
  164.9 4.8 %unpack_text.1 = (bf16[333,1280]{1,0:T(8,128)(2,1)}, bf16[333,1280]{1,0:T(8,128)(2,1)}, bf16[333,1280]{1,0:T(8,128)(2,1)}) custom-call(s32[1]{0:T(128)} %bitcast.16.core, bf16[8,848,128]{2,1,0:T(8,128)(2,1)} %all-to-all-done.2.mine, bf16[8,848,128]{2,1,0:T(8,128)(2,1)} %copy-done.4), custom_call_target="tpu_custom_call" | custom-call | tf_op jit(solution)/shard_map/unpack_text/pallas_call | solution.py:513
  (28 shorter events, 0.2 us)
Async XLA Ops:
  9.7 9.4 %copy-start.3 = (bf16[1,128,2432]{2,1,0:T(8,128)(2,1)S(1)}, bf16[1,128,2432]{2,1,0:T(8,128)(2,1)}, u32[]{:S(2)}) copy-start(bf16[1,128,2432]{2,1,0:T(8,128)(2,1)} %param.17) | copy-start | bytes 1867780
  9.7 33.0 %all-to-all-start = ((bf16[16,400,128]{2,1,0:T(8,128)(2,1)}), bf16[16,400,128]{2,1,0:T(8,128)(2,1)S(1)}, u32[]{:S(2)}, u32[]{:S(2)}) async-start(bf16[16,400,128]{2,1,0:T(8,128)(2,1)} %pack.1), calls=%async_computation | async-start | bytes 3276800 | tf_op jit(solution)/shard_map/all_to_all | solution.py:524
  19.1 1.3 copy-start.5
  19.1 1.7 %copy-start.7 = (f32[1,333,20]{1,0,2:T(1,128)S(1)}, f32[1,333,20]{1,0,2:T(1,128)}, u32[]{:S(2)}) copy-start(f32[1,333,20]{1,0,2:T(1,128)} %param.24) | copy-start | bytes 79924
  20.4 38.6 %collective-permute-start.1 = (bf16[4,2,4,40,128]{4,3,0,1,2:T(8,128)(2,1)}, bf16[4,2,4,40,128]{4,3,0,1,2:T(8,128)(2,1)S(1)}, u32[]{:S(2)}, u32[]{:S(2)}) collective-permute-start(bf16[4,2,4,40,128]{4,3,0,1,2:T(8,128)(2,1)} %get-tuple-element.67), channel_id=1, source_target_pairs={{0,1},{1,0},{2,3},{3,2},{4,5},{5,4},{6,7},{7,6},{8,9},{9,8},{10,11... | collective-permute-start | bytes 983048 | tf_op jit(solution)/shard_map/ppermute | solution.py:528
  20.5 38.6 %collective-permute-start.2 = (bf16[128,1280]{1,0:T(8,128)(2,1)S(1)}, bf16[128,1280]{1,0:T(8,128)(2,1)S(1)}, u32[]{:S(2)}, u32[]{:S(2)}) collective-permute-start(bf16[128,1280]{1,0:T(8,128)(2,1)S(1)} %bitcast.93), channel_id=1, source_target_pairs={{0,1},{1,0},{2,3},{3,2},{4,5},{5,4},{6,7},{7,6},{8,9},{9,8},{10,11... | collective-permute-start | bytes 983048 | tf_op jit(solution)/shard_map/ppermute | solution.py:528
  42.7 1.2 copy-start
  53.9 48.7 %all-to-all-start.2 = ((bf16[8,848,128]{2,1,0:T(8,128)(2,1)}), bf16[8,848,128]{2,1,0:T(8,128)(2,1)}, u32[]{:S(2)}, u32[]{:S(2)}) async-start(bf16[8,848,128]{2,1,0:T(8,128)(2,1)} %get-tuple-element.48), calls=%async_computation.2 | async-start | bytes 3473408 | tf_op jit(solution)/shard_map/all_to_all | solution.py:524
  59.0 0.7 copy-start.6
  63.5 23.5 %collective-permute-start.3 = (bf16[2,4,40,1280]{3,2,1,0:T(8,128)(2,1)}, bf16[2,4,40,1280]{3,2,1,0:T(8,128)(2,1)}, u32[]{:S(2)}, u32[]{:S(2)}) collective-permute-start(bf16[2,4,40,1280]{3,2,1,0:T(8,128)(2,1)} %get-tuple-element.65), channel_id=1, source_target_pairs={{0,32},{32,64},{64,96},{96,0},{1,33},{33,65},{65,97},{97,1},{2,34}... | collective-permute-start | bytes 2457608 | tf_op jit(solution)/shard_map/ppermute | solution.py:533
  64.8 37.8 %collective-permute-start.4 = (bf16[2,4,40,1280]{3,2,1,0:T(8,128)(2,1)}, bf16[2,4,40,1280]{3,2,1,0:T(8,128)(2,1)}, u32[]{:S(2)}, u32[]{:S(2)}) collective-permute-start(bf16[2,4,40,1280]{3,2,1,0:T(8,128)(2,1)} %get-tuple-element.64), channel_id=1, source_target_pairs={{0,64},{32,96},{64,0},{96,32},{1,65},{33,97},{65,1},{97,33},{2,66}... | collective-permute-start | bytes 2457608 | tf_op jit(solution)/shard_map/ppermute | solution.py:533
  67.4 35.2 %collective-permute-start.5 = (bf16[2,4,40,1280]{3,2,1,0:T(8,128)(2,1)}, bf16[2,4,40,1280]{3,2,1,0:T(8,128)(2,1)}, u32[]{:S(2)}, u32[]{:S(2)}) collective-permute-start(bf16[2,4,40,1280]{3,2,1,0:T(8,128)(2,1)} %get-tuple-element.63), channel_id=1, source_target_pairs={{0,96},{32,0},{64,32},{96,64},{1,97},{33,1},{65,33},{97,65},{2,98}... | collective-permute-start | bytes 2457608 | tf_op jit(solution)/shard_map/ppermute | solution.py:533
  104.6 0.9 copy-start.2
  105.5 10.7 %collective-permute-start.6 = (bf16[4,40,1280]{2,1,0:T(8,128)(2,1)S(1)}, bf16[4,40,1280]{2,1,0:T(8,128)(2,1)S(1)}, u32[]{:S(2)}, u32[]{:S(2)}) collective-permute-start(bf16[4,40,1280]{2,1,0:T(8,128)(2,1)S(1)} %dynamic-slice_bitcast_fusion.3), channel_id=1, source_target_pairs={{0,2},{2,0},{1,3},{3,1},{4,6},{6,4},{5,7},{7,5},{8,10},{10,8},{9,1... | collective-permute-start | bytes 1228808 | tf_op jit(solution)/shard_map/ppermute | solution.py:533
  117.4 12.6 %collective-permute-start.7 = (bf16[40,1280]{1,0:T(8,128)(2,1)S(1)}, bf16[40,1280]{1,0:T(8,128)(2,1)S(1)}, u32[]{:S(2)}, u32[]{:S(2)}) collective-permute-start(bf16[40,1280]{1,0:T(8,128)(2,1)S(1)} %get-tuple-element.70), channel_id=1, source_target_pairs={{0,4},{4,8},{8,12},{12,0},{1,5},{5,9},{9,13},{13,1},{2,6},{6,10},{... | collective-permute-start | bytes 307208 | tf_op jit(solution)/shard_map/ppermute | solution.py:533
  118.2 11.8 %collective-permute-start.8 = (bf16[40,1280]{1,0:T(8,128)(2,1)S(1)}, bf16[40,1280]{1,0:T(8,128)(2,1)S(1)}, u32[]{:S(2)}, u32[]{:S(2)}) collective-permute-start(bf16[40,1280]{1,0:T(8,128)(2,1)S(1)} %get-tuple-element.69), channel_id=1, source_target_pairs={{0,8},{4,12},{8,0},{12,4},{1,9},{5,13},{9,1},{13,5},{2,10},{6,14},... | collective-permute-start | bytes 307208 | tf_op jit(solution)/shard_map/ppermute | solution.py:533
  120.6 9.3 %collective-permute-start.9 = (bf16[40,1280]{1,0:T(8,128)(2,1)S(1)}, bf16[40,1280]{1,0:T(8,128)(2,1)S(1)}, u32[]{:S(2)}, u32[]{:S(2)}) collective-permute-start(bf16[40,1280]{1,0:T(8,128)(2,1)S(1)} %get-tuple-element.68), channel_id=1, source_target_pairs={{0,12},{4,0},{8,4},{12,8},{1,13},{5,1},{9,5},{13,9},{2,14},{6,2},{... | collective-permute-start | bytes 307208 | tf_op jit(solution)/shard_map/ppermute | solution.py:533
  121.8 26.8 %all-to-all-start.1 = ((bf16[16,288,128]{2,1,0:T(8,128)(2,1)}), bf16[16,288,128]{2,1,0:T(8,128)(2,1)S(1)}, u32[]{:S(2)}, u32[]{:S(2)}) async-start(bf16[16,288,128]{2,1,0:T(8,128)(2,1)} %image_pairs.1), calls=%async_computation.1 | async-start | bytes 2359296 | tf_op jit(solution)/shard_map/all_to_all | solution.py:524
  130.1 16.4 %collective-permute-start.10 = (bf16[40,1280]{1,0:T(8,128)(2,1)S(1)}, bf16[40,1280]{1,0:T(8,128)(2,1)S(1)}, u32[]{:S(2)}, u32[]{:S(2)}) collective-permute-start(bf16[40,1280]{1,0:T(8,128)(2,1)S(1)} %fusion.12), channel_id=1, source_target_pairs={{0,16},{16,0},{1,17},{17,1},{2,18},{18,2},{3,19},{19,3},{4,20},{20... | collective-permute-start | bytes 307208 | tf_op jit(solution)/shard_map/ppermute | solution.py:533
  146.5 11.1 %collective-permute-start.11 = (bf16[40,1280]{1,0:T(8,128)(2,1)S(1)}, bf16[40,1280]{1,0:T(8,128)(2,1)S(1)}, u32[]{:S(2)}, u32[]{:S(2)}) collective-permute-start(bf16[40,1280]{1,0:T(8,128)(2,1)S(1)} %get-tuple-element.62), channel_id=1, source_target_pairs={{0,32},{32,64},{64,96},{96,0},{1,33},{33,65},{65,97},{97,1},{2,34}... | collective-permute-start | bytes 307208 | tf_op jit(solution)/shard_map/ppermute | solution.py:533
  148.6 1.0 copy-start.1
  152.2 11.5 %collective-permute-start = (bf16[8,848,128]{2,1,0:T(8,128)(2,1)}, bf16[8,848,128]{2,1,0:T(8,128)(2,1)S(1)}, u32[]{:S(2)}, u32[]{:S(2)}) collective-permute-start(bf16[8,848,128]{2,1,0:T(8,128)(2,1)} %all-to-all-done.2.mine), channel_id=1, source_target_pairs={{0,1},{1,0},{2,3},{3,2},{4,5},{5,4},{6,7},{7,6},{8,9},{9,8},{10,11... | collective-permute-start | bytes 5210120 | tf_op jit(solution)/shard_map/ppermute | solution.py:528
  153.6 6.0 %collective-permute-start.12 = (bf16[40,1280]{1,0:T(8,128)(2,1)S(1)}, bf16[40,1280]{1,0:T(8,128)(2,1)S(1)}, u32[]{:S(2)}, u32[]{:S(2)}) collective-permute-start(bf16[40,1280]{1,0:T(8,128)(2,1)S(1)} %get-tuple-element.62), channel_id=1, source_target_pairs={{0,64},{32,96},{64,0},{96,32},{1,65},{33,97},{65,1},{97,33},{2,66}... | collective-permute-start | bytes 307208 | tf_op jit(solution)/shard_map/ppermute | solution.py:533
  155.7 7.1 %collective-permute-start.13 = (bf16[40,1280]{1,0:T(8,128)(2,1)S(1)}, bf16[40,1280]{1,0:T(8,128)(2,1)S(1)}, u32[]{:S(2)}, u32[]{:S(2)}) collective-permute-start(bf16[40,1280]{1,0:T(8,128)(2,1)S(1)} %get-tuple-element.62), channel_id=1, source_target_pairs={{0,96},{32,0},{64,32},{96,64},{1,97},{33,1},{65,33},{97,65},{2,98}... | collective-permute-start | bytes 307208 | tf_op jit(solution)/shard_map/ppermute | solution.py:533
  163.7 1.2 copy-start.4

commit v3 on v2

--- a/solution.py
+++ b/solution.py
@@ -28,6 +28,7 @@
 MSG = 400
 OUT = 288
 TOUT = TXT_K + HALF + TXT_K
+WOUT = 400
 VMEM_LIMIT = 56 * 2**20
 
 
@@ -336,6 +337,7 @@
     h.block(0, SH, SH, HALF_Q)
     h.block(SH, HALF, 0, SH)
 
+    tout[:, 0:WOUT, :] = jnp.zeros((N // 2, WOUT, 128), BF)
     w_dkv[...] = w.dkv[0:S, :]
     w_dqt[...] = w.dqt[:, 0:S]
     h_dkv[...] = h.dkv[0:SH, :]
@@ -346,7 +348,7 @@
     def put(at, value):
         value = value.astype(BF)
         for n in range(N // 2):
-            tout[n, at : at + value.shape[0], :] = value
+            tout[n, WOUT + at : WOUT + at + value.shape[0], :] = value
 
     for m in range(TXT_Q // 128):
         rows = min(128, TXT_K - 128 * m)
@@ -367,7 +369,7 @@
         text_pairs_kernel,
         in_specs=[full] * 7,
         out_specs=[full] * 5,
-        out_shape=[jax.ShapeDtypeStruct((N // 2, TOUT, 128), BF)]
+        out_shape=[jax.ShapeDtypeStruct((N // 2, WOUT + TOUT, 128), BF)]
         + [jax.ShapeDtypeStruct(s, F32) for s in STATE],
         scratch_shapes=Head.scratch(W_ROWS) + Head.scratch(L_ROWS),
         compiler_params=pltpu.CompilerParams(vmem_limit_bytes=VMEM_LIMIT),
@@ -473,6 +475,7 @@
     odd_core = core[0] == 1
 
     def part(d, rows):
+        rows = slice(WOUT + rows.start, WOUT + rows.stop)
         a, b = mine[d // 2, rows, :].astype(F32), other[d // 2, rows, :].astype(F32)
         return jnp.where(odd_core, b, a) if d % 2 == 0 else jnp.where(odd_core, a, b)
 
@@ -533,19 +536,6 @@
     return lax.ppermute(x, axis, [(i, (i + by) % size) for i in range(size)])
 
 
-def scattered_sum(x, axis, after=()):
-    size, me = lax.axis_size(axis), lax.axis_index(axis)
-    pieces = [
-        shifted(lax.dynamic_index_in_dim(x, (me + by) % size, 0, False), axis, by)
-        for by in range(1, size)
-    ]
-    pieces, _ = lax.optimization_barrier((pieces, after))
-    own = lax.dynamic_index_in_dim(x, me, 0, False).astype(F32)
-    for piece in pieces:
-        own = own + piece.astype(F32)
-    return own.astype(BF)
-
-
 def gathered(x, axis):
     size, me = lax.axis_size(axis), lax.axis_index(axis)
     out = jnp.zeros((size, *x.shape), x.dtype)
@@ -555,29 +545,69 @@
     return out
 
 
-def weight_gradient(og, o, before, after):
+def weight_operands(og, o):
     z, xh, y = (lax.axis_size(a) for a in ("z", "xh", "y"))
-    core = lax.axis_index("core")
+    core, me = lax.axis_index("core"), lax.axis_index("y")
     tokens = og.shape[0]
     rows = og.shape[1] // (2 * z * xh)
     padded = -(-rows // (8 * y)) * 8 * y
-    blocks = og.T.reshape(z, xh, 2, rows, tokens)
-    blocks = jnp.pad(blocks, ((0, 0),) * 3 + ((0, padded - rows), (0, 0)))
-    blocks = blocks.reshape(z, xh, 2, y, padded // y, tokens).transpose(2, 3, 1, 0, 4, 5)
+    blocks = og.T.reshape(z * xh, 2, rows, tokens)
+    blocks = jnp.pad(blocks, ((0, 0),) * 2 + ((0, padded - rows), (0, 0)))
+    blocks = blocks.reshape(z * xh, 2, y, padded // y, tokens).transpose(1, 2, 0, 3, 4)
+    blocks = blocks.reshape(2, y, -1, tokens)
     mine = lax.dynamic_index_in_dim(blocks, core, 0, False)
-    theirs = lax.dynamic_index_in_dim(blocks, 1 - core, 0, False)
-    left = jnp.concatenate([mine, other_core(theirs)], 4)
-    right = jnp.concatenate([o, other_core(o)], 0)
-    part = jnp.dot(left.reshape(-1, 2 * tokens), right, preferred_element_type=F32).astype(BF)
-    part = part.reshape(y, xh, z, padded // y, -1)
-    part, _ = lax.optimization_barrier((part, before))
-    part = scattered_sum(part, "y", after)
-    for axis in ("xh", "z"):
-        part = scattered_sum(part, axis)
+    theirs = other_core(lax.dynamic_index_in_dim(blocks, 1 - core, 0, False))
+    both = jnp.concatenate([mine, theirs], 2)
+    left = [lax.dynamic_index_in_dim(both, me, 0, False)]
+    right = [o]
+    for by in range(1, y):
+        left.append(shifted(lax.dynamic_index_in_dim(both, (me + by) % y, 0, False), "y", by))
+        right.append(shifted(o, "y", by))
+    return left, right, [other_core(x) for x in right]
+
+
+def weight_kernel(*refs):
+    count = (len(refs) - 3) // 3
+    left, own, cross = refs[:count], refs[count : 2 * count], refs[2 * count : 3 * count]
+    out, scratch = refs[-2:]
+    total = None
+    for l, a, b in zip(left, own, cross):
+        term = dot(l[:, 0:TOK], a[...]) + dot(l[:, TOK:], b[...])
+        total = term if total is None else total + term
+    each = total.shape[0] // (N // 2)
+    for p in range(N // 2):
+        for t in range(WOUT // each):
+            scratch[p, each * t : each * t + each, :] = total[
+                each * p : each * p + each, 128 * t : 128 * t + 128
+            ]
+        out[p] = scratch[p].astype(BF)
+
+
+def add_weight_part(message, left, own, cross):
+    full = pl.BlockSpec(memory_space=pltpu.VMEM)
+    args = [*left, *own, *cross]
+    return pl.pallas_call(
+        weight_kernel,
+        grid=(1,),
+        in_specs=[pl.BlockSpec(x.shape, lambda i: (0, 0)) for x in args]
+        + [pl.BlockSpec(memory_space=pl.ANY)],
+        out_specs=pl.BlockSpec((N // 2, WOUT, 128), lambda i: (0, 0, 0)),
+        out_shape=jax.ShapeDtypeStruct(message.shape, BF),
+        scratch_shapes=[pltpu.VMEM((N // 2, WOUT, 128), F32)],
+        input_output_aliases={len(args): 0},
+        compiler_params=pltpu.CompilerParams(vmem_limit_bytes=VMEM_LIMIT),
+        name="weight",
+    )(*args, message)
+
+
+def weight_total(parts, rows):
+    part = parts.astype(F32).sum(0).astype(BF)
     if lax.axis_size("xl") > 1:
         part = (part.astype(F32) + shifted(part, "xl", 1).astype(F32)).astype(BF)
-    part = gathered(part, "y").astype(F32)
-    return part.reshape(padded, -1)[:rows]
+    part = gathered(part, "y")
+    y, height, lanes = part.shape
+    part = part.reshape(y, 10, height // 10, lanes).swapaxes(1, 2)
+    return part.reshape(-1, 10 * lanes)[:rows].astype(F32)
 
 
 def shards(
@@ -618,12 +648,18 @@
         text_grad[0],
         text_logsum[0].T,
     )
+    upstream, _ = lax.optimization_barrier((upstream, texts[0]))
+    operands = weight_operands(upstream, outputs)
     text_out, *state = text_pairs(recv, texts)
-    mine = exchange(text_out, CHIPS)
+    operands, text_out = lax.optimization_barrier((operands, text_out))
+    mine = exchange(add_weight_part(text_out, *operands), CHIPS)
+    out = image_pairs(recv, state)
+    mine, out = lax.optimization_barrier((mine, out))
     text_grads = unpack_text(core, mine, other_core(mine))
-    out = image_pairs(recv, state)
-    grads = unpack(exchange(out, SEQ))
-    weight_grad = weight_gradient(upstream, outputs, texts, (out, mine))
+    got = exchange(out, SEQ)
+    got, text_grads = lax.optimization_barrier((got, text_grads))
+    grads = unpack(got)
+    weight_grad = weight_total(mine[:, :WOUT], output_grad.shape[2] // N)
     return (*(g[None] for g in grads), *(g[None] for g in text_grads), weight_grad)
 
 

time: 170 us -> 139 us (0.82)
  waiting for transfers between devices: 63.9 us -> 35.3 us
  Pallas kernels: 46.1 us -> 51.6 us
  local copies, waits for them, and re-layouts: 10.5 us -> 6.06 us
  matrix products: 2.19 us -> 0 us
    ppermute x11 -> x10, waiting for transfers between devices: 44.7 us -> 16.5 us  [shifted(): return lax.ppermute(x, axis, [(i, (i + by) % size) for i in range(size)])]
    ppermute x3 -> x6, starting transfers between devices: 1.85 us -> 9.92 us  [other_core(): return lax.ppermute(x, 'core', [(0, 1), (1, 0)])]
    ppermute x11 -> x10, starting transfers between devices: 18.3 us -> 10.3 us  [shifted(): return lax.ppermute(x, axis, [(i, (i + by) % size) for i in range(size)])]
    pallas_call x0 -> x1, Pallas kernels: none -> 4.68 us  [add_weight_part(): pl.pallas_call(weight_kernel, grid=(1,), in_specs=[pl.BlockSpec(x.shape,...]
    unnamed x18 -> x27, local copies, waits for them, and re-layouts: 6.94 us -> 4.64 us
    convert_element_type x3 -> x1, other arithmetic: 3.2 us -> 0.93 us  [weight_total(): return part.reshape(-1, 10 * lanes)[:rows].astype(F32)]
    dot_general x1 -> x0, matrix products: 2.19 us -> none  [weight_gradient(): jnp.dot(left.reshape(-1, 2 * tokens), right, preferred_element_type=F32)]
    squeeze x0 -> x1, other arithmetic: none -> 1.8 us  [weight_operands(): lax.dynamic_index_in_dim(both, (me + by) % y, 0, False)]
  transfers between devices with their start and end apart: 17 -> 19, of which waited for: 7 -> 7; matrix products, arithmetic and copies ran while one was open for 4% -> 4% of each run, Pallas kernels for 20% -> 26%
where the time goes in v3:
time: 139 us
  Pallas kernels  51.6 us (37%)
  starting transfers between devices  41.9 us (30%)
  waiting for transfers between devices  35.3 us (25%)
  local copies, waits for them, and re-layouts  6.06 us (4%)
  other arithmetic  2.9 us (2%)
    all_to_all x3, starting transfers between devices, exchange(): return lax.all_to_all(x, axes, 0, 0, tiled=True)  21.7 us
    all_to_all x3, waiting for transfers between devices, exchange(): return lax.all_to_all(x, axes, 0, 0, tiled=True)  18.8 us
    pallas_call x1, Pallas kernels, image_pairs(): pl.pallas_call(image_pairs_kernel, in_specs=[full] * 5, out_specs=full, o...  18.6 us
    ppermute x10, waiting for transfers between devices, shifted(): return lax.ppermute(x, axis, [(i, (i + by) % size) for i in range(size)])  16.5 us
    pallas_call x1, Pallas kernels, text_pairs(): pl.pallas_call(text_pairs_kernel, in_specs=[full] * 7, out_specs=[full] *...  10.3 us
    ppermute x10, starting transfers between devices, shifted(): return lax.ppermute(x, axis, [(i, (i + by) % size) for i in range(size)])  10.3 us
    ppermute x6, starting transfers between devices, other_core(): return lax.ppermute(x, 'core', [(0, 1), (1, 0)])  9.92 us
    pallas_call x1, Pallas kernels, pack(): pl.pallas_call(pack_kernel, grid_spec=pltpu.PrefetchScalarGridSpec(num_sc...  7.74 us
  transfers between devices with their start and end apart: 19, of which 7 were waited for; matrix products, arithmetic and copies ran while one was open for 4% of the time, Pallas kernels for 26%

profile of v3, /device:TPU:1, one launch (start us, length us, event | category | flops | bytes accessed | tf_op | source)
XLA Modules:
  0.0 138.6 jit_solution(3826040152615648201)
XLA Ops:
  0.6 1.3 copy.35
  1.9 7.7 %pack.1 = bf16[16,400,128]{2,1,0:T(8,128)(2,1)} custom-call(s32[1]{0:T(128)} %bitcast.index, bf16[128,2432]{1,0:T(8,128)(2,1)} %bitcast.76, bf16[2432,1280]{1,0:T(8,128)(2,1)} %w.1, bf16[128,1280]{1,0:T(8,128)(2,1)} %bitcast.86, bf16[128,1280]{1,0:T(8,128)(2,1)} %bitcast.87, bf16[128,1280]{1,0:T(8,128)(2,1)} %bitcast.88, bf16[128,1280]{1,0:T(8,128)(2,1)} %bitcast.80, ...), custom_call_target="tpu_custom_call" | custom-call | tf_op jit(solution)/shard_map/pack/pallas_call | solution.py:129
  9.7 9.4 %all-to-all-start = ((bf16[16,400,128]{2,1,0:T(8,128)(2,1)}), bf16[16,400,128]{2,1,0:T(8,128)(2,1)S(1)}, u32[]{:S(2)}, u32[]{:S(2)}) async-start(bf16[16,400,128]{2,1,0:T(8,128)(2,1)} %pack.1), calls=%async_computation | async-start | bytes 3276800 | tf_op jit(solution)/shard_map/all_to_all | solution.py:527
  19.1 0.6 copy.34
  19.7 2.4 %text_prep.1 = (bf16[384,128]{1,0:T(8,128)(2,1)}, bf16[384,128]{1,0:T(8,128)(2,1)}, bf16[16,384]{1,0:T(8,128)(2,1)}, bf16[256,128]{1,0:T(8,128)(2,1)}, bf16[256,...) custom-call(s32[1]{0:T(128)} %bitcast.index, bf16[333,1280]{1,0:T(8,128)(2,1)} %bitcast.62, bf16[333,1280]{1,0:T(8,128)(2,1)} %bitcast.64, ...), custom_call_target="tpu_custom_call" | custom-call | tf_op jit(solution)/shard_map/text_prep/pallas_call | solution.py:209
  22.2 0.3 copy.24
  22.5 0.1 pad.4
  22.5 0.1 copy.25
  22.6 0.8 dynamic-slice_bitcast_fusion
  23.4 0.1 collective-permute-start
  23.5 2.7 %collective-permute-start.6 = (bf16[128,1280]{1,0:T(8,128)(2,1)S(1)}, bf16[128,1280]{1,0:T(8,128)(2,1)S(1)}, u32[]{:S(2)}, u32[]{:S(2)}) collective-permute-start(bf16[128,1280]{1,0:T(8,128)(2,1)S(1)} %bitcast.82), channel_id=1, source_target_pairs={{0,96},{32,0},{64,32},{96,64},{1,97},{33,1},{65,33},{97,65},{2,98}... | collective-permute-start | bytes 983048 | tf_op jit(solution)/shard_map/ppermute | solution.py:536
  26.2 1.6 %collective-permute-start.5 = (bf16[128,1280]{1,0:T(8,128)(2,1)S(1)}, bf16[128,1280]{1,0:T(8,128)(2,1)S(1)}, u32[]{:S(2)}, u32[]{:S(2)}) collective-permute-start(bf16[128,1280]{1,0:T(8,128)(2,1)S(1)} %bitcast.84), channel_id=1, source_target_pairs={{0,64},{32,96},{64,0},{96,32},{1,65},{33,97},{65,1},{97,33},{2,66}... | collective-permute-start | bytes 983048 | tf_op jit(solution)/shard_map/ppermute | solution.py:536
  27.9 1.2 collective-permute-start.7
  29.1 1.8 %fusion.1 = (bf16[320,256]{1,0:T(8,128)(2,1)S(1)}, bf16[320,256]{1,0:T(8,128)(2,1)}, bf16[320,256]{1,0:T(8,128)(2,1)S(1)}, bf16[320,256]{1,0:T(8,128)(2,1)}) fusion(s32[]{:T(128)S(6)} %select_n.72, bf16[4,320,128]{2,1,0:T(8,128)(2,1)S(1)} %get-tuple-element.94, bf16[4,320,128]{2,1,0:T(8,128)(2,1)} %collective-permute-done, s32[]{:T(128)S(6)} %select_n.66, ...), kind=kLoop, calls=%fused_computation.15 | loop fusion | flops 1310720 | bytes 1310736 | tf_op jit(solution)/shard_map/jit(dynamic_index_in_dim)/squeeze | solution.py:564
  30.9 1.6 %collective-permute-start.1 = (bf16[320,256]{1,0:T(8,128)(2,1)S(1)}, bf16[320,256]{1,0:T(8,128)(2,1)S(1)}, u32[]{:S(2)}, u32[]{:S(2)}) collective-permute-start(bf16[320,256]{1,0:T(8,128)(2,1)S(1)} %get-tuple-element.91), channel_id=1, source_target_pairs={{0,32},{32,64},{64,96},{96,0},{1,33},{33,65},{65,97},{97,1},{2,34}... | collective-permute-start | bytes 491528 | tf_op jit(solution)/shard_map/ppermute | solution.py:536
  32.5 7.3 %collective-permute-done.6.refs_7_ = bf16[128,1280]{1,0:T(8,128)(2,1)S(1)} collective-permute-done((bf16[128,1280]{1,0:T(8,128)(2,1)S(1)}, bf16[128,1280]{1,0:T(8,128)(2,1)S(1)}, u32[]{:S(2)}, u32[]{:S(2)}) %collective-permute-start.6) | collective-permute-done | bytes 327712 | tf_op jit(solution)/shard_map/ppermute | solution.py:536
  39.8 1.4 collective-permute-start.10
  41.2 4.6 %collective-permute-start.8 = (bf16[128,1280]{1,0:T(8,128)(2,1)S(1)}, bf16[128,1280]{1,0:T(8,128)(2,1)}, u32[]{:S(2)}, u32[]{:S(2)}) collective-permute-start(bf16[128,1280]{1,0:T(8,128)(2,1)S(1)} %collective-permute-done.4.refs_5_), channel_id=1, source_target_pairs={{0,1},{1,0},{2,3},{3,2},{4,5},{5,4},{6,7},{7,6},{8,9},{9,8},{10,11... | collective-permute-start | bytes 983048 | tf_op jit(solution)/shard_map/ppermute | solution.py:531
  45.8 0.1 collective-permute-start.9
  45.9 0.7 collective-permute-done.1.refs_1_
  46.5 0.7 copy-done.8
  47.2 1.2 copy-done
  48.4 10.3 %text_pairs.1 = (bf16[8,1248,128]{2,1,0:T(8,128)(2,1)}, f32[2048,128]{1,0:T(8,128)}, f32[64,2048]{1,0:T(8,128)}, f32[1024,128]{1,0:T(8,128)}, f32[64,1024]{1,0:T(8,128)}) custom-call(bf16[16,400,128]{2,1,0:T(8,128)(2,1)} %copy-done, bf16[384,128]{1,0:T(8,128)(2,1)} %get-tuple-element.48.wqg, bf16[384,128]{1,0:T(8,128)(2,1)} %get-tuple-element.52.wkv, ...), custom_call_target="tpu_custom_call" | custom-call | tf_op jit(solution)/shard_map/text_pairs/pallas_call | solution.py:368
  58.8 0.6 copy-done.9
  59.4 0.0 copy-done.10
  59.4 0.1 copy-done.7
  59.5 4.7 %weight.1 = bf16[8,1248,128]{2,1,0:T(8,128)(2,1)} custom-call(bf16[320,256]{1,0:T(8,128)(2,1)} %get-tuple-element.58.refs_0_, bf16[320,256]{1,0:T(8,128)(2,1)} %copy-done.8, bf16[320,256]{1,0:T(8,128)(2,1)} %copy-done.9, bf16[320,256]{1,0:T(8,128)(2,1)} %copy-done.10, bf16[128,1280]{1,0:T(8,128)(2,1)} %bitcast.81, ...), custom_call_target="tpu_custom_call", output_to_operand_aliasing={{}: (12, {})} | custom-call | tf_op jit(solution)/shard_map/weight/pallas_call | solution.py:589
  64.2 7.1 %all-to-all-start.1 = ((bf16[8,1248,128]{2,1,0:T(8,128)(2,1)}), bf16[8,1248,128]{2,1,0:T(8,128)(2,1)S(1)}, u32[]{:S(2)}, u32[]{:S(2)}) async-start(bf16[8,1248,128]{2,1,0:T(8,128)(2,1)} %weight.1), calls=%async_computation.1 | async-start | bytes 5111808 | tf_op jit(solution)/shard_map/all_to_all | solution.py:527
  71.3 18.6 %image_pairs.1 = bf16[16,288,128]{2,1,0:T(8,128)(2,1)} custom-call(bf16[16,400,128]{2,1,0:T(8,128)(2,1)} %copy-done, f32[2048,128]{1,0:T(8,128)} %get-tuple-element.71.a, f32[64,2048]{1,0:T(8,128)} %get-tuple-element.72.b, f32[1024,128]{1,0:T(8,128)} %get-tuple-element.73.c, f32[64,1024]{1,0:T(8,128)} %get-tuple-element.74.d), custom_call_target="tpu_custom_call" | custom-call | tf_op jit(solution)/shard_map/image_pairs/pallas_call | solution.py:408
  89.9 13.2 %all-to-all-done.1.mine = bf16[8,1248,128]{2,1,0:T(8,128)(2,1)S(1)} async-done(((bf16[8,1248,128]{2,1,0:T(8,128)(2,1)}), bf16[8,1248,128]{2,1,0:T(8,128)(2,1)S(1)}, u32[]{:S(2)}, u32[]{:S(2)}) %all-to-all-start.1) | async-done | bytes 2555936 | tf_op jit(solution)/shard_map/all_to_all | solution.py:527
  103.1 2.5 %collective-permute-start.11 = (bf16[8,1248,128]{2,1,0:T(8,128)(2,1)S(1)}, bf16[8,1248,128]{2,1,0:T(8,128)(2,1)}, u32[]{:S(2)}, u32[]{:S(2)}) collective-permute-start(bf16[8,1248,128]{2,1,0:T(8,128)(2,1)S(1)} %all-to-all-done.1.mine), channel_id=1, source_target_pairs={{0,1},{1,0},{2,3},{3,2},{4,5},{5,4},{6,7},{7,6},{8,9},{9,8},{10,11... | collective-permute-start | bytes 7667720 | tf_op jit(solution)/shard_map/ppermute | solution.py:531
  105.7 0.1 slice_reduce_fusion
  105.8 0.4 collective-permute-start.12
  106.2 4.2 %collective-permute-done.12 = bf16[400,128]{1,0:T(8,128)(2,1)S(1)} collective-permute-done((bf16[400,128]{1,0:T(8,128)(2,1)S(1)}, bf16[400,128]{1,0:T(8,128)(2,1)S(1)}, u32[]{:S(2)}, u32[]{:S(2)}) %collective-permute-start.12) | collective-permute-done | bytes 102432 | tf_op jit(solution)/shard_map/ppermute | solution.py:536
  110.4 0.1 broadcast_in_dim.40
  110.4 0.1 bitcast_dynamic-update-slice_fusion.3
  110.5 1.5 %collective-permute-start.13 = (bf16[400,128]{1,0:T(8,128)(2,1)S(1)}, bf16[400,128]{1,0:T(8,128)(2,1)S(1)}, u32[]{:S(2)}, u32[]{:S(2)}) collective-permute-start(bf16[400,128]{1,0:T(8,128)(2,1)S(1)} %get-tuple-element.88), channel_id=1, source_target_pairs={{0,32},{32,64},{64,96},{96,0},{1,33},{33,65},{65,97},{97,1},{2,34}... | collective-permute-start | bytes 307208 | tf_op jit(solution)/shard_map/ppermute | solution.py:536
  112.0 5.2 %all-to-all-start.2 = ((bf16[16,288,128]{2,1,0:T(8,128)(2,1)}), bf16[16,288,128]{2,1,0:T(8,128)(2,1)}, u32[]{:S(2)}, u32[]{:S(2)}) async-start(bf16[16,288,128]{2,1,0:T(8,128)(2,1)} %image_pairs.1), calls=%async_computation.2 | async-start | bytes 2359296 | tf_op jit(solution)/shard_map/all_to_all | solution.py:527
  117.2 1.7 %collective-permute-start.14 = (bf16[400,128]{1,0:T(8,128)(2,1)S(1)}, bf16[400,128]{1,0:T(8,128)(2,1)S(1)}, u32[]{:S(2)}, u32[]{:S(2)}) collective-permute-start(bf16[400,128]{1,0:T(8,128)(2,1)S(1)} %get-tuple-element.88), channel_id=1, source_target_pairs={{0,64},{32,96},{64,0},{96,32},{1,65},{33,97},{65,1},{97,33},{2,66}... | collective-permute-start | bytes 307208 | tf_op jit(solution)/shard_map/ppermute | solution.py:536
  118.9 0.6 collective-permute-start.15
  119.6 3.2 %collective-permute-done.14 = bf16[400,128]{1,0:T(8,128)(2,1)S(1)} collective-permute-done((bf16[400,128]{1,0:T(8,128)(2,1)S(1)}, bf16[400,128]{1,0:T(8,128)(2,1)S(1)}, u32[]{:S(2)}, u32[]{:S(2)}) %collective-permute-start.14) | collective-permute-done | bytes 102432 | tf_op jit(solution)/shard_map/ppermute | solution.py:536
  122.8 1.1 collective-permute-done.15
  123.9 0.1 copy.26
  124.1 0.1 copy.33
  124.2 0.9 slice_convert_fusion
  125.1 5.3 %unpack_text.1 = (bf16[333,1280]{1,0:T(8,128)(2,1)}, bf16[333,1280]{1,0:T(8,128)(2,1)}, bf16[333,1280]{1,0:T(8,128)(2,1)}) custom-call(s32[1]{0:T(128)} %bitcast.24.core, bf16[8,1248,128]{2,1,0:T(8,128)(2,1)} %copy-done.1, bf16[8,1248,128]{2,1,0:T(8,128)(2,1)} %collective-permute-done.11.other), custom_call_target="tpu_custom_call" | custom-call | tf_op jit(solution)/shard_map/unpack_text/pallas_call | solution.py:516
  130.5 5.6 %all-to-all-done.2.recv = bf16[16,288,128]{2,1,0:T(8,128)(2,1)} async-done(((bf16[16,288,128]{2,1,0:T(8,128)(2,1)}), bf16[16,288,128]{2,1,0:T(8,128)(2,1)}, u32[]{:S(2)}, u32[]{:S(2)}) %all-to-all-start.2) | async-done | bytes 1179680 | tf_op jit(solution)/shard_map/all_to_all | solution.py:527
  136.0 2.6 %unpack.1 = (bf16[128,1280]{1,0:T(8,128)(2,1)}, bf16[128,1280]{1,0:T(8,128)(2,1)}, bf16[128,1280]{1,0:T(8,128)(2,1)}) custom-call(bf16[16,288,128]{2,1,0:T(8,128)(2,1)} %all-to-all-done.2.recv), custom_call_target="tpu_custom_call" | custom-call | tf_op jit(solution)/shard_map/unpack/pallas_call | solution.py:464
  (37 shorter events, 0.1 us)
Async XLA Ops:
  9.7 9.4 %copy-start.11 = (f32[1,333,20]{1,0,2:T(1,128)S(1)}, f32[1,333,20]{1,0,2:T(1,128)}, u32[]{:S(2)}) copy-start(f32[1,333,20]{1,0,2:T(1,128)} %param.24) | copy-start | bytes 79924
  9.7 37.5 %all-to-all-start = ((bf16[16,400,128]{2,1,0:T(8,128)(2,1)}), bf16[16,400,128]{2,1,0:T(8,128)(2,1)S(1)}, u32[]{:S(2)}, u32[]{:S(2)}) async-start(bf16[16,400,128]{2,1,0:T(8,128)(2,1)} %pack.1), calls=%async_computation | async-start | bytes 3276800 | tf_op jit(solution)/shard_map/all_to_all | solution.py:527
  19.7 2.4 %copy-start.2 = (bf16[1,128,2432]{2,1,0:T(8,128)(2,1)S(1)}, bf16[1,128,2432]{2,1,0:T(8,128)(2,1)}, u32[]{:S(2)}) copy-start(bf16[1,128,2432]{2,1,0:T(8,128)(2,1)} %param.17) | copy-start | bytes 1867780
  22.1 1.4 copy-start.3
  23.4 5.7 %collective-permute-start = (bf16[4,320,128]{2,1,0:T(8,128)(2,1)}, bf16[4,320,128]{2,1,0:T(8,128)(2,1)}, u32[]{:S(2)}, u32[]{:S(2)}) collective-permute-start(bf16[4,320,128]{2,1,0:T(8,128)(2,1)} %get-tuple-element.93), channel_id=1, source_target_pairs={{0,1},{1,0},{2,3},{3,2},{4,5},{5,4},{6,7},{7,6},{8,9},{9,8},{10,11... | collective-permute-start | bytes 983048 | tf_op jit(solution)/shard_map/ppermute | solution.py:531
  23.5 16.3 %collective-permute-start.6 = (bf16[128,1280]{1,0:T(8,128)(2,1)S(1)}, bf16[128,1280]{1,0:T(8,128)(2,1)S(1)}, u32[]{:S(2)}, u32[]{:S(2)}) collective-permute-start(bf16[128,1280]{1,0:T(8,128)(2,1)S(1)} %bitcast.82), channel_id=1, source_target_pairs={{0,96},{32,0},{64,32},{96,64},{1,97},{33,1},{65,33},{97,65},{2,98}... | collective-permute-start | bytes 983048 | tf_op jit(solution)/shard_map/ppermute | solution.py:536
  26.2 15.0 %collective-permute-start.4 = (bf16[128,1280]{1,0:T(8,128)(2,1)S(1)}, bf16[128,1280]{1,0:T(8,128)(2,1)S(1)}, u32[]{:S(2)}, u32[]{:S(2)}) collective-permute-start(bf16[128,1280]{1,0:T(8,128)(2,1)S(1)} %bitcast.83), channel_id=1, source_target_pairs={{0,32},{32,64},{64,96},{96,0},{1,33},{33,65},{65,97},{97,1},{2,34}... | collective-permute-start | bytes 983048 | tf_op jit(solution)/shard_map/ppermute | solution.py:536
  26.2 19.5 %collective-permute-start.5 = (bf16[128,1280]{1,0:T(8,128)(2,1)S(1)}, bf16[128,1280]{1,0:T(8,128)(2,1)S(1)}, u32[]{:S(2)}, u32[]{:S(2)}) collective-permute-start(bf16[128,1280]{1,0:T(8,128)(2,1)S(1)} %bitcast.84), channel_id=1, source_target_pairs={{0,64},{32,96},{64,0},{96,32},{1,65},{33,97},{65,1},{97,33},{2,66}... | collective-permute-start | bytes 983048 | tf_op jit(solution)/shard_map/ppermute | solution.py:536
  27.9 18.0 %collective-permute-start.7 = (bf16[128,1280]{1,0:T(8,128)(2,1)S(1)}, bf16[128,1280]{1,0:T(8,128)(2,1)}, u32[]{:S(2)}, u32[]{:S(2)}) collective-permute-start(bf16[128,1280]{1,0:T(8,128)(2,1)S(1)} %bitcast.85), channel_id=1, source_target_pairs={{0,1},{1,0},{2,3},{3,2},{4,5},{5,4},{6,7},{7,6},{8,9},{9,8},{10,11... | collective-permute-start | bytes 983048 | tf_op jit(solution)/shard_map/ppermute | solution.py:531
  30.9 15.6 %collective-permute-start.1 = (bf16[320,256]{1,0:T(8,128)(2,1)S(1)}, bf16[320,256]{1,0:T(8,128)(2,1)S(1)}, u32[]{:S(2)}, u32[]{:S(2)}) collective-permute-start(bf16[320,256]{1,0:T(8,128)(2,1)S(1)} %get-tuple-element.91), channel_id=1, source_target_pairs={{0,32},{32,64},{64,96},{96,0},{1,33},{33,65},{65,97},{97,1},{2,34}... | collective-permute-start | bytes 491528 | tf_op jit(solution)/shard_map/ppermute | solution.py:536
  39.8 19.0 %copy-start.4 = (bf16[128,1280]{1,0:T(8,128)(2,1)}, bf16[128,1280]{1,0:T(8,128)(2,1)S(1)}, u32[]{:S(2)}) copy-start(bf16[128,1280]{1,0:T(8,128)(2,1)S(1)} %collective-permute-done.6.refs_7_) | copy-start | bytes 983044
  39.8 18.9 %collective-permute-start.10 = (bf16[128,1280]{1,0:T(8,128)(2,1)S(1)}, bf16[128,1280]{1,0:T(8,128)(2,1)S(1)}, u32[]{:S(2)}, u32[]{:S(2)}) collective-permute-start(bf16[128,1280]{1,0:T(8,128)(2,1)S(1)} %collective-permute-done.6.refs_7_), channel_id=1, source_target_pairs={{0,1},{1,0},{2,3},{3,2},{4,5},{5,4},{6,7},{7,6},{8,9},{9,8},{10,11... | collective-permute-start | bytes 983048 | tf_op jit(solution)/shard_map/ppermute | solution.py:531
  41.2 17.6 %copy-start.5 = (bf16[128,1280]{1,0:T(8,128)(2,1)}, bf16[128,1280]{1,0:T(8,128)(2,1)S(1)}, u32[]{:S(2)}) copy-start(bf16[128,1280]{1,0:T(8,128)(2,1)S(1)} %collective-permute-done.4.refs_5_) | copy-start | bytes 983044
  41.2 17.5 %collective-permute-start.8 = (bf16[128,1280]{1,0:T(8,128)(2,1)S(1)}, bf16[128,1280]{1,0:T(8,128)(2,1)}, u32[]{:S(2)}, u32[]{:S(2)}) collective-permute-start(bf16[128,1280]{1,0:T(8,128)(2,1)S(1)} %collective-permute-done.4.refs_5_), channel_id=1, source_target_pairs={{0,1},{1,0},{2,3},{3,2},{4,5},{5,4},{6,7},{7,6},{8,9},{9,8},{10,11... | collective-permute-start | bytes 983048 | tf_op jit(solution)/shard_map/ppermute | solution.py:531
  45.8 13.0 %copy-start.6 = (bf16[128,1280]{1,0:T(8,128)(2,1)}, bf16[128,1280]{1,0:T(8,128)(2,1)S(1)}, u32[]{:S(2)}) copy-start(bf16[128,1280]{1,0:T(8,128)(2,1)S(1)} %collective-permute-done.5.refs_6_) | copy-start | bytes 983044
  45.8 13.0 %collective-permute-start.9 = (bf16[128,1280]{1,0:T(8,128)(2,1)S(1)}, bf16[128,1280]{1,0:T(8,128)(2,1)}, u32[]{:S(2)}, u32[]{:S(2)}) collective-permute-start(bf16[128,1280]{1,0:T(8,128)(2,1)S(1)} %collective-permute-done.5.refs_6_), channel_id=1, source_target_pairs={{0,1},{1,0},{2,3},{3,2},{4,5},{5,4},{6,7},{7,6},{8,9},{9,8},{10,11... | collective-permute-start | bytes 983048 | tf_op jit(solution)/shard_map/ppermute | solution.py:531
  45.9 12.8 %collective-permute-start.2 = (bf16[320,256]{1,0:T(8,128)(2,1)}, bf16[320,256]{1,0:T(8,128)(2,1)S(1)}, u32[]{:S(2)}, u32[]{:S(2)}) collective-permute-start(bf16[320,256]{1,0:T(8,128)(2,1)} %get-tuple-element.92), channel_id=1, source_target_pairs={{0,64},{32,96},{64,0},{96,32},{1,65},{33,97},{65,1},{97,33},{2,66}... | collective-permute-start | bytes 491528 | tf_op jit(solution)/shard_map/ppermute | solution.py:536
  46.5 0.7 copy-start.8
  47.2 11.5 %collective-permute-start.3 = (bf16[320,256]{1,0:T(8,128)(2,1)S(1)}, bf16[320,256]{1,0:T(8,128)(2,1)S(1)}, u32[]{:S(2)}, u32[]{:S(2)}) collective-permute-start(bf16[320,256]{1,0:T(8,128)(2,1)S(1)} %get-tuple-element.89), channel_id=1, source_target_pairs={{0,96},{32,0},{64,32},{96,64},{1,97},{33,1},{65,33},{97,65},{2,98}... | collective-permute-start | bytes 491528 | tf_op jit(solution)/shard_map/ppermute | solution.py:536
  47.2 1.2 copy-start
  58.7 0.7 copy-start.9
  58.7 0.7 copy-start.10
  58.7 0.8 copy-start.7
  64.2 38.9 %all-to-all-start.1 = ((bf16[8,1248,128]{2,1,0:T(8,128)(2,1)}), bf16[8,1248,128]{2,1,0:T(8,128)(2,1)S(1)}, u32[]{:S(2)}, u32[]{:S(2)}) async-start(bf16[8,1248,128]{2,1,0:T(8,128)(2,1)} %weight.1), calls=%async_computation.1 | async-start | bytes 5111808 | tf_op jit(solution)/shard_map/all_to_all | solution.py:527
  103.1 20.9 %copy-start.1 = (bf16[8,1248,128]{2,1,0:T(8,128)(2,1)}, bf16[8,1248,128]{2,1,0:T(8,128)(2,1)S(1)}, u32[]{:S(2)}) copy-start(bf16[8,1248,128]{2,1,0:T(8,128)(2,1)S(1)} %all-to-all-done.1.mine) | copy-start | bytes 7667716
  103.1 22.0 %collective-permute-start.11 = (bf16[8,1248,128]{2,1,0:T(8,128)(2,1)S(1)}, bf16[8,1248,128]{2,1,0:T(8,128)(2,1)}, u32[]{:S(2)}, u32[]{:S(2)}) collective-permute-start(bf16[8,1248,128]{2,1,0:T(8,128)(2,1)S(1)} %all-to-all-done.1.mine), channel_id=1, source_target_pairs={{0,1},{1,0},{2,3},{3,2},{4,5},{5,4},{6,7},{7,6},{8,9},{9,8},{10,11... | collective-permute-start | bytes 7667720 | tf_op jit(solution)/shard_map/ppermute | solution.py:531
  105.8 4.6 %collective-permute-start.12 = (bf16[400,128]{1,0:T(8,128)(2,1)S(1)}, bf16[400,128]{1,0:T(8,128)(2,1)S(1)}, u32[]{:S(2)}, u32[]{:S(2)}) collective-permute-start(bf16[400,128]{1,0:T(8,128)(2,1)S(1)} %slice_reduce_fusion), channel_id=1, source_target_pairs={{0,16},{16,0},{1,17},{17,1},{2,18},{18,2},{3,19},{19,3},{4,20},{20... | collective-permute-start | bytes 307208 | tf_op jit(solution)/shard_map/ppermute | solution.py:536
  110.5 9.1 %collective-permute-start.13 = (bf16[400,128]{1,0:T(8,128)(2,1)S(1)}, bf16[400,128]{1,0:T(8,128)(2,1)S(1)}, u32[]{:S(2)}, u32[]{:S(2)}) collective-permute-start(bf16[400,128]{1,0:T(8,128)(2,1)S(1)} %get-tuple-element.88), channel_id=1, source_target_pairs={{0,32},{32,64},{64,96},{96,0},{1,33},{33,65},{65,97},{97,1},{2,34}... | collective-permute-start | bytes 307208 | tf_op jit(solution)/shard_map/ppermute | solution.py:536
  112.0 24.0 %all-to-all-start.2 = ((bf16[16,288,128]{2,1,0:T(8,128)(2,1)}), bf16[16,288,128]{2,1,0:T(8,128)(2,1)}, u32[]{:S(2)}, u32[]{:S(2)}) async-start(bf16[16,288,128]{2,1,0:T(8,128)(2,1)} %image_pairs.1), calls=%async_computation.2 | async-start | bytes 2359296 | tf_op jit(solution)/shard_map/all_to_all | solution.py:527
  117.2 5.6 %collective-permute-start.14 = (bf16[400,128]{1,0:T(8,128)(2,1)S(1)}, bf16[400,128]{1,0:T(8,128)(2,1)S(1)}, u32[]{:S(2)}, u32[]{:S(2)}) collective-permute-start(bf16[400,128]{1,0:T(8,128)(2,1)S(1)} %get-tuple-element.88), channel_id=1, source_target_pairs={{0,64},{32,96},{64,0},{96,32},{1,65},{33,97},{65,1},{97,33},{2,66}... | collective-permute-start | bytes 307208 | tf_op jit(solution)/shard_map/ppermute | solution.py:536
  118.9 5.0 %collective-permute-start.15 = (bf16[400,128]{1,0:T(8,128)(2,1)S(1)}, bf16[400,128]{1,0:T(8,128)(2,1)S(1)}, u32[]{:S(2)}, u32[]{:S(2)}) collective-permute-start(bf16[400,128]{1,0:T(8,128)(2,1)S(1)} %get-tuple-element.88), channel_id=1, source_target_pairs={{0,96},{32,0},{64,32},{96,64},{1,97},{33,1},{65,33},{97,65},{2,98}... | collective-permute-start | bytes 307208 | tf_op jit(solution)/shard_map/ppermute | solution.py:536

commit v4 on v3

--- a/solution.py
+++ b/solution.py
@@ -27,7 +27,9 @@
 SCALE = 0.125
 MSG = 400
 OUT = 288
-TOUT = TXT_K + HALF + TXT_K
+W_FOLD = 176
+L_FOLD = 96
+TOUT = TXT_K + HALF + W_FOLD + L_FOLD
 WOUT = 400
 VMEM_LIMIT = 56 * 2**20
 
@@ -353,11 +355,15 @@
     for m in range(TXT_Q // 128):
         rows = min(128, TXT_K - 128 * m)
         put(128 * m, w.dkv[S + 128 * m : S + 128 * m + rows, :] * factor[:rows])
-        lower = h.dqt[:, SH + 128 * m : SH + 128 * m + 128] if m < 2 else jnp.zeros((64, 128), F32)
-        both = jnp.concatenate([w.dqt[:, S + 128 * m : S + 128 * m + 128], lower], 0)
-        put(TXT_K + HALF + 128 * m, (both * SCALE).T[:rows])
     put(TXT_K, h.dkv[SH : SH + 128, :] * factor)
     put(TXT_K + 128, h.dkv[SH + 128 : SH + HALF, :] * factor[: HALF - 128])
+    for dqt, at, fold in (
+        (w.dqt[:, S:], TXT_K + HALF, W_FOLD),
+        (h.dqt[:, SH:], TXT_K + HALF + W_FOLD, L_FOLD),
+    ):
+        part = dqt * SCALE
+        both = jnp.concatenate([part, pltpu.roll(part, part.shape[1] - fold, 1)], 0)
+        put(at, both[:, 0:256].T[:fold])
 
 
 STATE = [(S, 128), (64, S), (SH, 128), (64, SH)]
@@ -480,35 +486,37 @@
         return jnp.where(odd_core, b, a) if d % 2 == 0 else jnp.where(odd_core, a, b)
 
     at = TXT_K + HALF
+    whole_q = slice(at, at + W_FOLD)
     for t in range(N // 2):
         lanes = slice(128 * t, 128 * t + 128)
         keys, values = lane_pair(part(2 * t, slice(0, TXT_K)), part(2 * t + 1, slice(0, TXT_K)))
         dk[:, lanes] = keys[:TXT].astype(BF)
         dv[:, lanes] = values[:TXT].astype(BF)
-        queries, _ = lane_pair(part(2 * t, slice(at, TOUT)), part(2 * t + 1, slice(at, TOUT)))
-        dq[:, lanes] = queries[:TXT].astype(BF)
+        first, second = lane_pair(part(2 * t, whole_q), part(2 * t + 1, whole_q))
+        dq[0:W_FOLD, lanes] = first.astype(BF)
+        dq[W_FOLD:TXT, lanes] = second[: TXT - W_FOLD].astype(BF)
     shared = slice(TXT_K, TXT_K + HALF)
-    shared_q = slice(at, at + HALF)
+    shared_q = slice(at + W_FOLD, at + W_FOLD + L_FOLD)
     for t in range(2):
         lanes = slice(1024 + 128 * t, 1024 + 128 * t + 128)
         for half in range(2):
-            size = min(HALF, TXT - HALF * half)
-            rows = slice(HALF * half, HALF * half + size)
+            begin, end = HALF * half, min(HALF * half + HALF, TXT)
             keys, values = lane_pair(
                 *(
                     part(4 * r + half, shared) + part(4 * r + 2 + half, shared)
                     for r in (2 * t, 2 * t + 1)
                 )
             )
-            dk[rows, lanes] = keys[:size].astype(BF)
-            dv[rows, lanes] = values[:size].astype(BF)
-            _, queries = lane_pair(
+            dk[begin:end, lanes] = keys[: end - begin].astype(BF)
+            dv[begin:end, lanes] = values[: end - begin].astype(BF)
+            first, second = lane_pair(
                 *(
                     part(4 * r + 2 * half, shared_q) + part(4 * r + 2 * half + 1, shared_q)
                     for r in (2 * t, 2 * t + 1)
                 )
             )
-            dq[rows, lanes] = queries[:size].astype(BF)
+            dq[begin : begin + L_FOLD, lanes] = first.astype(BF)
+            dq[begin + L_FOLD : end, lanes] = second[: end - begin - L_FOLD].astype(BF)
 
 
 def unpack_text(core, mine, other):
@@ -546,48 +554,46 @@
 
 
 def weight_operands(og, o):
-    z, xh, y = (lax.axis_size(a) for a in ("z", "xh", "y"))
+    chips, y = lax.axis_size(CHIPS), lax.axis_size("y")
     core, me = lax.axis_index("core"), lax.axis_index("y")
     tokens = og.shape[0]
-    rows = og.shape[1] // (2 * z * xh)
+    rows = og.shape[1] // (2 * chips)
     padded = -(-rows // (8 * y)) * 8 * y
-    blocks = og.T.reshape(z * xh, 2, rows, tokens)
+    blocks = og.T.reshape(chips, 2, rows, tokens)
     blocks = jnp.pad(blocks, ((0, 0),) * 2 + ((0, padded - rows), (0, 0)))
-    blocks = blocks.reshape(z * xh, 2, y, padded // y, tokens).transpose(1, 2, 0, 3, 4)
+    blocks = blocks.reshape(chips, 2, y, padded // y, tokens).transpose(1, 2, 0, 3, 4)
     blocks = blocks.reshape(2, y, -1, tokens)
     mine = lax.dynamic_index_in_dim(blocks, core, 0, False)
     theirs = other_core(lax.dynamic_index_in_dim(blocks, 1 - core, 0, False))
-    both = jnp.concatenate([mine, theirs], 2)
-    left = [lax.dynamic_index_in_dim(both, me, 0, False)]
-    right = [o]
-    for by in range(1, y):
-        left.append(shifted(lax.dynamic_index_in_dim(both, (me + by) % y, 0, False), "y", by))
-        right.append(shifted(o, "y", by))
-    return left, right, [other_core(x) for x in right]
+    tiles = o.reshape(tokens, -1, 128).swapaxes(0, 1).reshape(-1, 128)
+    everyone = jnp.broadcast_to(tiles[None], (y, *tiles.shape))
+    both = jnp.concatenate([mine, theirs, everyone], 1)
+    pieces = [lax.dynamic_index_in_dim(both, (me + by) % y, 0, False) for by in range(y)]
+    return pieces[:1] + [shifted(p, "y", by) for by, p in enumerate(pieces) if by]
 
 
 def weight_kernel(*refs):
-    count = (len(refs) - 3) // 3
-    left, own, cross = refs[:count], refs[count : 2 * count], refs[2 * count : 3 * count]
-    out, scratch = refs[-2:]
-    total = None
-    for l, a, b in zip(left, own, cross):
-        term = dot(l[:, 0:TOK], a[...]) + dot(l[:, TOK:], b[...])
-        total = term if total is None else total + term
-    each = total.shape[0] // (N // 2)
+    *operands, out, scratch = refs
+    count = len(operands) // 2
+    each = WOUT // 10
+    rows = each * (N // 2)
+    left = jnp.concatenate([x[k * rows : k * rows + rows, :] for x in operands[:count] for k in (0, 1)], 1)
+    for t in range(10):
+        right = []
+        for x, cross in zip(operands[:count], operands[count:]):
+            right.append(x[2 * rows + TOK * t : 2 * rows + TOK * t + TOK, :])
+            right.append(cross[TOK * t : TOK * t + TOK, :])
+        total = dot(left, jnp.concatenate(right, 0))
+        for p in range(N // 2):
+            scratch[p, each * t : each * t + each, :] = total[each * p : each * p + each]
     for p in range(N // 2):
-        for t in range(WOUT // each):
-            scratch[p, each * t : each * t + each, :] = total[
-                each * p : each * p + each, 128 * t : 128 * t + 128
-            ]
         out[p] = scratch[p].astype(BF)
 
 
-def add_weight_part(message, left, own, cross):
-    full = pl.BlockSpec(memory_space=pltpu.VMEM)
-    args = [*left, *own, *cross]
+def add_weight_part(message, operands, cross):
+    args = [*operands, *cross]
     return pl.pallas_call(
-        weight_kernel,
+        lambda *refs: weight_kernel(*refs[:-3], *refs[-2:]),
         grid=(1,),
         in_specs=[pl.BlockSpec(x.shape, lambda i: (0, 0)) for x in args]
         + [pl.BlockSpec(memory_space=pl.ANY)],
@@ -600,10 +606,11 @@
     )(*args, message)
 
 
-def weight_total(parts, rows):
+def weight_total(parts, rows, after):
     part = parts.astype(F32).sum(0).astype(BF)
     if lax.axis_size("xl") > 1:
         part = (part.astype(F32) + shifted(part, "xl", 1).astype(F32)).astype(BF)
+    part, _ = lax.optimization_barrier((part, after))
     part = gathered(part, "y")
     y, height, lanes = part.shape
     part = part.reshape(y, 10, height // 10, lanes).swapaxes(1, 2)
@@ -637,7 +644,7 @@
         image_output[0],
         image_logsum[0].T,
     )
-    send, upstream, outputs = lax.optimization_barrier((send, output_grad[0], image_output[0]))
+    send, upstream = lax.optimization_barrier((send, output_grad[0]))
     recv = exchange(send, SEQ)
     texts = text_prep(
         device,
@@ -648,18 +655,20 @@
         text_grad[0],
         text_logsum[0].T,
     )
-    upstream, _ = lax.optimization_barrier((upstream, texts[0]))
+    upstream, outputs, _ = lax.optimization_barrier((upstream, image_output[0], texts[0]))
     operands = weight_operands(upstream, outputs)
     text_out, *state = text_pairs(recv, texts)
     operands, text_out = lax.optimization_barrier((operands, text_out))
-    mine = exchange(add_weight_part(text_out, *operands), CHIPS)
+    below = operands[0].shape[0] - 10 * TOK
+    cross = [other_core(x[below:]) for x in operands]
+    mine = exchange(add_weight_part(text_out, operands, cross), CHIPS)
     out = image_pairs(recv, state)
-    mine, out = lax.optimization_barrier((mine, out))
+    mine, _ = lax.optimization_barrier((mine, out))
     text_grads = unpack_text(core, mine, other_core(mine))
     got = exchange(out, SEQ)
     got, text_grads = lax.optimization_barrier((got, text_grads))
     grads = unpack(got)
-    weight_grad = weight_total(mine[:, :WOUT], output_grad.shape[2] // N)
+    weight_grad = weight_total(mine[:, :WOUT], output_grad.shape[2] // N, grads)
     return (*(g[None] for g in grads), *(g[None] for g in text_grads), weight_grad)
 
 

time: 139 us -> 141 us (1.014)
  starting transfers between devices: 41.9 us -> 32.2 us
  waiting for transfers between devices: 35.3 us -> 44.8 us
  local copies, waits for them, and re-layouts: 6.06 us -> 8.09 us
    ppermute x6, starting transfers between devices: 9.92 us -> 3.25 us  [other_core(): return lax.ppermute(x, 'core', [(0, 1), (1, 0)])]
    all_to_all x3, waiting for transfers between devices: 18.8 us -> 23.7 us  [exchange(): return lax.all_to_all(x, axes, 0, 0, tiled=True)]
    all_to_all x3, starting transfers between devices: 21.7 us -> 19.1 us  [exchange(): return lax.all_to_all(x, axes, 0, 0, tiled=True)]
    ppermute x10 -> x7, waiting for transfers between devices: 16.5 us -> 18.9 us  [shifted(): return lax.ppermute(x, axis, [(i, (i + by) % size) for i in range(size)])]
    ppermute x6, waiting for transfers between devices: 0.02 us -> 2.18 us  [other_core(): return lax.ppermute(x, 'core', [(0, 1), (1, 0)])]
    squeeze x1 -> x0, other arithmetic: 1.8 us -> none  [weight_operands(): lax.dynamic_index_in_dim(both, (me + by) % y, 0, False)]
    ppermute x10 -> x7, starting transfers between devices: 10.3 us -> 9.84 us  [shifted(): return lax.ppermute(x, axis, [(i, (i + by) % size) for i in range(size)])]
  transfers between devices with their start and end apart: 19 -> 16, of which waited for: 7 -> 9; matrix products, arithmetic and copies ran while one was open for 4% -> 4% of each run, Pallas kernels for 26% -> 26%
where the time goes in v4:
time: 141 us; the launch traced here: 139 us
  Pallas kernels  51.3 us (36%)
  waiting for transfers between devices  44.8 us (32%)
  starting transfers between devices  32.2 us (23%)
  local copies, waits for them, and re-layouts  8.09 us (6%)
  other arithmetic  2.17 us (2%)
    all_to_all x3, waiting for transfers between devices, exchange(): return lax.all_to_all(x, axes, 0, 0, tiled=True)  23.7 us
    all_to_all x3, starting transfers between devices, exchange(): return lax.all_to_all(x, axes, 0, 0, tiled=True)  19.1 us
    ppermute x7, waiting for transfers between devices, shifted(): return lax.ppermute(x, axis, [(i, (i + by) % size) for i in range(size)])  18.9 us
    pallas_call x1, Pallas kernels, image_pairs(): pl.pallas_call(image_pairs_kernel, in_specs=[full] * 5, out_specs=full, o...  18.6 us
    pallas_call x1, Pallas kernels, text_pairs(): pl.pallas_call(text_pairs_kernel, in_specs=[full] * 7, out_specs=[full] *...  10.2 us
    ppermute x7, starting transfers between devices, shifted(): return lax.ppermute(x, axis, [(i, (i + by) % size) for i in range(size)])  9.84 us
    pallas_call x1, Pallas kernels, pack(): pl.pallas_call(pack_kernel, grid_spec=pltpu.PrefetchScalarGridSpec(num_sc...  7.76 us
    pallas_call x1, Pallas kernels, unpack_text(): pl.pallas_call(unpack_text_kernel, in_specs=[pl.BlockSpec(memory_space=pl...  5.11 us
  transfers between devices with their start and end apart: 16, of which 9 were waited for; matrix products, arithmetic and copies ran while one was open for 4% of the time, Pallas kernels for 26%

profile of v4, /device:TPU:1, one launch (start us, length us, event | category | flops | bytes accessed | tf_op | source)
XLA Modules:
  0.0 139.5 jit_solution(9531780603835742954)
XLA Ops:
  0.6 1.3 copy.39
  1.9 7.8 %pack.1 = bf16[16,400,128]{2,1,0:T(8,128)(2,1)} custom-call(s32[1]{0:T(128)} %bitcast.index, bf16[128,2432]{1,0:T(8,128)(2,1)} %bitcast.80, bf16[2432,1280]{1,0:T(8,128)(2,1)} %w.1, bf16[128,1280]{1,0:T(8,128)(2,1)} %bitcast.88, bf16[128,1280]{1,0:T(8,128)(2,1)} %bitcast.89, bf16[128,1280]{1,0:T(8,128)(2,1)} %bitcast.90, bf16[128,1280]{1,0:T(8,128)(2,1)} %bitcast.86, ...), custom_call_target="tpu_custom_call" | custom-call | tf_op jit(solution)/shard_map/pack/pallas_call | solution.py:131
  9.7 9.4 %all-to-all-start = ((bf16[16,400,128]{2,1,0:T(8,128)(2,1)}), bf16[16,400,128]{2,1,0:T(8,128)(2,1)S(1)}, u32[]{:S(2)}, u32[]{:S(2)}) async-start(bf16[16,400,128]{2,1,0:T(8,128)(2,1)} %pack.1), calls=%async_computation | async-start | bytes 3276800 | tf_op jit(solution)/shard_map/all_to_all | solution.py:535
  19.1 0.6 copy.38
  19.8 2.4 %text_prep.1 = (bf16[384,128]{1,0:T(8,128)(2,1)}, bf16[384,128]{1,0:T(8,128)(2,1)}, bf16[16,384]{1,0:T(8,128)(2,1)}, bf16[256,128]{1,0:T(8,128)(2,1)}, bf16[256,...) custom-call(s32[1]{0:T(128)} %bitcast.index, bf16[333,1280]{1,0:T(8,128)(2,1)} %bitcast.66, bf16[333,1280]{1,0:T(8,128)(2,1)} %bitcast.68, ...), custom_call_target="tpu_custom_call" | custom-call | tf_op jit(solution)/shard_map/text_prep/pallas_call | solution.py:211
  22.2 0.3 copy.26
  22.7 0.2 collective-permute-start
  22.9 0.6 copy-done.6
  23.5 0.2 copy.28
  23.7 0.2 copy.29
  23.9 0.6 collective-permute-done
  24.5 0.2 broadcast_in_dim.42
  24.7 1.1 pad_maximum_fusion
  25.8 1.2 dynamic-slice_bitcast_fusion
  27.0 1.3 collective-permute-start.1
  28.3 2.6 %collective-permute-start.2 = (bf16[1920,128]{1,0:T(8,128)(2,1)}, bf16[1920,128]{1,0:T(8,128)(2,1)S(1)}, u32[]{:S(2)}, u32[]{:S(2)}) collective-permute-start(bf16[1920,128]{1,0:T(8,128)(2,1)} %get-tuple-element.72), channel_id=1, source_target_pairs={{0,64},{32,96},{64,0},{96,32},{1,65},{33,97},{65,1},{97,33},{2,66}... | collective-permute-start | bytes 1474568 | tf_op jit(solution)/shard_map/ppermute | solution.py:544
  30.9 1.1 collective-permute-start.3
  32.0 10.7 %all-to-all-done.recv = bf16[16,400,128]{2,1,0:T(8,128)(2,1)S(1)} async-done(((bf16[16,400,128]{2,1,0:T(8,128)(2,1)}), bf16[16,400,128]{2,1,0:T(8,128)(2,1)S(1)}, u32[]{:S(2)}, u32[]{:S(2)}) %all-to-all-start) | async-done | bytes 1638432 | tf_op jit(solution)/shard_map/all_to_all | solution.py:535
  42.7 1.2 copy-done
  43.9 10.2 %text_pairs.1 = (bf16[8,1184,128]{2,1,0:T(8,128)(2,1)}, f32[2048,128]{1,0:T(8,128)}, f32[64,2048]{1,0:T(8,128)}, f32[1024,128]{1,0:T(8,128)}, f32[64,1024]{1,0:T(8,128)}) custom-call(bf16[16,400,128]{2,1,0:T(8,128)(2,1)} %copy-done, bf16[384,128]{1,0:T(8,128)(2,1)} %get-tuple-element.40.wqg, bf16[384,128]{1,0:T(8,128)(2,1)} %get-tuple-element.41.wkv, ...), custom_call_target="tpu_custom_call" | custom-call | tf_op jit(solution)/shard_map/text_pairs/pallas_call | solution.py:374
  54.2 1.0 collective-permute-start.4
  55.2 0.1 collective-permute-start.5
  55.3 0.6 collective-permute-start.6
  55.9 1.0 slice.21
  56.9 0.1 collective-permute-start.7
  57.0 0.3 collective-permute-done.6.refs_6_
  57.4 1.2 collective-permute-done.7.refs_7_
  58.6 0.7 copy-done.10
  59.3 4.6 %weight.1 = bf16[8,1184,128]{2,1,0:T(8,128)(2,1)} custom-call(bf16[1920,128]{1,0:T(8,128)(2,1)} %copy-done.2, bf16[1920,128]{1,0:T(8,128)(2,1)} %copy-done.4, bf16[1920,128]{1,0:T(8,128)(2,1)} %copy-done.5, bf16[1920,128]{1,0:T(8,128)(2,1)} %collective-permute-done.3.refs_3_, bf16[1280,128]{1,0:T(8,128)(2,1)} %copy-done.7, ...), custom_call_target="tpu_custom_call", output_to_operand_aliasing={{}: (8, {})} | custom-call | tf_op jit(solution)/shard_map/weight/pallas_call | solution.py:595
  64.0 5.4 %all-to-all-start.2 = ((bf16[8,1184,128]{2,1,0:T(8,128)(2,1)}), bf16[8,1184,128]{2,1,0:T(8,128)(2,1)S(1)}, u32[]{:S(2)}, u32[]{:S(2)}) async-start(bf16[8,1184,128]{2,1,0:T(8,128)(2,1)} %weight.1), calls=%async_computation.2 | async-start | bytes 4849664 | tf_op jit(solution)/shard_map/all_to_all | solution.py:535
  69.3 18.6 %image_pairs.1 = bf16[16,288,128]{2,1,0:T(8,128)(2,1)} custom-call(bf16[16,400,128]{2,1,0:T(8,128)(2,1)} %copy-done, f32[2048,128]{1,0:T(8,128)} %get-tuple-element.46.a, f32[64,2048]{1,0:T(8,128)} %get-tuple-element.47.b, f32[1024,128]{1,0:T(8,128)} %get-tuple-element.48.c, f32[64,1024]{1,0:T(8,128)} %get-tuple-element.49.d), custom_call_target="tpu_custom_call" | custom-call | tf_op jit(solution)/shard_map/image_pairs/pallas_call | solution.py:414
  87.9 13.0 %all-to-all-done.2.mine = bf16[8,1184,128]{2,1,0:T(8,128)(2,1)S(1)} async-done(((bf16[8,1184,128]{2,1,0:T(8,128)(2,1)}), bf16[8,1184,128]{2,1,0:T(8,128)(2,1)S(1)}, u32[]{:S(2)}, u32[]{:S(2)}) %all-to-all-start.2) | async-done | bytes 2424864 | tf_op jit(solution)/shard_map/all_to_all | solution.py:535
  101.0 1.3 collective-permute-start.8
  102.3 4.3 %all-to-all-start.1 = ((bf16[16,288,128]{2,1,0:T(8,128)(2,1)}), bf16[16,288,128]{2,1,0:T(8,128)(2,1)}, u32[]{:S(2)}, u32[]{:S(2)}) async-start(bf16[16,288,128]{2,1,0:T(8,128)(2,1)} %image_pairs.1), calls=%async_computation.1 | async-start | bytes 2359296 | tf_op jit(solution)/shard_map/all_to_all | solution.py:535
  106.6 0.1 slice_reduce_fusion
  106.7 0.4 collective-permute-start.9
  107.1 15.6 %collective-permute-done.9 = bf16[400,128]{1,0:T(8,128)(2,1)S(1)} collective-permute-done((bf16[400,128]{1,0:T(8,128)(2,1)S(1)}, bf16[400,128]{1,0:T(8,128)(2,1)S(1)}, u32[]{:S(2)}, u32[]{:S(2)}) %collective-permute-start.9) | collective-permute-done | bytes 102432 | tf_op jit(solution)/shard_map/ppermute | solution.py:544
  122.8 5.1 %unpack_text.1 = (bf16[333,1280]{1,0:T(8,128)(2,1)}, bf16[333,1280]{1,0:T(8,128)(2,1)}, bf16[333,1280]{1,0:T(8,128)(2,1)}) custom-call(s32[1]{0:T(128)} %bitcast.13.core, bf16[8,1184,128]{2,1,0:T(8,128)(2,1)} %copy-done.1, bf16[8,1184,128]{2,1,0:T(8,128)(2,1)} %collective-permute-done.8.other), custom_call_target="tpu_custom_call" | custom-call | tf_op jit(solution)/shard_map/unpack_text/pallas_call | solution.py:524
  127.9 2.6 %unpack.1 = (bf16[128,1280]{1,0:T(8,128)(2,1)}, bf16[128,1280]{1,0:T(8,128)(2,1)}, bf16[128,1280]{1,0:T(8,128)(2,1)}) custom-call(bf16[16,288,128]{2,1,0:T(8,128)(2,1)} %all-to-all-done.1.recv), custom_call_target="tpu_custom_call" | custom-call | tf_op jit(solution)/shard_map/unpack/pallas_call | solution.py:470
  130.5 1.0 collective-permute-start.10
  131.4 2.1 %collective-permute-start.11 = (bf16[400,128]{1,0:T(8,128)(2,1)S(1)}, bf16[400,128]{1,0:T(8,128)(2,1)S(1)}, u32[]{:S(2)}, u32[]{:S(2)}) collective-permute-start(bf16[400,128]{1,0:T(8,128)(2,1)S(1)} %add_convert_fusion), channel_id=1, source_target_pairs={{0,64},{32,96},{64,0},{96,32},{1,65},{33,97},{65,1},{97,33},{2,66}... | collective-permute-start | bytes 307208 | tf_op jit(solution)/shard_map/ppermute | solution.py:544
  133.5 1.4 %collective-permute-start.12 = (bf16[400,128]{1,0:T(8,128)(2,1)S(1)}, bf16[400,128]{1,0:T(8,128)(2,1)S(1)}, u32[]{:S(2)}, u32[]{:S(2)}) collective-permute-start(bf16[400,128]{1,0:T(8,128)(2,1)S(1)} %add_convert_fusion), channel_id=1, source_target_pairs={{0,96},{32,0},{64,32},{96,64},{1,97},{33,1},{65,33},{97,65},{2,98}... | collective-permute-start | bytes 307208 | tf_op jit(solution)/shard_map/ppermute | solution.py:544
  135.0 0.2 collective-permute-done.10
  135.2 2.5 %collective-permute-done.11 = bf16[400,128]{1,0:T(8,128)(2,1)S(1)} collective-permute-done((bf16[400,128]{1,0:T(8,128)(2,1)S(1)}, bf16[400,128]{1,0:T(8,128)(2,1)S(1)}, u32[]{:S(2)}, u32[]{:S(2)}) %collective-permute-start.11) | collective-permute-done | bytes 102432 | tf_op jit(solution)/shard_map/ppermute | solution.py:544
  137.7 0.6 collective-permute-done.12
  138.3 0.1 copy.30
  138.4 0.1 copy.37
  138.5 0.9 slice_convert_fusion
  (40 shorter events, 0.4 us)
Async XLA Ops:
  9.7 9.4 %copy-start.11 = (f32[1,333,20]{1,0,2:T(1,128)S(1)}, f32[1,333,20]{1,0,2:T(1,128)}, u32[]{:S(2)}) copy-start(f32[1,333,20]{1,0,2:T(1,128)} %param.24) | copy-start | bytes 79924
  9.7 33.0 %all-to-all-start = ((bf16[16,400,128]{2,1,0:T(8,128)(2,1)}), bf16[16,400,128]{2,1,0:T(8,128)(2,1)S(1)}, u32[]{:S(2)}, u32[]{:S(2)}) async-start(bf16[16,400,128]{2,1,0:T(8,128)(2,1)} %pack.1), calls=%async_computation | async-start | bytes 3276800 | tf_op jit(solution)/shard_map/all_to_all | solution.py:535
  19.8 2.4 %copy-start.3 = (bf16[1,128,2432]{2,1,0:T(8,128)(2,1)S(1)}, bf16[1,128,2432]{2,1,0:T(8,128)(2,1)}, u32[]{:S(2)}) copy-start(bf16[1,128,2432]{2,1,0:T(8,128)(2,1)} %param.17) | copy-start | bytes 1867780
  22.5 1.0 copy-start.6
  22.7 1.8 %collective-permute-start = (bf16[4,320,128]{2,1,0:T(8,128)(2,1)S(1)}, bf16[4,320,128]{2,1,0:T(8,128)(2,1)}, u32[]{:S(2)}, u32[]{:S(2)}) collective-permute-start(bf16[4,320,128]{2,1,0:T(8,128)(2,1)S(1)} %get-tuple-element.76), channel_id=1, source_target_pairs={{0,1},{1,0},{2,3},{3,2},{4,5},{5,4},{6,7},{7,6},{8,9},{9,8},{10,11... | collective-permute-start | bytes 983048 | tf_op jit(solution)/shard_map/ppermute | solution.py:539
  27.0 31.6 %copy-start.2 = (bf16[1920,128]{1,0:T(8,128)(2,1)}, bf16[1920,128]{1,0:T(8,128)(2,1)S(1)}, u32[]{:S(2)}) copy-start(bf16[1920,128]{1,0:T(8,128)(2,1)S(1)} %get-tuple-element.54.refs_0_) | copy-start | bytes 1474564
  27.0 27.1 %collective-permute-start.1 = (bf16[1920,128]{1,0:T(8,128)(2,1)}, bf16[1920,128]{1,0:T(8,128)(2,1)S(1)}, u32[]{:S(2)}, u32[]{:S(2)}) collective-permute-start(bf16[1920,128]{1,0:T(8,128)(2,1)} %get-tuple-element.73), channel_id=1, source_target_pairs={{0,32},{32,64},{64,96},{96,0},{1,33},{33,65},{65,97},{97,1},{2,34}... | collective-permute-start | bytes 1474568 | tf_op jit(solution)/shard_map/ppermute | solution.py:544
  28.3 25.8 %collective-permute-start.2 = (bf16[1920,128]{1,0:T(8,128)(2,1)}, bf16[1920,128]{1,0:T(8,128)(2,1)S(1)}, u32[]{:S(2)}, u32[]{:S(2)}) collective-permute-start(bf16[1920,128]{1,0:T(8,128)(2,1)} %get-tuple-element.72), channel_id=1, source_target_pairs={{0,64},{32,96},{64,0},{96,32},{1,65},{33,97},{65,1},{97,33},{2,66}... | collective-permute-start | bytes 1474568 | tf_op jit(solution)/shard_map/ppermute | solution.py:544
  30.9 23.2 %collective-permute-start.3 = (bf16[1920,128]{1,0:T(8,128)(2,1)}, bf16[1920,128]{1,0:T(8,128)(2,1)}, u32[]{:S(2)}, u32[]{:S(2)}) collective-permute-start(bf16[1920,128]{1,0:T(8,128)(2,1)} %get-tuple-element.71), channel_id=1, source_target_pairs={{0,96},{32,0},{64,32},{96,64},{1,97},{33,1},{65,33},{97,65},{2,98}... | collective-permute-start | bytes 1474568 | tf_op jit(solution)/shard_map/ppermute | solution.py:544
  42.7 1.2 copy-start
  54.1 4.5 %copy-start.4 = (bf16[1920,128]{1,0:T(8,128)(2,1)}, bf16[1920,128]{1,0:T(8,128)(2,1)S(1)}, u32[]{:S(2)}) copy-start(bf16[1920,128]{1,0:T(8,128)(2,1)S(1)} %collective-permute-done.1.refs_1_) | copy-start | bytes 1474564
  54.1 4.5 %copy-start.5 = (bf16[1920,128]{1,0:T(8,128)(2,1)}, bf16[1920,128]{1,0:T(8,128)(2,1)S(1)}, u32[]{:S(2)}) copy-start(bf16[1920,128]{1,0:T(8,128)(2,1)S(1)} %collective-permute-done.2.refs_2_) | copy-start | bytes 1474564
  54.2 2.8 %collective-permute-start.4 = (bf16[1280,128]{1,0:T(8,128)(2,1)S(1)}, bf16[1280,128]{1,0:T(8,128)(2,1)S(1)}, u32[]{:S(2)}, u32[]{:S(2)}) collective-permute-start(bf16[1280,128]{1,0:T(8,128)(2,1)S(1)} %slice.18), channel_id=1, source_target_pairs={{0,1},{1,0},{2,3},{3,2},{4,5},{5,4},{6,7},{7,6},{8,9},{9,8},{10,11... | collective-permute-start | bytes 983048 | tf_op jit(solution)/shard_map/ppermute | solution.py:539
  55.2 1.8 %collective-permute-start.5 = (bf16[1280,128]{1,0:T(8,128)(2,1)S(1)}, bf16[1280,128]{1,0:T(8,128)(2,1)S(1)}, u32[]{:S(2)}, u32[]{:S(2)}) collective-permute-start(bf16[1280,128]{1,0:T(8,128)(2,1)S(1)} %slice.19), channel_id=1, source_target_pairs={{0,1},{1,0},{2,3},{3,2},{4,5},{5,4},{6,7},{7,6},{8,9},{9,8},{10,11... | collective-permute-start | bytes 983048 | tf_op jit(solution)/shard_map/ppermute | solution.py:539
  55.3 2.1 %collective-permute-start.6 = (bf16[1280,128]{1,0:T(8,128)(2,1)S(1)}, bf16[1280,128]{1,0:T(8,128)(2,1)S(1)}, u32[]{:S(2)}, u32[]{:S(2)}) collective-permute-start(bf16[1280,128]{1,0:T(8,128)(2,1)S(1)} %slice.20), channel_id=1, source_target_pairs={{0,1},{1,0},{2,3},{3,2},{4,5},{5,4},{6,7},{7,6},{8,9},{9,8},{10,11... | collective-permute-start | bytes 983048 | tf_op jit(solution)/shard_map/ppermute | solution.py:539
  56.9 1.7 %collective-permute-start.7 = (bf16[1280,128]{1,0:T(8,128)(2,1)S(1)}, bf16[1280,128]{1,0:T(8,128)(2,1)S(1)}, u32[]{:S(2)}, u32[]{:S(2)}) collective-permute-start(bf16[1280,128]{1,0:T(8,128)(2,1)S(1)} %slice.21), channel_id=1, source_target_pairs={{0,1},{1,0},{2,3},{3,2},{4,5},{5,4},{6,7},{7,6},{8,9},{9,8},{10,11... | collective-permute-start | bytes 983048 | tf_op jit(solution)/shard_map/ppermute | solution.py:539
  57.0 1.6 %copy-start.7 = (bf16[1280,128]{1,0:T(8,128)(2,1)}, bf16[1280,128]{1,0:T(8,128)(2,1)S(1)}, u32[]{:S(2)}) copy-start(bf16[1280,128]{1,0:T(8,128)(2,1)S(1)} %collective-permute-done.4.refs_4_) | copy-start | bytes 983044
  57.0 1.6 %copy-start.8 = (bf16[1280,128]{1,0:T(8,128)(2,1)}, bf16[1280,128]{1,0:T(8,128)(2,1)S(1)}, u32[]{:S(2)}) copy-start(bf16[1280,128]{1,0:T(8,128)(2,1)S(1)} %collective-permute-done.5.refs_5_) | copy-start | bytes 983044
  57.4 1.3 copy-start.9
  58.6 0.7 copy-start.10
  64.0 37.0 %all-to-all-start.2 = ((bf16[8,1184,128]{2,1,0:T(8,128)(2,1)}), bf16[8,1184,128]{2,1,0:T(8,128)(2,1)S(1)}, u32[]{:S(2)}, u32[]{:S(2)}) async-start(bf16[8,1184,128]{2,1,0:T(8,128)(2,1)} %weight.1), calls=%async_computation.2 | async-start | bytes 4849664 | tf_op jit(solution)/shard_map/all_to_all | solution.py:535
  101.0 21.8 %copy-start.1 = (bf16[8,1184,128]{2,1,0:T(8,128)(2,1)}, bf16[8,1184,128]{2,1,0:T(8,128)(2,1)S(1)}, u32[]{:S(2)}) copy-start(bf16[8,1184,128]{2,1,0:T(8,128)(2,1)S(1)} %all-to-all-done.2.mine) | copy-start | bytes 7274500
  101.0 21.8 %collective-permute-start.8 = (bf16[8,1184,128]{2,1,0:T(8,128)(2,1)S(1)}, bf16[8,1184,128]{2,1,0:T(8,128)(2,1)}, u32[]{:S(2)}, u32[]{:S(2)}) collective-permute-start(bf16[8,1184,128]{2,1,0:T(8,128)(2,1)S(1)} %all-to-all-done.2.mine), channel_id=1, source_target_pairs={{0,1},{1,0},{2,3},{3,2},{4,5},{5,4},{6,7},{7,6},{8,9},{9,8},{10,11... | collective-permute-start | bytes 7274504 | tf_op jit(solution)/shard_map/ppermute | solution.py:539
  102.3 25.6 %all-to-all-start.1 = ((bf16[16,288,128]{2,1,0:T(8,128)(2,1)}), bf16[16,288,128]{2,1,0:T(8,128)(2,1)}, u32[]{:S(2)}, u32[]{:S(2)}) async-start(bf16[16,288,128]{2,1,0:T(8,128)(2,1)} %image_pairs.1), calls=%async_computation.1 | async-start | bytes 2359296 | tf_op jit(solution)/shard_map/all_to_all | solution.py:535
  106.7 16.0 %collective-permute-start.9 = (bf16[400,128]{1,0:T(8,128)(2,1)S(1)}, bf16[400,128]{1,0:T(8,128)(2,1)S(1)}, u32[]{:S(2)}, u32[]{:S(2)}) collective-permute-start(bf16[400,128]{1,0:T(8,128)(2,1)S(1)} %slice_reduce_fusion), channel_id=1, source_target_pairs={{0,16},{16,0},{1,17},{17,1},{2,18},{18,2},{3,19},{19,3},{4,20},{20... | collective-permute-start | bytes 307208 | tf_op jit(solution)/shard_map/ppermute | solution.py:544
  130.5 4.7 %collective-permute-start.10 = (bf16[400,128]{1,0:T(8,128)(2,1)S(1)}, bf16[400,128]{1,0:T(8,128)(2,1)S(1)}, u32[]{:S(2)}, u32[]{:S(2)}) collective-permute-start(bf16[400,128]{1,0:T(8,128)(2,1)S(1)} %add_convert_fusion), channel_id=1, source_target_pairs={{0,32},{32,64},{64,96},{96,0},{1,33},{33,65},{65,97},{97,1},{2,34}... | collective-permute-start | bytes 307208 | tf_op jit(solution)/shard_map/ppermute | solution.py:544
  131.4 6.3 %collective-permute-start.11 = (bf16[400,128]{1,0:T(8,128)(2,1)S(1)}, bf16[400,128]{1,0:T(8,128)(2,1)S(1)}, u32[]{:S(2)}, u32[]{:S(2)}) collective-permute-start(bf16[400,128]{1,0:T(8,128)(2,1)S(1)} %add_convert_fusion), channel_id=1, source_target_pairs={{0,64},{32,96},{64,0},{96,32},{1,65},{33,97},{65,1},{97,33},{2,66}... | collective-permute-start | bytes 307208 | tf_op jit(solution)/shard_map/ppermute | solution.py:544
  133.5 4.7 %collective-permute-start.12 = (bf16[400,128]{1,0:T(8,128)(2,1)S(1)}, bf16[400,128]{1,0:T(8,128)(2,1)S(1)}, u32[]{:S(2)}, u32[]{:S(2)}) collective-permute-start(bf16[400,128]{1,0:T(8,128)(2,1)S(1)} %add_convert_fusion), channel_id=1, source_target_pairs={{0,96},{32,0},{64,32},{96,64},{1,97},{33,1},{65,33},{97,65},{2,98}... | collective-permute-start | bytes 307208 | tf_op jit(solution)/shard_map/ppermute | solution.py:544

commit v5 on v4

--- a/solution.py
+++ b/solution.py
@@ -89,7 +89,7 @@
         g * o[...].astype(F32),
     )
     lsum = picked_rows(
-        jnp.where(iota((8, 20), 1) == 4 * j + iota((8, 20), 0), 1.0, 0.0), l[...]
+        jnp.where(iota((8, 20), 1) == 4 * j + iota((8, 20), 0), 1.0, 0.0), l[:, 0, :]
     )
     low = iota((TOK, 128), 1) < 64
 
@@ -140,7 +140,7 @@
                 column,
                 column,
                 column,
-                pl.BlockSpec((20, TOK), lambda j, s: (0, 0)),
+                pl.BlockSpec((20, 1, TOK), lambda j, s: (0, 0, 0)),
             ],
             out_specs=pl.BlockSpec((N, MSG, 128), lambda j, s: (0, 0, 0)),
         ),
@@ -158,7 +158,7 @@
         buf[n] = jnp.zeros(buf.shape[1:], F32)
         buf[n, 0:TXT, :] = ref[...].astype(F32)
     lbuf[...] = jnp.zeros(lbuf.shape, F32)
-    lbuf[:, 0:TXT] = l[...]
+    lbuf[:, 0:TXT] = l[:, 0, :]
 
     def gather(first, odd, q_rows, k_rows):
         q, k, v = buf[first, q_rows, :], buf[first + 1, k_rows, :], buf[first + 2, k_rows, :]
@@ -213,7 +213,7 @@
         grid_spec=pltpu.PrefetchScalarGridSpec(
             num_scalar_prefetch=1,
             grid=(1,),
-            in_specs=[whole] * 5 + [shared] * 5 + [pl.BlockSpec((20, TXT), lambda i, s: (0, 0))],
+            in_specs=[whole] * 5 + [shared] * 5 + [pl.BlockSpec((20, 1, TXT), lambda i, s: (0, 0, 0))],
             out_specs=[pl.BlockSpec(s, lambda i, s_: (0, 0)) for s in shapes],
             scratch_shapes=[
                 pltpu.VMEM((10, HALF + HALF_Q, 128), F32),
@@ -565,35 +565,35 @@
     blocks = blocks.reshape(2, y, -1, tokens)
     mine = lax.dynamic_index_in_dim(blocks, core, 0, False)
     theirs = other_core(lax.dynamic_index_in_dim(blocks, 1 - core, 0, False))
-    tiles = o.reshape(tokens, -1, 128).swapaxes(0, 1).reshape(-1, 128)
-    everyone = jnp.broadcast_to(tiles[None], (y, *tiles.shape))
-    both = jnp.concatenate([mine, theirs, everyone], 1)
+    both = jnp.concatenate([mine, theirs], 2)
     pieces = [lax.dynamic_index_in_dim(both, (me + by) % y, 0, False) for by in range(y)]
-    return pieces[:1] + [shifted(p, "y", by) for by, p in enumerate(pieces) if by]
+    left, right = pieces[:1], [o]
+    for by in range(1, y):
+        right.append(shifted(o, "y", by))
+        left.append(shifted(pieces[by], "y", by))
+    return left, right
 
 
 def weight_kernel(*refs):
-    *operands, out, scratch = refs
-    count = len(operands) // 2
+    *operands, _, out, scratch = refs
+    count = len(operands) // 3
+    total = None
+    for left, own, cross in zip(*(operands[k * count : k * count + count] for k in range(3))):
+        term = dot(left[...], jnp.concatenate([own[...], cross[...]], 0))
+        total = term if total is None else total + term
     each = WOUT // 10
-    rows = each * (N // 2)
-    left = jnp.concatenate([x[k * rows : k * rows + rows, :] for x in operands[:count] for k in (0, 1)], 1)
-    for t in range(10):
-        right = []
-        for x, cross in zip(operands[:count], operands[count:]):
-            right.append(x[2 * rows + TOK * t : 2 * rows + TOK * t + TOK, :])
-            right.append(cross[TOK * t : TOK * t + TOK, :])
-        total = dot(left, jnp.concatenate(right, 0))
-        for p in range(N // 2):
-            scratch[p, each * t : each * t + each, :] = total[each * p : each * p + each]
     for p in range(N // 2):
+        for t in range(10):
+            scratch[p, each * t : each * t + each, :] = total[
+                each * p : each * p + each, 128 * t : 128 * t + 128
+            ]
         out[p] = scratch[p].astype(BF)
 
 
-def add_weight_part(message, operands, cross):
-    args = [*operands, *cross]
+def add_weight_part(message, left, own, cross):
+    args = [*left, *own, *cross]
     return pl.pallas_call(
-        lambda *refs: weight_kernel(*refs[:-3], *refs[-2:]),
+        weight_kernel,
         grid=(1,),
         in_specs=[pl.BlockSpec(x.shape, lambda i: (0, 0)) for x in args]
         + [pl.BlockSpec(memory_space=pl.ANY)],
@@ -607,11 +607,10 @@
 
 
 def weight_total(parts, rows, after):
-    part = parts.astype(F32).sum(0).astype(BF)
+    part = gathered(parts.astype(F32).sum(0).astype(BF), "y")
     if lax.axis_size("xl") > 1:
-        part = (part.astype(F32) + shifted(part, "xl", 1).astype(F32)).astype(BF)
-    part, _ = lax.optimization_barrier((part, after))
-    part = gathered(part, "y")
+        other, _ = lax.optimization_barrier((shifted(part, "xl", 1), after))
+        part = part.astype(F32) + other.astype(F32)
     y, height, lanes = part.shape
     part = part.reshape(y, 10, height // 10, lanes).swapaxes(1, 2)
     return part.reshape(-1, 10 * lanes)[:rows].astype(F32)
@@ -642,7 +641,7 @@
         image_key[0],
         image_value[0],
         image_output[0],
-        image_logsum[0].T,
+        image_logsum.transpose(2, 0, 1),
     )
     send, upstream = lax.optimization_barrier((send, output_grad[0]))
     recv = exchange(send, SEQ)
@@ -653,15 +652,15 @@
         text_value[0],
         text_output[0],
         text_grad[0],
-        text_logsum[0].T,
+        text_logsum.transpose(2, 0, 1),
     )
     upstream, outputs, _ = lax.optimization_barrier((upstream, image_output[0], texts[0]))
-    operands = weight_operands(upstream, outputs)
+    left, own = weight_operands(upstream, outputs)
     text_out, *state = text_pairs(recv, texts)
-    operands, text_out = lax.optimization_barrier((operands, text_out))
-    below = operands[0].shape[0] - 10 * TOK
-    cross = [other_core(x[below:]) for x in operands]
-    mine = exchange(add_weight_part(text_out, operands, cross), CHIPS)
+    cross = [other_core(outputs)]
+    left, own, text_out = lax.optimization_barrier((left, own, text_out))
+    cross += [other_core(x) for x in own[1:]]
+    mine = exchange(add_weight_part(text_out, left, own, cross), CHIPS)
     out = image_pairs(recv, state)
     mine, _ = lax.optimization_barrier((mine, out))
     text_grads = unpack_text(core, mine, other_core(mine))

time: 141 us -> 128 us (0.908)
  waiting for transfers between devices: 44.8 us -> 34.2 us
  local copies, waits for them, and re-layouts: 8.09 us -> 4.94 us
  starting transfers between devices: 32.2 us -> 33.8 us
    ppermute x7 -> x10, waiting for transfers between devices: 18.9 us -> 8.6 us  [shifted(): return lax.ppermute(x, axis, [(i, (i + by) % size) for i in range(size)])]
    ppermute x7 -> x10, starting transfers between devices: 9.84 us -> 13.4 us  [shifted(): return lax.ppermute(x, axis, [(i, (i + by) % size) for i in range(size)])]
    unnamed x27 -> x23, local copies, waits for them, and re-layouts: 4.55 us -> 2.48 us
    squeeze x0 -> x1, other arithmetic: none -> 1.8 us  [weight_operands(): lax.dynamic_index_in_dim(both, (me + by) % y, 0, False)]
    all_to_all x3, starting transfers between devices: 19.1 us -> 17.4 us  [exchange(): return lax.all_to_all(x, axes, 0, 0, tiled=True)]
  transfers between devices with their start and end apart: 16 -> 19, of which waited for: 9 -> 11; matrix products, arithmetic and copies ran while one was open for 4% -> 3% of each run, Pallas kernels for 26% -> 31%
where the time goes in v5:
time: 128 us; the launch traced here: 126 us
  Pallas kernels  50.6 us (40%)
  waiting for transfers between devices  34.2 us (27%)
  starting transfers between devices  33.8 us (26%)
  local copies, waits for them, and re-layouts  4.94 us (4%)
  other arithmetic  1.99 us (2%)
    all_to_all x3, waiting for transfers between devices, exchange(): return lax.all_to_all(x, axes, 0, 0, tiled=True)  23.7 us
    pallas_call x1, Pallas kernels, image_pairs(): pl.pallas_call(image_pairs_kernel, in_specs=[full] * 5, out_specs=full, o...  18.6 us
    all_to_all x3, starting transfers between devices, exchange(): return lax.all_to_all(x, axes, 0, 0, tiled=True)  17.4 us
    ppermute x10, starting transfers between devices, shifted(): return lax.ppermute(x, axis, [(i, (i + by) % size) for i in range(size)])  13.4 us
    pallas_call x1, Pallas kernels, text_pairs(): pl.pallas_call(text_pairs_kernel, in_specs=[full] * 7, out_specs=[full] *...  10.2 us
    ppermute x10, waiting for transfers between devices, shifted(): return lax.ppermute(x, axis, [(i, (i + by) % size) for i in range(size)])  8.6 us
    pallas_call x1, Pallas kernels, pack(): pl.pallas_call(pack_kernel, grid_spec=pltpu.PrefetchScalarGridSpec(num_sc...  7.79 us
    pallas_call x1, Pallas kernels, unpack_text(): pl.pallas_call(unpack_text_kernel, in_specs=[pl.BlockSpec(memory_space=pl...  5.11 us
  transfers between devices with their start and end apart: 19, of which 11 were waited for; matrix products, arithmetic and copies ran while one was open for 3% of the time, Pallas kernels for 31%

profile of v5, /device:TPU:1, one launch (start us, length us, event | category | flops | bytes accessed | tf_op | source)
XLA Modules:
  0.0 126.4 jit_solution(11579751147136348133)
XLA Ops:
  0.6 7.8 %pack.1 = bf16[16,400,128]{2,1,0:T(8,128)(2,1)} custom-call(s32[1]{0:T(128)} %bitcast.index, bf16[128,2432]{1,0:T(8,128)(2,1)} %bitcast.69, bf16[2432,1280]{1,0:T(8,128)(2,1)} %w.1, bf16[128,1280]{1,0:T(8,128)(2,1)} %bitcast.78, bf16[128,1280]{1,0:T(8,128)(2,1)} %bitcast.79, bf16[128,1280]{1,0:T(8,128)(2,1)} %bitcast.80, bf16[128,1280]{1,0:T(8,128)(2,1)} %bitcast.72, ...), custom_call_target="tpu_custom_call" | custom-call | tf_op jit(solution)/shard_map/pack/pallas_call | solution.py:131
  8.4 9.3 %all-to-all-start = ((bf16[16,400,128]{2,1,0:T(8,128)(2,1)}), bf16[16,400,128]{2,1,0:T(8,128)(2,1)S(1)}, u32[]{:S(2)}, u32[]{:S(2)}) async-start(bf16[16,400,128]{2,1,0:T(8,128)(2,1)} %pack.1), calls=%async_computation | async-start | bytes 3276800 | tf_op jit(solution)/shard_map/all_to_all | solution.py:535
  17.7 2.4 %text_prep.1 = (bf16[384,128]{1,0:T(8,128)(2,1)}, bf16[384,128]{1,0:T(8,128)(2,1)}, bf16[16,384]{1,0:T(8,128)(2,1)}, bf16[256,128]{1,0:T(8,128)(2,1)}, bf16[256,...) custom-call(s32[1]{0:T(128)} %bitcast.index, bf16[333,1280]{1,0:T(8,128)(2,1)} %bitcast.55, bf16[333,1280]{1,0:T(8,128)(2,1)} %bitcast.57, ...), custom_call_target="tpu_custom_call" | custom-call | tf_op jit(solution)/shard_map/text_prep/pallas_call | solution.py:211
  20.2 0.3 copy.24
  20.7 0.8 dynamic-slice_bitcast_fusion
  21.4 0.1 collective-permute-start
  21.5 1.3 %collective-permute-start.4 = (bf16[128,1280]{1,0:T(8,128)(2,1)S(1)}, bf16[128,1280]{1,0:T(8,128)(2,1)S(1)}, u32[]{:S(2)}, u32[]{:S(2)}) collective-permute-start(bf16[128,1280]{1,0:T(8,128)(2,1)S(1)} %bitcast.74), channel_id=1, source_target_pairs={{0,32},{32,64},{64,96},{96,0},{1,33},{33,65},{65,97},{97,1},{2,34}... | collective-permute-start | bytes 983048 | tf_op jit(solution)/shard_map/ppermute | solution.py:544
  22.8 2.6 %collective-permute-start.5 = (bf16[128,1280]{1,0:T(8,128)(2,1)S(1)}, bf16[128,1280]{1,0:T(8,128)(2,1)S(1)}, u32[]{:S(2)}, u32[]{:S(2)}) collective-permute-start(bf16[128,1280]{1,0:T(8,128)(2,1)S(1)} %bitcast.75), channel_id=1, source_target_pairs={{0,64},{32,96},{64,0},{96,32},{1,65},{33,97},{65,1},{97,33},{2,66}... | collective-permute-start | bytes 983048 | tf_op jit(solution)/shard_map/ppermute | solution.py:544
  25.5 1.1 collective-permute-start.6
  26.5 1.8 %fusion.1 = (bf16[320,256]{1,0:T(8,128)(2,1)S(1)}, bf16[320,256]{1,0:T(8,128)(2,1)}, bf16[320,256]{1,0:T(8,128)(2,1)}, bf16[320,256]{1,0:T(8,128)(2,1)}) fusion(s32[]{:T(128)S(6)} %select_n.73, bf16[4,320,128]{2,1,0:T(8,128)(2,1)S(1)} %get-tuple-element.84, bf16[4,320,128]{2,1,0:T(8,128)(2,1)} %collective-permute-done, s32[]{:T(128)S(6)} %select_n.67, ...), kind=kLoop, calls=%fused_computation.14 | loop fusion | flops 1310720 | bytes 1310736 | tf_op jit(solution)/shard_map/jit(dynamic_index_in_dim)/squeeze | solution.py:569
  28.3 0.4 collective-permute-start.1
  28.7 0.8 collective-permute-start.2
  29.5 2.2 %collective-permute-done.4.refs_5_ = bf16[128,1280]{1,0:T(8,128)(2,1)S(1)} collective-permute-done((bf16[128,1280]{1,0:T(8,128)(2,1)S(1)}, bf16[128,1280]{1,0:T(8,128)(2,1)S(1)}, u32[]{:S(2)}, u32[]{:S(2)}) %collective-permute-start.4) | collective-permute-done | bytes 327712 | tf_op jit(solution)/shard_map/ppermute | solution.py:544
  31.8 1.4 %collective-permute-start.3 = (bf16[320,256]{1,0:T(8,128)(2,1)S(1)}, bf16[320,256]{1,0:T(8,128)(2,1)}, u32[]{:S(2)}, u32[]{:S(2)}) collective-permute-start(bf16[320,256]{1,0:T(8,128)(2,1)S(1)} %get-tuple-element.79), channel_id=1, source_target_pairs={{0,96},{32,0},{64,32},{96,64},{1,97},{33,1},{65,33},{97,65},{2,98}... | collective-permute-start | bytes 491528 | tf_op jit(solution)/shard_map/ppermute | solution.py:544
  33.2 8.1 %all-to-all-done.recv = bf16[16,400,128]{2,1,0:T(8,128)(2,1)S(1)} async-done(((bf16[16,400,128]{2,1,0:T(8,128)(2,1)}), bf16[16,400,128]{2,1,0:T(8,128)(2,1)S(1)}, u32[]{:S(2)}, u32[]{:S(2)}) %all-to-all-start) | async-done | bytes 1638432 | tf_op jit(solution)/shard_map/all_to_all | solution.py:535
  41.3 1.2 copy-done
  42.5 10.2 %text_pairs.1 = (bf16[8,1184,128]{2,1,0:T(8,128)(2,1)}, f32[2048,128]{1,0:T(8,128)}, f32[64,2048]{1,0:T(8,128)}, f32[1024,128]{1,0:T(8,128)}, f32[64,1024]{1,0:T(8,128)}) custom-call(bf16[16,400,128]{2,1,0:T(8,128)(2,1)} %copy-done, bf16[384,128]{1,0:T(8,128)(2,1)} %get-tuple-element.44.wqg, bf16[384,128]{1,0:T(8,128)(2,1)} %get-tuple-element.45.wkv, ...), custom_call_target="tpu_custom_call" | custom-call | tf_op jit(solution)/shard_map/text_pairs/pallas_call | solution.py:374
  52.7 1.0 collective-permute-start.7
  53.7 0.1 collective-permute-start.8
  53.9 0.5 collective-permute-start.9
  54.3 0.1 collective-permute-start.10
  54.4 0.5 collective-permute-done.7.refs_8_
  55.0 0.5 collective-permute-done.8.refs_9_
  55.5 0.5 collective-permute-done.9.refs_10_
  55.9 0.5 collective-permute-done.10.refs_11_
  56.4 0.2 copy-done.9
  56.6 0.7 copy-done.10
  57.4 3.9 %weight.1 = bf16[8,1184,128]{2,1,0:T(8,128)(2,1)} custom-call(bf16[320,256]{1,0:T(8,128)(2,1)} %get-tuple-element.58.refs_0_, bf16[320,256]{1,0:T(8,128)(2,1)} %collective-permute-done.1.refs_1_, bf16[320,256]{1,0:T(8,128)(2,1)} %collective-permute-done.2.refs_2_, bf16[320,256]{1,0:T(8,128)(2,1)} %collective-permute-done.3.refs_3_, ...), custom_call_target="tpu_custom_call", output_to_operand_aliasing={{}: (12, {})} | custom-call | tf_op jit(solution)/shard_map/weight/pallas_call | solution.py:595
  61.3 3.8 %all-to-all-start.2 = ((bf16[8,1184,128]{2,1,0:T(8,128)(2,1)}), bf16[8,1184,128]{2,1,0:T(8,128)(2,1)S(1)}, u32[]{:S(2)}, u32[]{:S(2)}) async-start(bf16[8,1184,128]{2,1,0:T(8,128)(2,1)} %weight.1), calls=%async_computation.2 | async-start | bytes 4849664 | tf_op jit(solution)/shard_map/all_to_all | solution.py:535
  65.1 18.6 %image_pairs.1 = bf16[16,288,128]{2,1,0:T(8,128)(2,1)} custom-call(bf16[16,400,128]{2,1,0:T(8,128)(2,1)} %copy-done, f32[2048,128]{1,0:T(8,128)} %get-tuple-element.50.a, f32[64,2048]{1,0:T(8,128)} %get-tuple-element.51.b, f32[1024,128]{1,0:T(8,128)} %get-tuple-element.52.c, f32[64,1024]{1,0:T(8,128)} %get-tuple-element.53.d), custom_call_target="tpu_custom_call" | custom-call | tf_op jit(solution)/shard_map/image_pairs/pallas_call | solution.py:414
  83.7 12.9 %all-to-all-done.2.mine = bf16[8,1184,128]{2,1,0:T(8,128)(2,1)S(1)} async-done(((bf16[8,1184,128]{2,1,0:T(8,128)(2,1)}), bf16[8,1184,128]{2,1,0:T(8,128)(2,1)S(1)}, u32[]{:S(2)}, u32[]{:S(2)}) %all-to-all-start.2) | async-done | bytes 2424864 | tf_op jit(solution)/shard_map/all_to_all | solution.py:535
  96.5 1.2 collective-permute-start.11
  97.8 4.3 %all-to-all-start.1 = ((bf16[16,288,128]{2,1,0:T(8,128)(2,1)}), bf16[16,288,128]{2,1,0:T(8,128)(2,1)}, u32[]{:S(2)}, u32[]{:S(2)}) async-start(bf16[16,288,128]{2,1,0:T(8,128)(2,1)} %image_pairs.1), calls=%async_computation.1 | async-start | bytes 2359296 | tf_op jit(solution)/shard_map/all_to_all | solution.py:535
  102.1 0.1 slice_reduce_fusion
  102.2 1.4 %collective-permute-start.12 = (bf16[400,128]{1,0:T(8,128)(2,1)S(1)}, bf16[400,128]{1,0:T(8,128)(2,1)S(1)}, u32[]{:S(2)}, u32[]{:S(2)}) collective-permute-start(bf16[400,128]{1,0:T(8,128)(2,1)S(1)} %slice_reduce_fusion), channel_id=1, source_target_pairs={{0,32},{32,64},{64,96},{96,0},{1,33},{33,65},{65,97},{97,1},{2,34}... | collective-permute-start | bytes 307208 | tf_op jit(solution)/shard_map/ppermute | solution.py:544
  103.6 3.7 %collective-permute-start.13 = (bf16[400,128]{1,0:T(8,128)(2,1)S(1)}, bf16[400,128]{1,0:T(8,128)(2,1)S(1)}, u32[]{:S(2)}, u32[]{:S(2)}) collective-permute-start(bf16[400,128]{1,0:T(8,128)(2,1)S(1)} %slice_reduce_fusion), channel_id=1, source_target_pairs={{0,64},{32,96},{64,0},{96,32},{1,65},{33,97},{65,1},{97,33},{2,66}... | collective-permute-start | bytes 307208 | tf_op jit(solution)/shard_map/ppermute | solution.py:544
  107.2 0.4 collective-permute-start.14
  107.7 1.6 %collective-permute-done.12 = bf16[400,128]{1,0:T(8,128)(2,1)S(1)} collective-permute-done((bf16[400,128]{1,0:T(8,128)(2,1)S(1)}, bf16[400,128]{1,0:T(8,128)(2,1)S(1)}, u32[]{:S(2)}, u32[]{:S(2)}) %collective-permute-start.12) | collective-permute-done | bytes 102432 | tf_op jit(solution)/shard_map/ppermute | solution.py:544
  109.3 3.2 %collective-permute-done.13 = bf16[400,128]{1,0:T(8,128)(2,1)S(1)} collective-permute-done((bf16[400,128]{1,0:T(8,128)(2,1)S(1)}, bf16[400,128]{1,0:T(8,128)(2,1)S(1)}, u32[]{:S(2)}, u32[]{:S(2)}) %collective-permute-start.13) | collective-permute-done | bytes 102432 | tf_op jit(solution)/shard_map/ppermute | solution.py:544
  112.6 0.4 collective-permute-start.15
  112.9 5.1 %unpack_text.1 = (bf16[333,1280]{1,0:T(8,128)(2,1)}, bf16[333,1280]{1,0:T(8,128)(2,1)}, bf16[333,1280]{1,0:T(8,128)(2,1)}) custom-call(s32[1]{0:T(128)} %bitcast.13.core, bf16[8,1184,128]{2,1,0:T(8,128)(2,1)} %copy-done.1, bf16[8,1184,128]{2,1,0:T(8,128)(2,1)} %collective-permute-done.11.other), custom_call_target="tpu_custom_call" | custom-call | tf_op jit(solution)/shard_map/unpack_text/pallas_call | solution.py:524
  118.1 2.7 %all-to-all-done.1.recv = bf16[16,288,128]{2,1,0:T(8,128)(2,1)} async-done(((bf16[16,288,128]{2,1,0:T(8,128)(2,1)}), bf16[16,288,128]{2,1,0:T(8,128)(2,1)}, u32[]{:S(2)}, u32[]{:S(2)}) %all-to-all-start.1) | async-done | bytes 1179680 | tf_op jit(solution)/shard_map/all_to_all | solution.py:535
  120.7 2.6 %unpack.1 = (bf16[128,1280]{1,0:T(8,128)(2,1)}, bf16[128,1280]{1,0:T(8,128)(2,1)}, bf16[128,1280]{1,0:T(8,128)(2,1)}) custom-call(bf16[16,288,128]{2,1,0:T(8,128)(2,1)} %all-to-all-done.1.recv), custom_call_target="tpu_custom_call" | custom-call | tf_op jit(solution)/shard_map/unpack/pallas_call | solution.py:470
  123.3 1.5 %collective-permute-done.15 = bf16[4,400,128]{2,1,0:T(8,128)(2,1)S(1)} collective-permute-done((bf16[4,400,128]{2,1,0:T(8,128)(2,1)S(1)}, bf16[4,400,128]{2,1,0:T(8,128)(2,1)S(1)}, u32[]{:S(2)}, u32[]{:S(2)}) %collective-permute-start.15) | collective-permute-done | bytes 409632 | tf_op jit(solution)/shard_map/ppermute | solution.py:544
  124.9 0.1 convert_add_fusion
  124.9 0.2 copy.26
  125.2 0.3 copy.29
  125.5 0.9 slice.8
  (34 shorter events, 0.3 us)
Async XLA Ops:
  8.4 32.8 %all-to-all-start = ((bf16[16,400,128]{2,1,0:T(8,128)(2,1)}), bf16[16,400,128]{2,1,0:T(8,128)(2,1)S(1)}, u32[]{:S(2)}, u32[]{:S(2)}) async-start(bf16[16,400,128]{2,1,0:T(8,128)(2,1)} %pack.1), calls=%async_computation | async-start | bytes 3276800 | tf_op jit(solution)/shard_map/all_to_all | solution.py:535
  17.7 2.4 %copy-start.2 = (bf16[1,128,2432]{2,1,0:T(8,128)(2,1)S(1)}, bf16[1,128,2432]{2,1,0:T(8,128)(2,1)}, u32[]{:S(2)}) copy-start(bf16[1,128,2432]{2,1,0:T(8,128)(2,1)} %param.17) | copy-start | bytes 1867780
  20.2 1.4 %copy-start.3 = (bf16[1,128,1280]{2,1,0:T(8,128)(2,1)S(1)}, bf16[1,128,1280]{2,1,0:T(8,128)(2,1)}, u32[]{:S(2)}) copy-start(bf16[1,128,1280]{2,1,0:T(8,128)(2,1)} %param.16) | copy-start | bytes 983044
  21.4 5.1 %collective-permute-start = (bf16[4,320,128]{2,1,0:T(8,128)(2,1)}, bf16[4,320,128]{2,1,0:T(8,128)(2,1)}, u32[]{:S(2)}, u32[]{:S(2)}) collective-permute-start(bf16[4,320,128]{2,1,0:T(8,128)(2,1)} %get-tuple-element.83), channel_id=1, source_target_pairs={{0,1},{1,0},{2,3},{3,2},{4,5},{5,4},{6,7},{7,6},{8,9},{9,8},{10,11... | collective-permute-start | bytes 983048 | tf_op jit(solution)/shard_map/ppermute | solution.py:539
  21.5 10.2 %collective-permute-start.4 = (bf16[128,1280]{1,0:T(8,128)(2,1)S(1)}, bf16[128,1280]{1,0:T(8,128)(2,1)S(1)}, u32[]{:S(2)}, u32[]{:S(2)}) collective-permute-start(bf16[128,1280]{1,0:T(8,128)(2,1)S(1)} %bitcast.74), channel_id=1, source_target_pairs={{0,32},{32,64},{64,96},{96,0},{1,33},{33,65},{65,97},{97,1},{2,34}... | collective-permute-start | bytes 983048 | tf_op jit(solution)/shard_map/ppermute | solution.py:544
  22.8 29.9 %collective-permute-start.5 = (bf16[128,1280]{1,0:T(8,128)(2,1)S(1)}, bf16[128,1280]{1,0:T(8,128)(2,1)S(1)}, u32[]{:S(2)}, u32[]{:S(2)}) collective-permute-start(bf16[128,1280]{1,0:T(8,128)(2,1)S(1)} %bitcast.75), channel_id=1, source_target_pairs={{0,64},{32,96},{64,0},{96,32},{1,65},{33,97},{65,1},{97,33},{2,66}... | collective-permute-start | bytes 983048 | tf_op jit(solution)/shard_map/ppermute | solution.py:544
  25.5 28.3 %collective-permute-start.6 = (bf16[128,1280]{1,0:T(8,128)(2,1)S(1)}, bf16[128,1280]{1,0:T(8,128)(2,1)S(1)}, u32[]{:S(2)}, u32[]{:S(2)}) collective-permute-start(bf16[128,1280]{1,0:T(8,128)(2,1)S(1)} %bitcast.76), channel_id=1, source_target_pairs={{0,96},{32,0},{64,32},{96,64},{1,97},{33,1},{65,33},{97,65},{2,98}... | collective-permute-start | bytes 983048 | tf_op jit(solution)/shard_map/ppermute | solution.py:544
  28.3 25.4 %collective-permute-start.1 = (bf16[320,256]{1,0:T(8,128)(2,1)}, bf16[320,256]{1,0:T(8,128)(2,1)}, u32[]{:S(2)}, u32[]{:S(2)}) collective-permute-start(bf16[320,256]{1,0:T(8,128)(2,1)} %get-tuple-element.81), channel_id=1, source_target_pairs={{0,32},{32,64},{64,96},{96,0},{1,33},{33,65},{65,97},{97,1},{2,34}... | collective-permute-start | bytes 491528 | tf_op jit(solution)/shard_map/ppermute | solution.py:544
  28.7 25.0 %collective-permute-start.2 = (bf16[320,256]{1,0:T(8,128)(2,1)}, bf16[320,256]{1,0:T(8,128)(2,1)}, u32[]{:S(2)}, u32[]{:S(2)}) collective-permute-start(bf16[320,256]{1,0:T(8,128)(2,1)} %get-tuple-element.82), channel_id=1, source_target_pairs={{0,64},{32,96},{64,0},{96,32},{1,65},{33,97},{65,1},{97,33},{2,66}... | collective-permute-start | bytes 491528 | tf_op jit(solution)/shard_map/ppermute | solution.py:544
  31.8 24.6 %copy-start.4 = (bf16[128,1280]{1,0:T(8,128)(2,1)}, bf16[128,1280]{1,0:T(8,128)(2,1)S(1)}, u32[]{:S(2)}) copy-start(bf16[128,1280]{1,0:T(8,128)(2,1)S(1)} %collective-permute-done.4.refs_5_) | copy-start | bytes 983044
  31.8 22.0 %collective-permute-start.3 = (bf16[320,256]{1,0:T(8,128)(2,1)S(1)}, bf16[320,256]{1,0:T(8,128)(2,1)}, u32[]{:S(2)}, u32[]{:S(2)}) collective-permute-start(bf16[320,256]{1,0:T(8,128)(2,1)S(1)} %get-tuple-element.79), channel_id=1, source_target_pairs={{0,96},{32,0},{64,32},{96,64},{1,97},{33,1},{65,33},{97,65},{2,98}... | collective-permute-start | bytes 491528 | tf_op jit(solution)/shard_map/ppermute | solution.py:544
  41.3 1.2 copy-start
  52.7 3.7 %copy-start.5 = (bf16[128,1280]{1,0:T(8,128)(2,1)}, bf16[128,1280]{1,0:T(8,128)(2,1)S(1)}, u32[]{:S(2)}) copy-start(bf16[128,1280]{1,0:T(8,128)(2,1)S(1)} %collective-permute-done.5.refs_6_) | copy-start | bytes 983044
  52.7 2.3 %collective-permute-start.7 = (bf16[128,1280]{1,0:T(8,128)(2,1)S(1)}, bf16[128,1280]{1,0:T(8,128)(2,1)S(1)}, u32[]{:S(2)}, u32[]{:S(2)}) collective-permute-start(bf16[128,1280]{1,0:T(8,128)(2,1)S(1)} %bitcast.77), channel_id=1, source_target_pairs={{0,1},{1,0},{2,3},{3,2},{4,5},{5,4},{6,7},{7,6},{8,9},{9,8},{10,11... | collective-permute-start | bytes 983048 | tf_op jit(solution)/shard_map/ppermute | solution.py:539
  53.7 2.7 %copy-start.6 = (bf16[128,1280]{1,0:T(8,128)(2,1)}, bf16[128,1280]{1,0:T(8,128)(2,1)S(1)}, u32[]{:S(2)}) copy-start(bf16[128,1280]{1,0:T(8,128)(2,1)S(1)} %collective-permute-done.6.refs_7_) | copy-start | bytes 983044
  53.7 1.7 %collective-permute-start.8 = (bf16[128,1280]{1,0:T(8,128)(2,1)S(1)}, bf16[128,1280]{1,0:T(8,128)(2,1)S(1)}, u32[]{:S(2)}, u32[]{:S(2)}) collective-permute-start(bf16[128,1280]{1,0:T(8,128)(2,1)S(1)} %collective-permute-done.4.refs_5_), channel_id=1, source_target_pairs={{0,1},{1,0},{2,3},{3,2},{4,5},{5,4},{6,7},{7,6},{8,9},{9,8},{10,11... | collective-permute-start | bytes 983048 | tf_op jit(solution)/shard_map/ppermute | solution.py:539
  53.9 2.1 %collective-permute-start.9 = (bf16[128,1280]{1,0:T(8,128)(2,1)S(1)}, bf16[128,1280]{1,0:T(8,128)(2,1)S(1)}, u32[]{:S(2)}, u32[]{:S(2)}) collective-permute-start(bf16[128,1280]{1,0:T(8,128)(2,1)S(1)} %collective-permute-done.5.refs_6_), channel_id=1, source_target_pairs={{0,1},{1,0},{2,3},{3,2},{4,5},{5,4},{6,7},{7,6},{8,9},{9,8},{10,11... | collective-permute-start | bytes 983048 | tf_op jit(solution)/shard_map/ppermute | solution.py:539
  54.3 2.1 %collective-permute-start.10 = (bf16[128,1280]{1,0:T(8,128)(2,1)S(1)}, bf16[128,1280]{1,0:T(8,128)(2,1)S(1)}, u32[]{:S(2)}, u32[]{:S(2)}) collective-permute-start(bf16[128,1280]{1,0:T(8,128)(2,1)S(1)} %collective-permute-done.6.refs_7_), channel_id=1, source_target_pairs={{0,1},{1,0},{2,3},{3,2},{4,5},{5,4},{6,7},{7,6},{8,9},{9,8},{10,11... | collective-permute-start | bytes 983048 | tf_op jit(solution)/shard_map/ppermute | solution.py:539
  55.0 1.4 %copy-start.7 = (bf16[128,1280]{1,0:T(8,128)(2,1)}, bf16[128,1280]{1,0:T(8,128)(2,1)S(1)}, u32[]{:S(2)}) copy-start(bf16[128,1280]{1,0:T(8,128)(2,1)S(1)} %collective-permute-done.7.refs_8_) | copy-start | bytes 983044
  55.5 1.0 copy-start.8
  55.9 0.7 copy-start.9
  56.6 0.7 copy-start.10
  61.3 35.3 %all-to-all-start.2 = ((bf16[8,1184,128]{2,1,0:T(8,128)(2,1)}), bf16[8,1184,128]{2,1,0:T(8,128)(2,1)S(1)}, u32[]{:S(2)}, u32[]{:S(2)}) async-start(bf16[8,1184,128]{2,1,0:T(8,128)(2,1)} %weight.1), calls=%async_computation.2 | async-start | bytes 4849664 | tf_op jit(solution)/shard_map/all_to_all | solution.py:535
  96.5 16.4 %copy-start.1 = (bf16[8,1184,128]{2,1,0:T(8,128)(2,1)}, bf16[8,1184,128]{2,1,0:T(8,128)(2,1)S(1)}, u32[]{:S(2)}) copy-start(bf16[8,1184,128]{2,1,0:T(8,128)(2,1)S(1)} %all-to-all-done.2.mine) | copy-start | bytes 7274500
  96.5 16.4 %collective-permute-start.11 = (bf16[8,1184,128]{2,1,0:T(8,128)(2,1)S(1)}, bf16[8,1184,128]{2,1,0:T(8,128)(2,1)}, u32[]{:S(2)}, u32[]{:S(2)}) collective-permute-start(bf16[8,1184,128]{2,1,0:T(8,128)(2,1)S(1)} %all-to-all-done.2.mine), channel_id=1, source_target_pairs={{0,1},{1,0},{2,3},{3,2},{4,5},{5,4},{6,7},{7,6},{8,9},{9,8},{10,11... | collective-permute-start | bytes 7274504 | tf_op jit(solution)/shard_map/ppermute | solution.py:539
  97.8 23.0 %all-to-all-start.1 = ((bf16[16,288,128]{2,1,0:T(8,128)(2,1)}), bf16[16,288,128]{2,1,0:T(8,128)(2,1)}, u32[]{:S(2)}, u32[]{:S(2)}) async-start(bf16[16,288,128]{2,1,0:T(8,128)(2,1)} %image_pairs.1), calls=%async_computation.1 | async-start | bytes 2359296 | tf_op jit(solution)/shard_map/all_to_all | solution.py:535
  102.2 7.1 %collective-permute-start.12 = (bf16[400,128]{1,0:T(8,128)(2,1)S(1)}, bf16[400,128]{1,0:T(8,128)(2,1)S(1)}, u32[]{:S(2)}, u32[]{:S(2)}) collective-permute-start(bf16[400,128]{1,0:T(8,128)(2,1)S(1)} %slice_reduce_fusion), channel_id=1, source_target_pairs={{0,32},{32,64},{64,96},{96,0},{1,33},{33,65},{65,97},{97,1},{2,34}... | collective-permute-start | bytes 307208 | tf_op jit(solution)/shard_map/ppermute | solution.py:544
  103.6 8.9 %collective-permute-start.13 = (bf16[400,128]{1,0:T(8,128)(2,1)S(1)}, bf16[400,128]{1,0:T(8,128)(2,1)S(1)}, u32[]{:S(2)}, u32[]{:S(2)}) collective-permute-start(bf16[400,128]{1,0:T(8,128)(2,1)S(1)} %slice_reduce_fusion), channel_id=1, source_target_pairs={{0,64},{32,96},{64,0},{96,32},{1,65},{33,97},{65,1},{97,33},{2,66}... | collective-permute-start | bytes 307208 | tf_op jit(solution)/shard_map/ppermute | solution.py:544
  107.2 5.3 %collective-permute-start.14 = (bf16[400,128]{1,0:T(8,128)(2,1)S(1)}, bf16[400,128]{1,0:T(8,128)(2,1)S(1)}, u32[]{:S(2)}, u32[]{:S(2)}) collective-permute-start(bf16[400,128]{1,0:T(8,128)(2,1)S(1)} %slice_reduce_fusion), channel_id=1, source_target_pairs={{0,96},{32,0},{64,32},{96,64},{1,97},{33,1},{65,33},{97,65},{2,98}... | collective-permute-start | bytes 307208 | tf_op jit(solution)/shard_map/ppermute | solution.py:544
  112.6 12.3 %collective-permute-start.15 = (bf16[4,400,128]{2,1,0:T(8,128)(2,1)S(1)}, bf16[4,400,128]{2,1,0:T(8,128)(2,1)S(1)}, u32[]{:S(2)}, u32[]{:S(2)}) collective-permute-start(bf16[4,400,128]{2,1,0:T(8,128)(2,1)S(1)} %bitcast_dynamic-update-slice_fusion), channel_id=1, source_target_pairs={{0,16},{16,0},{1,17},{17,1},{2,18},{18,2},{3,19},{19,3},{4,20},{20... | collective-permute-start | bytes 1228808 | tf_op jit(solution)/shard_map/ppermute | solution.py:544

commit v6 on v5

--- a/solution.py
+++ b/solution.py
@@ -80,74 +80,82 @@
     return tile
 
 
-def pack_kernel(index, og, w, q, k, v, o, l, send):
-    j = pl.program_id(0)
-    g = dot(og[...], w[...]).astype(BF).astype(F32)
-    qf, kf, vf = q[...].astype(F32), k[...].astype(F32), v[...].astype(F32)
-    delta = picked_sum(
-        jnp.where(iota((8, 256), 1) // 64 == iota((8, 256), 0), 1.0, 0.0),
-        g * o[...].astype(F32),
-    )
-    lsum = picked_rows(
-        jnp.where(iota((8, 20), 1) == 4 * j + iota((8, 20), 0), 1.0, 0.0), l[:, 0, :]
-    )
+def pack_kernel(
+    index, og_hbm, w_hbm, q_hbm, k_hbm, v_hbm, o_hbm, l, send, og, w, q, k, v, o, acc, sems
+):
+    depth = w.shape[0]
+    chunk = 640
+    parts = [(at, min(chunk, depth - at)) for at in range(0, depth, chunk)]
+    copies = [
+        pltpu.make_async_copy(source, target, sems.at[n])
+        for n, (source, target) in enumerate(
+            [(k_hbm, k), (v_hbm, v), (og_hbm, og)]
+            + [(w_hbm.at[pl.ds(at, size)], w.at[pl.ds(at, size)]) for at, size in parts]
+            + [(q_hbm, q), (o_hbm, o)]
+        )
+    ]
+    for copy in copies:
+        copy.start()
     low = iota((TOK, 128), 1) < 64
 
-    def packed(a, b, r):
-        t = 128 * (r // 2)
-        a, b = a[:, t : t + 128], b[:, t : t + 128]
-        if r % 2 == 0:
+    def packed(a, b, head):
+        lanes = slice(128 * (head // 2), 128 * (head // 2) + 128)
+        a, b = a[:, lanes].astype(F32), b[:, lanes].astype(F32)
+        if head % 2 == 0:
             return jnp.where(low, a, swap_halves(b)).astype(BF)
         return jnp.where(low, swap_halves(a), b).astype(BF)
 
-    @pl.when(j < 4)
-    def whole():
-        for r in range(4):
-            d = 4 * j + r
-            send[d, 0:128, :] = packed(qf, g, r)
-            send[d, 128:256, :] = packed(kf, vf, r)
-            send[d, 384:400, :] = stat_rows(lsum, delta, 0, r).astype(BF)
-
-    @pl.when(j == 4)
-    def shared():
-        parity = index[0] % 2
-        here = iota((16, 128), 1) // 64 == parity
-        for r in range(4):
-            qg, kv = packed(qf, g, r), packed(kf, vf, r)
-            stat = stat_rows(lsum, delta, 4, r)
-            moved = swap_halves(stat)
-            for qi in range(2):
-                mine = jnp.where(here, jnp.where(parity == qi, stat, moved), 0.0)
-                for ki in range(2):
-                    d = 4 * r + 2 * qi + ki
-                    send[d, 256:320, :] = qg[64 * qi : 64 * qi + 64]
-                    send[d, 320:384, :] = kv[64 * ki : 64 * ki + 64]
-                    send[d, 384:400, :] = (send[d, 384:400, :].astype(F32) + mine).astype(BF)
+    copies[0].wait()
+    copies[1].wait()
+    for d in range(N):
+        send[d, 128:256, :] = packed(k, v, d)
+    for r in range(4):
+        kv = packed(k, v, 16 + r)
+        for qi in range(2):
+            for ki in range(2):
+                send[4 * r + 2 * qi + ki, 320:384, :] = kv[64 * ki : 64 * ki + 64]
+
+    copies[2].wait()
+    for n, (at, size) in enumerate(parts):
+        copies[3 + n].wait()
+        term = dot(og[:, at : at + size], w[at : at + size, :])
+        acc[...] = term if n == 0 else acc[...] + term
+    copies[-2].wait()
+    copies[-1].wait()
+    acc[...] = acc[...].astype(BF).astype(F32)
+    delta = picked_sum(
+        jnp.where(iota((24, 1280), 1) // 64 == iota((24, 1280), 0), 1.0, 0.0),
+        acc[...] * o[...].astype(F32),
+    )
+    lsum = l[:, 0, :]
+    here = iota((16, 128), 1) // 64 == index[0] % 2
+    for r in range(4):
+        qg = packed(q, acc, 16 + r)
+        stat = stat_rows(lsum, delta, 4, 16 + r)
+        moved = swap_halves(stat)
+        for qi in range(2):
+            mine = jnp.where(here, jnp.where(index[0] % 2 == qi, stat, moved), 0.0)
+            for ki in range(2):
+                d = 4 * r + 2 * qi + ki
+                send[d, 0:128, :] = packed(q, acc, d)
+                send[d, 256:320, :] = qg[64 * qi : 64 * qi + 64]
+                send[d, 384:400, :] = (stat_rows(lsum, delta, 0, d) + mine).astype(BF)
 
 
 def pack(index, og, w, q, k, v, o, l):
-    depth = og.shape[1]
-    column = pl.BlockSpec((TOK, 256), lambda j, s: (0, j))
+    anywhere = pl.BlockSpec(memory_space=pl.ANY)
+    full = pl.BlockSpec(memory_space=pltpu.VMEM)
+    arrays = [og, w, q, k, v, o]
     return pl.pallas_call(
         pack_kernel,
-        grid_spec=pltpu.PrefetchScalarGridSpec(
-            num_scalar_prefetch=1,
-            grid=(5,),
-            in_specs=[
-                pl.BlockSpec((TOK, depth), lambda j, s: (0, 0)),
-                pl.BlockSpec((depth, 256), lambda j, s: (0, j)),
-                column,
-                column,
-                column,
-                column,
-                pl.BlockSpec((20, 1, TOK), lambda j, s: (0, 0, 0)),
-            ],
-            out_specs=pl.BlockSpec((N, MSG, 128), lambda j, s: (0, 0, 0)),
-        ),
+        in_specs=[pl.BlockSpec(memory_space=pltpu.SMEM)] + [anywhere] * 6 + [full],
+        out_specs=full,
         out_shape=jax.ShapeDtypeStruct((N, MSG, 128), BF),
+        scratch_shapes=[pltpu.VMEM(x.shape, BF) for x in arrays]
+        + [pltpu.VMEM(q.shape, F32), pltpu.SemaphoreType.DMA((5 + -(-w.shape[0] // 640),))],
         compiler_params=pltpu.CompilerParams(vmem_limit_bytes=VMEM_LIMIT),
         name="pack",
-    )(index, og, w, q, k, v, o, l)
+    )(index, *arrays, l)
 
 
 def text_kernel(
@@ -329,12 +337,12 @@
     w.block(S, TXT_K, S, TXT_Q)
 
     def whole_text(n, _):
-        at = pl.multiple_of(n * 1024, 1024)
-        w.block(at, 1024, S, TXT_Q)
-        w.block(S, TXT_K, at, 1024)
+        at = pl.multiple_of(n * 2048, 2048)
+        w.block(at, 2048, S, TXT_Q)
+        w.block(S, TXT_K, at, 2048)
         return 0
 
-    lax.fori_loop(0, S // 1024, whole_text, 0)
+    lax.fori_loop(0, S // 2048, whole_text, 0)
     h.block(SH, HALF, SH, HALF_Q)
     h.block(0, SH, SH, HALF_Q)
     h.block(SH, HALF, 0, SH)

time: 128 us -> 125 us (0.977)
  Pallas kernels: 50.6 us -> 47.8 us
    pallas_call x1, Pallas kernels: 7.79 us -> 6.24 us  [pack(): pl.pallas_call(pack_kernel, in_specs=[pl.BlockSpec(memory_space=pltpu.SME...]
    pallas_call x1, Pallas kernels: 10.2 us -> 8.95 us  [text_pairs(): pl.pallas_call(text_pairs_kernel, in_specs=[full] * 7, out_specs=[full] *...]
  transfers between devices with their start and end apart: 19 -> 19, of which waited for: 11 -> 11; matrix products, arithmetic and copies ran while one was open for 3% -> 3% of each run, Pallas kernels for 31% -> 30%
where the time goes in v6:
time: 125 us; the launch traced here: 124 us
  Pallas kernels  47.8 us (38%)
  waiting for transfers between devices  34.6 us (28%)
  starting transfers between devices  33.6 us (27%)
  local copies, waits for them, and re-layouts  4.94 us (4%)
  other arithmetic  1.99 us (2%)
    all_to_all x3, waiting for transfers between devices, exchange(): return lax.all_to_all(x, axes, 0, 0, tiled=True)  24 us
    pallas_call x1, Pallas kernels, image_pairs(): pl.pallas_call(image_pairs_kernel, in_specs=[full] * 5, out_specs=full, o...  18.6 us
    all_to_all x3, starting transfers between devices, exchange(): return lax.all_to_all(x, axes, 0, 0, tiled=True)  17.2 us
    ppermute x10, starting transfers between devices, shifted(): return lax.ppermute(x, axis, [(i, (i + by) % size) for i in range(size)])  13.4 us
    pallas_call x1, Pallas kernels, text_pairs(): pl.pallas_call(text_pairs_kernel, in_specs=[full] * 7, out_specs=[full] *...  8.95 us
    ppermute x10, waiting for transfers between devices, shifted(): return lax.ppermute(x, axis, [(i, (i + by) % size) for i in range(size)])  8.61 us
    pallas_call x1, Pallas kernels, pack(): pl.pallas_call(pack_kernel, in_specs=[pl.BlockSpec(memory_space=pltpu.SME...  6.24 us
    pallas_call x1, Pallas kernels, unpack_text(): pl.pallas_call(unpack_text_kernel, in_specs=[pl.BlockSpec(memory_space=pl...  5.11 us
  transfers between devices with their start and end apart: 19, of which 11 were waited for; matrix products, arithmetic and copies ran while one was open for 3% of the time, Pallas kernels for 30%

profile of v6, /device:TPU:1, one launch (start us, length us, event | category | flops | bytes accessed | tf_op | source)
XLA Modules:
  0.0 123.8 jit_solution(17447064535437671713)
XLA Ops:
  0.6 6.2 %pack.1 = bf16[16,400,128]{2,1,0:T(8,128)(2,1)} custom-call(s32[1]{0:T(128)} %bitcast.index, bf16[128,2432]{1,0:T(8,128)(2,1)} %bitcast.69, bf16[2432,1280]{1,0:T(8,128)(2,1)} %w_hbm.1, bf16[128,1280]{1,0:T(8,128)(2,1)} %bitcast.78, bf16[128,1280]{1,0:T(8,128)(2,1)} %bitcast.79, bf16[128,1280]{1,0:T(8,128)(2,1)} %bitcast.80, bf16[128,1280]{1,0:T(8,128)(2,1)} %bitcast.72, ...), custom_call_target="tpu_custom_call" | custom-call | tf_op jit(solution)/shard_map/pack/pallas_call | solution.py:149
  6.9 9.3 %all-to-all-start = ((bf16[16,400,128]{2,1,0:T(8,128)(2,1)}), bf16[16,400,128]{2,1,0:T(8,128)(2,1)S(1)}, u32[]{:S(2)}, u32[]{:S(2)}) async-start(bf16[16,400,128]{2,1,0:T(8,128)(2,1)} %pack.1), calls=%async_computation | async-start | bytes 3276800 | tf_op jit(solution)/shard_map/all_to_all | solution.py:543
  16.2 2.4 %text_prep.1 = (bf16[384,128]{1,0:T(8,128)(2,1)}, bf16[384,128]{1,0:T(8,128)(2,1)}, bf16[16,384]{1,0:T(8,128)(2,1)}, bf16[256,128]{1,0:T(8,128)(2,1)}, bf16[256,...) custom-call(s32[1]{0:T(128)} %bitcast.index, bf16[333,1280]{1,0:T(8,128)(2,1)} %bitcast.55, bf16[333,1280]{1,0:T(8,128)(2,1)} %bitcast.57, ...), custom_call_target="tpu_custom_call" | custom-call | tf_op jit(solution)/shard_map/text_prep/pallas_call | solution.py:219
  18.7 0.3 copy.24
  19.1 0.8 dynamic-slice_bitcast_fusion
  19.9 0.1 collective-permute-start
  20.0 1.3 %collective-permute-start.4 = (bf16[128,1280]{1,0:T(8,128)(2,1)S(1)}, bf16[128,1280]{1,0:T(8,128)(2,1)S(1)}, u32[]{:S(2)}, u32[]{:S(2)}) collective-permute-start(bf16[128,1280]{1,0:T(8,128)(2,1)S(1)} %bitcast.74), channel_id=1, source_target_pairs={{0,32},{32,64},{64,96},{96,0},{1,33},{33,65},{65,97},{97,1},{2,34}... | collective-permute-start | bytes 983048 | tf_op jit(solution)/shard_map/ppermute | solution.py:552
  21.3 2.6 %collective-permute-start.5 = (bf16[128,1280]{1,0:T(8,128)(2,1)S(1)}, bf16[128,1280]{1,0:T(8,128)(2,1)S(1)}, u32[]{:S(2)}, u32[]{:S(2)}) collective-permute-start(bf16[128,1280]{1,0:T(8,128)(2,1)S(1)} %bitcast.75), channel_id=1, source_target_pairs={{0,64},{32,96},{64,0},{96,32},{1,65},{33,97},{65,1},{97,33},{2,66}... | collective-permute-start | bytes 983048 | tf_op jit(solution)/shard_map/ppermute | solution.py:552
  23.9 1.1 collective-permute-start.6
  25.0 1.8 %fusion.1 = (bf16[320,256]{1,0:T(8,128)(2,1)S(1)}, bf16[320,256]{1,0:T(8,128)(2,1)}, bf16[320,256]{1,0:T(8,128)(2,1)}, bf16[320,256]{1,0:T(8,128)(2,1)}) fusion(s32[]{:T(128)S(6)} %select_n.73, bf16[4,320,128]{2,1,0:T(8,128)(2,1)S(1)} %get-tuple-element.84, bf16[4,320,128]{2,1,0:T(8,128)(2,1)} %collective-permute-done, s32[]{:T(128)S(6)} %select_n.67, ...), kind=kLoop, calls=%fused_computation.14 | loop fusion | flops 1310720 | bytes 1310736 | tf_op jit(solution)/shard_map/jit(dynamic_index_in_dim)/squeeze | solution.py:577
  26.8 0.4 collective-permute-start.1
  27.2 0.8 collective-permute-start.2
  28.0 2.2 %collective-permute-done.4.refs_5_ = bf16[128,1280]{1,0:T(8,128)(2,1)S(1)} collective-permute-done((bf16[128,1280]{1,0:T(8,128)(2,1)S(1)}, bf16[128,1280]{1,0:T(8,128)(2,1)S(1)}, u32[]{:S(2)}, u32[]{:S(2)}) %collective-permute-start.4) | collective-permute-done | bytes 327712 | tf_op jit(solution)/shard_map/ppermute | solution.py:552
  30.2 1.4 %collective-permute-start.3 = (bf16[320,256]{1,0:T(8,128)(2,1)S(1)}, bf16[320,256]{1,0:T(8,128)(2,1)}, u32[]{:S(2)}, u32[]{:S(2)}) collective-permute-start(bf16[320,256]{1,0:T(8,128)(2,1)S(1)} %get-tuple-element.79), channel_id=1, source_target_pairs={{0,96},{32,0},{64,32},{96,64},{1,97},{33,1},{65,33},{97,65},{2,98}... | collective-permute-start | bytes 491528 | tf_op jit(solution)/shard_map/ppermute | solution.py:552
  31.6 8.1 %all-to-all-done.recv = bf16[16,400,128]{2,1,0:T(8,128)(2,1)S(1)} async-done(((bf16[16,400,128]{2,1,0:T(8,128)(2,1)}), bf16[16,400,128]{2,1,0:T(8,128)(2,1)S(1)}, u32[]{:S(2)}, u32[]{:S(2)}) %all-to-all-start) | async-done | bytes 1638432 | tf_op jit(solution)/shard_map/all_to_all | solution.py:543
  39.8 1.2 copy-done
  40.9 9.0 %text_pairs.1 = (bf16[8,1184,128]{2,1,0:T(8,128)(2,1)}, f32[2048,128]{1,0:T(8,128)}, f32[64,2048]{1,0:T(8,128)}, f32[1024,128]{1,0:T(8,128)}, f32[64,1024]{1,0:T(8,128)}) custom-call(bf16[16,400,128]{2,1,0:T(8,128)(2,1)} %copy-done, bf16[384,128]{1,0:T(8,128)(2,1)} %get-tuple-element.44.wqg, bf16[384,128]{1,0:T(8,128)(2,1)} %get-tuple-element.45.wkv, ...), custom_call_target="tpu_custom_call" | custom-call | tf_op jit(solution)/shard_map/text_pairs/pallas_call | solution.py:382
  49.9 1.0 collective-permute-start.7
  50.9 0.3 collective-permute-start.8
  51.2 0.5 collective-permute-start.9
  51.7 0.1 collective-permute-start.10
  51.8 0.4 collective-permute-done.7.refs_8_
  52.2 0.7 collective-permute-done.8.refs_9_
  52.8 0.5 collective-permute-done.9.refs_10_
  53.3 0.5 collective-permute-done.10.refs_11_
  53.8 0.2 copy-done.9
  54.0 0.7 copy-done.10
  54.8 3.9 %weight.1 = bf16[8,1184,128]{2,1,0:T(8,128)(2,1)} custom-call(bf16[320,256]{1,0:T(8,128)(2,1)} %get-tuple-element.58.refs_0_, bf16[320,256]{1,0:T(8,128)(2,1)} %collective-permute-done.1.refs_1_, bf16[320,256]{1,0:T(8,128)(2,1)} %collective-permute-done.2.refs_2_, bf16[320,256]{1,0:T(8,128)(2,1)} %collective-permute-done.3.refs_3_, ...), custom_call_target="tpu_custom_call", output_to_operand_aliasing={{}: (12, {})} | custom-call | tf_op jit(solution)/shard_map/weight/pallas_call | solution.py:603
  58.6 3.6 %all-to-all-start.2 = ((bf16[8,1184,128]{2,1,0:T(8,128)(2,1)}), bf16[8,1184,128]{2,1,0:T(8,128)(2,1)S(1)}, u32[]{:S(2)}, u32[]{:S(2)}) async-start(bf16[8,1184,128]{2,1,0:T(8,128)(2,1)} %weight.1), calls=%async_computation.2 | async-start | bytes 4849664 | tf_op jit(solution)/shard_map/all_to_all | solution.py:543
  62.2 18.6 %image_pairs.1 = bf16[16,288,128]{2,1,0:T(8,128)(2,1)} custom-call(bf16[16,400,128]{2,1,0:T(8,128)(2,1)} %copy-done, f32[2048,128]{1,0:T(8,128)} %get-tuple-element.50.a, f32[64,2048]{1,0:T(8,128)} %get-tuple-element.51.b, f32[1024,128]{1,0:T(8,128)} %get-tuple-element.52.c, f32[64,1024]{1,0:T(8,128)} %get-tuple-element.53.d), custom_call_target="tpu_custom_call" | custom-call | tf_op jit(solution)/shard_map/image_pairs/pallas_call | solution.py:422
  80.9 13.3 %all-to-all-done.2.mine = bf16[8,1184,128]{2,1,0:T(8,128)(2,1)S(1)} async-done(((bf16[8,1184,128]{2,1,0:T(8,128)(2,1)}), bf16[8,1184,128]{2,1,0:T(8,128)(2,1)S(1)}, u32[]{:S(2)}, u32[]{:S(2)}) %all-to-all-start.2) | async-done | bytes 2424864 | tf_op jit(solution)/shard_map/all_to_all | solution.py:543
  94.1 1.0 collective-permute-start.11
  95.1 4.3 %all-to-all-start.1 = ((bf16[16,288,128]{2,1,0:T(8,128)(2,1)}), bf16[16,288,128]{2,1,0:T(8,128)(2,1)}, u32[]{:S(2)}, u32[]{:S(2)}) async-start(bf16[16,288,128]{2,1,0:T(8,128)(2,1)} %image_pairs.1), calls=%async_computation.1 | async-start | bytes 2359296 | tf_op jit(solution)/shard_map/all_to_all | solution.py:543
  99.4 0.1 slice_reduce_fusion
  99.5 1.4 %collective-permute-start.12 = (bf16[400,128]{1,0:T(8,128)(2,1)S(1)}, bf16[400,128]{1,0:T(8,128)(2,1)S(1)}, u32[]{:S(2)}, u32[]{:S(2)}) collective-permute-start(bf16[400,128]{1,0:T(8,128)(2,1)S(1)} %slice_reduce_fusion), channel_id=1, source_target_pairs={{0,32},{32,64},{64,96},{96,0},{1,33},{33,65},{65,97},{97,1},{2,34}... | collective-permute-start | bytes 307208 | tf_op jit(solution)/shard_map/ppermute | solution.py:552
  100.9 3.7 %collective-permute-start.13 = (bf16[400,128]{1,0:T(8,128)(2,1)S(1)}, bf16[400,128]{1,0:T(8,128)(2,1)S(1)}, u32[]{:S(2)}, u32[]{:S(2)}) collective-permute-start(bf16[400,128]{1,0:T(8,128)(2,1)S(1)} %slice_reduce_fusion), channel_id=1, source_target_pairs={{0,64},{32,96},{64,0},{96,32},{1,65},{33,97},{65,1},{97,33},{2,66}... | collective-permute-start | bytes 307208 | tf_op jit(solution)/shard_map/ppermute | solution.py:552
  104.6 0.4 collective-permute-start.14
  105.1 1.6 %collective-permute-done.12 = bf16[400,128]{1,0:T(8,128)(2,1)S(1)} collective-permute-done((bf16[400,128]{1,0:T(8,128)(2,1)S(1)}, bf16[400,128]{1,0:T(8,128)(2,1)S(1)}, u32[]{:S(2)}, u32[]{:S(2)}) %collective-permute-start.12) | collective-permute-done | bytes 102432 | tf_op jit(solution)/shard_map/ppermute | solution.py:552
  106.7 3.2 %collective-permute-done.13 = bf16[400,128]{1,0:T(8,128)(2,1)S(1)} collective-permute-done((bf16[400,128]{1,0:T(8,128)(2,1)S(1)}, bf16[400,128]{1,0:T(8,128)(2,1)S(1)}, u32[]{:S(2)}, u32[]{:S(2)}) %collective-permute-start.13) | collective-permute-done | bytes 102432 | tf_op jit(solution)/shard_map/ppermute | solution.py:552
  109.9 0.4 collective-permute-start.15
  110.3 5.1 %unpack_text.1 = (bf16[333,1280]{1,0:T(8,128)(2,1)}, bf16[333,1280]{1,0:T(8,128)(2,1)}, bf16[333,1280]{1,0:T(8,128)(2,1)}) custom-call(s32[1]{0:T(128)} %bitcast.13.core, bf16[8,1184,128]{2,1,0:T(8,128)(2,1)} %copy-done.1, bf16[8,1184,128]{2,1,0:T(8,128)(2,1)} %collective-permute-done.11.other), custom_call_target="tpu_custom_call" | custom-call | tf_op jit(solution)/shard_map/unpack_text/pallas_call | solution.py:532
  115.4 2.7 %all-to-all-done.1.recv = bf16[16,288,128]{2,1,0:T(8,128)(2,1)} async-done(((bf16[16,288,128]{2,1,0:T(8,128)(2,1)}), bf16[16,288,128]{2,1,0:T(8,128)(2,1)}, u32[]{:S(2)}, u32[]{:S(2)}) %all-to-all-start.1) | async-done | bytes 1179680 | tf_op jit(solution)/shard_map/all_to_all | solution.py:543
  118.1 2.6 %unpack.1 = (bf16[128,1280]{1,0:T(8,128)(2,1)}, bf16[128,1280]{1,0:T(8,128)(2,1)}, bf16[128,1280]{1,0:T(8,128)(2,1)}) custom-call(bf16[16,288,128]{2,1,0:T(8,128)(2,1)} %all-to-all-done.1.recv), custom_call_target="tpu_custom_call" | custom-call | tf_op jit(solution)/shard_map/unpack/pallas_call | solution.py:478
  120.7 1.5 %collective-permute-done.15 = bf16[4,400,128]{2,1,0:T(8,128)(2,1)S(1)} collective-permute-done((bf16[4,400,128]{2,1,0:T(8,128)(2,1)S(1)}, bf16[4,400,128]{2,1,0:T(8,128)(2,1)S(1)}, u32[]{:S(2)}, u32[]{:S(2)}) %collective-permute-start.15) | collective-permute-done | bytes 409632 | tf_op jit(solution)/shard_map/ppermute | solution.py:552
  122.2 0.1 convert_add_fusion
  122.3 0.2 copy.26
  122.5 0.3 copy.29
  122.8 0.9 slice.8
  (34 shorter events, 0.3 us)
Async XLA Ops:
  6.9 32.9 %all-to-all-start = ((bf16[16,400,128]{2,1,0:T(8,128)(2,1)}), bf16[16,400,128]{2,1,0:T(8,128)(2,1)S(1)}, u32[]{:S(2)}, u32[]{:S(2)}) async-start(bf16[16,400,128]{2,1,0:T(8,128)(2,1)} %pack.1), calls=%async_computation | async-start | bytes 3276800 | tf_op jit(solution)/shard_map/all_to_all | solution.py:543
  16.2 2.4 %copy-start.2 = (bf16[1,128,2432]{2,1,0:T(8,128)(2,1)S(1)}, bf16[1,128,2432]{2,1,0:T(8,128)(2,1)}, u32[]{:S(2)}) copy-start(bf16[1,128,2432]{2,1,0:T(8,128)(2,1)} %param.17) | copy-start | bytes 1867780
  18.6 1.4 %copy-start.3 = (bf16[1,128,1280]{2,1,0:T(8,128)(2,1)S(1)}, bf16[1,128,1280]{2,1,0:T(8,128)(2,1)}, u32[]{:S(2)}) copy-start(bf16[1,128,1280]{2,1,0:T(8,128)(2,1)} %param.16) | copy-start | bytes 983044
  19.9 5.1 %collective-permute-start = (bf16[4,320,128]{2,1,0:T(8,128)(2,1)}, bf16[4,320,128]{2,1,0:T(8,128)(2,1)}, u32[]{:S(2)}, u32[]{:S(2)}) collective-permute-start(bf16[4,320,128]{2,1,0:T(8,128)(2,1)} %get-tuple-element.83), channel_id=1, source_target_pairs={{0,1},{1,0},{2,3},{3,2},{4,5},{5,4},{6,7},{7,6},{8,9},{9,8},{10,11... | collective-permute-start | bytes 983048 | tf_op jit(solution)/shard_map/ppermute | solution.py:547
  20.0 10.2 %collective-permute-start.4 = (bf16[128,1280]{1,0:T(8,128)(2,1)S(1)}, bf16[128,1280]{1,0:T(8,128)(2,1)S(1)}, u32[]{:S(2)}, u32[]{:S(2)}) collective-permute-start(bf16[128,1280]{1,0:T(8,128)(2,1)S(1)} %bitcast.74), channel_id=1, source_target_pairs={{0,32},{32,64},{64,96},{96,0},{1,33},{33,65},{65,97},{97,1},{2,34}... | collective-permute-start | bytes 983048 | tf_op jit(solution)/shard_map/ppermute | solution.py:552
  21.3 28.6 %collective-permute-start.5 = (bf16[128,1280]{1,0:T(8,128)(2,1)S(1)}, bf16[128,1280]{1,0:T(8,128)(2,1)S(1)}, u32[]{:S(2)}, u32[]{:S(2)}) collective-permute-start(bf16[128,1280]{1,0:T(8,128)(2,1)S(1)} %bitcast.75), channel_id=1, source_target_pairs={{0,64},{32,96},{64,0},{96,32},{1,65},{33,97},{65,1},{97,33},{2,66}... | collective-permute-start | bytes 983048 | tf_op jit(solution)/shard_map/ppermute | solution.py:552
  23.9 27.0 %collective-permute-start.6 = (bf16[128,1280]{1,0:T(8,128)(2,1)S(1)}, bf16[128,1280]{1,0:T(8,128)(2,1)S(1)}, u32[]{:S(2)}, u32[]{:S(2)}) collective-permute-start(bf16[128,1280]{1,0:T(8,128)(2,1)S(1)} %bitcast.76), channel_id=1, source_target_pairs={{0,96},{32,0},{64,32},{96,64},{1,97},{33,1},{65,33},{97,65},{2,98}... | collective-permute-start | bytes 983048 | tf_op jit(solution)/shard_map/ppermute | solution.py:552
  26.8 24.1 %collective-permute-start.1 = (bf16[320,256]{1,0:T(8,128)(2,1)}, bf16[320,256]{1,0:T(8,128)(2,1)}, u32[]{:S(2)}, u32[]{:S(2)}) collective-permute-start(bf16[320,256]{1,0:T(8,128)(2,1)} %get-tuple-element.81), channel_id=1, source_target_pairs={{0,32},{32,64},{64,96},{96,0},{1,33},{33,65},{65,97},{97,1},{2,34}... | collective-permute-start | bytes 491528 | tf_op jit(solution)/shard_map/ppermute | solution.py:552
  27.2 23.7 %collective-permute-start.2 = (bf16[320,256]{1,0:T(8,128)(2,1)}, bf16[320,256]{1,0:T(8,128)(2,1)}, u32[]{:S(2)}, u32[]{:S(2)}) collective-permute-start(bf16[320,256]{1,0:T(8,128)(2,1)} %get-tuple-element.82), channel_id=1, source_target_pairs={{0,64},{32,96},{64,0},{96,32},{1,65},{33,97},{65,1},{97,33},{2,66}... | collective-permute-start | bytes 491528 | tf_op jit(solution)/shard_map/ppermute | solution.py:552
  30.2 23.5 %copy-start.4 = (bf16[128,1280]{1,0:T(8,128)(2,1)}, bf16[128,1280]{1,0:T(8,128)(2,1)S(1)}, u32[]{:S(2)}) copy-start(bf16[128,1280]{1,0:T(8,128)(2,1)S(1)} %collective-permute-done.4.refs_5_) | copy-start | bytes 983044
  30.2 20.7 %collective-permute-start.3 = (bf16[320,256]{1,0:T(8,128)(2,1)S(1)}, bf16[320,256]{1,0:T(8,128)(2,1)}, u32[]{:S(2)}, u32[]{:S(2)}) collective-permute-start(bf16[320,256]{1,0:T(8,128)(2,1)S(1)} %get-tuple-element.79), channel_id=1, source_target_pairs={{0,96},{32,0},{64,32},{96,64},{1,97},{33,1},{65,33},{97,65},{2,98}... | collective-permute-start | bytes 491528 | tf_op jit(solution)/shard_map/ppermute | solution.py:552
  39.8 1.2 copy-start
  49.9 3.9 %copy-start.5 = (bf16[128,1280]{1,0:T(8,128)(2,1)}, bf16[128,1280]{1,0:T(8,128)(2,1)S(1)}, u32[]{:S(2)}) copy-start(bf16[128,1280]{1,0:T(8,128)(2,1)S(1)} %collective-permute-done.5.refs_6_) | copy-start | bytes 983044
  49.9 2.3 %collective-permute-start.7 = (bf16[128,1280]{1,0:T(8,128)(2,1)S(1)}, bf16[128,1280]{1,0:T(8,128)(2,1)S(1)}, u32[]{:S(2)}, u32[]{:S(2)}) collective-permute-start(bf16[128,1280]{1,0:T(8,128)(2,1)S(1)} %bitcast.77), channel_id=1, source_target_pairs={{0,1},{1,0},{2,3},{3,2},{4,5},{5,4},{6,7},{7,6},{8,9},{9,8},{10,11... | collective-permute-start | bytes 983048 | tf_op jit(solution)/shard_map/ppermute | solution.py:547
  50.9 2.9 %copy-start.6 = (bf16[128,1280]{1,0:T(8,128)(2,1)}, bf16[128,1280]{1,0:T(8,128)(2,1)S(1)}, u32[]{:S(2)}) copy-start(bf16[128,1280]{1,0:T(8,128)(2,1)S(1)} %collective-permute-done.6.refs_7_) | copy-start | bytes 983044
  50.9 1.9 %collective-permute-start.8 = (bf16[128,1280]{1,0:T(8,128)(2,1)S(1)}, bf16[128,1280]{1,0:T(8,128)(2,1)S(1)}, u32[]{:S(2)}, u32[]{:S(2)}) collective-permute-start(bf16[128,1280]{1,0:T(8,128)(2,1)S(1)} %collective-permute-done.4.refs_5_), channel_id=1, source_target_pairs={{0,1},{1,0},{2,3},{3,2},{4,5},{5,4},{6,7},{7,6},{8,9},{9,8},{10,11... | collective-permute-start | bytes 983048 | tf_op jit(solution)/shard_map/ppermute | solution.py:547
  51.2 2.1 %collective-permute-start.9 = (bf16[128,1280]{1,0:T(8,128)(2,1)S(1)}, bf16[128,1280]{1,0:T(8,128)(2,1)S(1)}, u32[]{:S(2)}, u32[]{:S(2)}) collective-permute-start(bf16[128,1280]{1,0:T(8,128)(2,1)S(1)} %collective-permute-done.5.refs_6_), channel_id=1, source_target_pairs={{0,1},{1,0},{2,3},{3,2},{4,5},{5,4},{6,7},{7,6},{8,9},{9,8},{10,11... | collective-permute-start | bytes 983048 | tf_op jit(solution)/shard_map/ppermute | solution.py:547
  51.7 2.1 %collective-permute-start.10 = (bf16[128,1280]{1,0:T(8,128)(2,1)S(1)}, bf16[128,1280]{1,0:T(8,128)(2,1)S(1)}, u32[]{:S(2)}, u32[]{:S(2)}) collective-permute-start(bf16[128,1280]{1,0:T(8,128)(2,1)S(1)} %collective-permute-done.6.refs_7_), channel_id=1, source_target_pairs={{0,1},{1,0},{2,3},{3,2},{4,5},{5,4},{6,7},{7,6},{8,9},{9,8},{10,11... | collective-permute-start | bytes 983048 | tf_op jit(solution)/shard_map/ppermute | solution.py:547
  52.2 1.6 %copy-start.7 = (bf16[128,1280]{1,0:T(8,128)(2,1)}, bf16[128,1280]{1,0:T(8,128)(2,1)S(1)}, u32[]{:S(2)}) copy-start(bf16[128,1280]{1,0:T(8,128)(2,1)S(1)} %collective-permute-done.7.refs_8_) | copy-start | bytes 983044
  52.8 1.0 copy-start.8
  53.3 0.7 copy-start.9
  54.0 0.7 copy-start.10
  58.6 35.5 %all-to-all-start.2 = ((bf16[8,1184,128]{2,1,0:T(8,128)(2,1)}), bf16[8,1184,128]{2,1,0:T(8,128)(2,1)S(1)}, u32[]{:S(2)}, u32[]{:S(2)}) async-start(bf16[8,1184,128]{2,1,0:T(8,128)(2,1)} %weight.1), calls=%async_computation.2 | async-start | bytes 4849664 | tf_op jit(solution)/shard_map/all_to_all | solution.py:543
  94.1 16.2 %copy-start.1 = (bf16[8,1184,128]{2,1,0:T(8,128)(2,1)}, bf16[8,1184,128]{2,1,0:T(8,128)(2,1)S(1)}, u32[]{:S(2)}) copy-start(bf16[8,1184,128]{2,1,0:T(8,128)(2,1)S(1)} %all-to-all-done.2.mine) | copy-start | bytes 7274500
  94.1 16.2 %collective-permute-start.11 = (bf16[8,1184,128]{2,1,0:T(8,128)(2,1)S(1)}, bf16[8,1184,128]{2,1,0:T(8,128)(2,1)}, u32[]{:S(2)}, u32[]{:S(2)}) collective-permute-start(bf16[8,1184,128]{2,1,0:T(8,128)(2,1)S(1)} %all-to-all-done.2.mine), channel_id=1, source_target_pairs={{0,1},{1,0},{2,3},{3,2},{4,5},{5,4},{6,7},{7,6},{8,9},{9,8},{10,11... | collective-permute-start | bytes 7274504 | tf_op jit(solution)/shard_map/ppermute | solution.py:547
  95.1 23.0 %all-to-all-start.1 = ((bf16[16,288,128]{2,1,0:T(8,128)(2,1)}), bf16[16,288,128]{2,1,0:T(8,128)(2,1)}, u32[]{:S(2)}, u32[]{:S(2)}) async-start(bf16[16,288,128]{2,1,0:T(8,128)(2,1)} %image_pairs.1), calls=%async_computation.1 | async-start | bytes 2359296 | tf_op jit(solution)/shard_map/all_to_all | solution.py:543
  99.5 7.1 %collective-permute-start.12 = (bf16[400,128]{1,0:T(8,128)(2,1)S(1)}, bf16[400,128]{1,0:T(8,128)(2,1)S(1)}, u32[]{:S(2)}, u32[]{:S(2)}) collective-permute-start(bf16[400,128]{1,0:T(8,128)(2,1)S(1)} %slice_reduce_fusion), channel_id=1, source_target_pairs={{0,32},{32,64},{64,96},{96,0},{1,33},{33,65},{65,97},{97,1},{2,34}... | collective-permute-start | bytes 307208 | tf_op jit(solution)/shard_map/ppermute | solution.py:552
  100.9 8.9 %collective-permute-start.13 = (bf16[400,128]{1,0:T(8,128)(2,1)S(1)}, bf16[400,128]{1,0:T(8,128)(2,1)S(1)}, u32[]{:S(2)}, u32[]{:S(2)}) collective-permute-start(bf16[400,128]{1,0:T(8,128)(2,1)S(1)} %slice_reduce_fusion), channel_id=1, source_target_pairs={{0,64},{32,96},{64,0},{96,32},{1,65},{33,97},{65,1},{97,33},{2,66}... | collective-permute-start | bytes 307208 | tf_op jit(solution)/shard_map/ppermute | solution.py:552
  104.6 5.3 %collective-permute-start.14 = (bf16[400,128]{1,0:T(8,128)(2,1)S(1)}, bf16[400,128]{1,0:T(8,128)(2,1)S(1)}, u32[]{:S(2)}, u32[]{:S(2)}) collective-permute-start(bf16[400,128]{1,0:T(8,128)(2,1)S(1)} %slice_reduce_fusion), channel_id=1, source_target_pairs={{0,96},{32,0},{64,32},{96,64},{1,97},{33,1},{65,33},{97,65},{2,98}... | collective-permute-start | bytes 307208 | tf_op jit(solution)/shard_map/ppermute | solution.py:552
  109.9 12.3 %collective-permute-start.15 = (bf16[4,400,128]{2,1,0:T(8,128)(2,1)S(1)}, bf16[4,400,128]{2,1,0:T(8,128)(2,1)S(1)}, u32[]{:S(2)}, u32[]{:S(2)}) collective-permute-start(bf16[4,400,128]{2,1,0:T(8,128)(2,1)S(1)} %bitcast_dynamic-update-slice_fusion), channel_id=1, source_target_pairs={{0,16},{16,0},{1,17},{17,1},{2,18},{18,2},{3,19},{19,3},{4,20},{20... | collective-permute-start | bytes 1228808 | tf_op jit(solution)/shard_map/ppermute | solution.py:552

commit v7 on v6

--- a/solution.py
+++ b/solution.py
@@ -320,7 +320,7 @@
 
 
 def text_pairs_kernel(
-    recv, wqg, wkv, wst, lqg, lkv, lst, tout, w_dkv, w_dqt, h_dkv, h_dqt, *refs
+    recv, wqg, wkv, wst, lqg, lkv, lst, message, w_dkv, w_dqt, h_dkv, h_dqt, tout, sems, *refs
 ):
     w, h = Head(refs[:9]), Head(refs[9:])
     fill_whole(w, recv)
@@ -347,7 +347,6 @@
     h.block(0, SH, SH, HALF_Q)
     h.block(SH, HALF, 0, SH)
 
-    tout[:, 0:WOUT, :] = jnp.zeros((N // 2, WOUT, 128), BF)
     w_dkv[...] = w.dkv[0:S, :]
     w_dqt[...] = w.dqt[:, 0:S]
     h_dkv[...] = h.dkv[0:SH, :]
@@ -356,9 +355,7 @@
     factor = jnp.where(iota((128, 128), 1) < 64, SCALE, 1.0)
 
     def put(at, value):
-        value = value.astype(BF)
-        for n in range(N // 2):
-            tout[n, WOUT + at : WOUT + at + value.shape[0], :] = value
+        tout[at : at + value.shape[0], :] = value.astype(BF)
 
     for m in range(TXT_Q // 128):
         rows = min(128, TXT_K - 128 * m)
@@ -372,6 +369,14 @@
         part = dqt * SCALE
         both = jnp.concatenate([part, pltpu.roll(part, part.shape[1] - fold, 1)], 0)
         put(at, both[:, 0:256].T[:fold])
+    copies = [
+        pltpu.make_async_copy(tout, message.at[n, pl.ds(WOUT, TOUT)], sems.at[n])
+        for n in range(N // 2)
+    ]
+    for copy in copies:
+        copy.start()
+    for copy in copies:
+        copy.wait()
 
 
 STATE = [(S, 128), (64, S), (SH, 128), (64, SH)]
@@ -382,10 +387,12 @@
     return pl.pallas_call(
         text_pairs_kernel,
         in_specs=[full] * 7,
-        out_specs=[full] * 5,
+        out_specs=[pl.BlockSpec(memory_space=pl.ANY)] + [full] * 4,
         out_shape=[jax.ShapeDtypeStruct((N // 2, WOUT + TOUT, 128), BF)]
         + [jax.ShapeDtypeStruct(s, F32) for s in STATE],
-        scratch_shapes=Head.scratch(W_ROWS) + Head.scratch(L_ROWS),
+        scratch_shapes=[pltpu.VMEM((TOUT, 128), BF), pltpu.SemaphoreType.DMA((N // 2,))]
+        + Head.scratch(W_ROWS)
+        + Head.scratch(L_ROWS),
         compiler_params=pltpu.CompilerParams(vmem_limit_bytes=VMEM_LIMIT),
         name="text_pairs",
     )(recv, *texts)
@@ -614,11 +621,25 @@
     )(*args, message)
 
 
-def weight_total(parts, rows, after):
-    part = gathered(parts.astype(F32).sum(0).astype(BF), "y")
-    if lax.axis_size("xl") > 1:
-        other, _ = lax.optimization_barrier((shifted(part, "xl", 1), after))
-        part = part.astype(F32) + other.astype(F32)
+def across(x, by):
+    y, xl = lax.axis_size("y"), lax.axis_size("xl")
+    pairs = [
+        (i * xl + j, (i + by) % y * xl + (j + 1) % xl) for i in range(y) for j in range(xl)
+    ]
+    return lax.ppermute(x, IMG, pairs)
+
+
+def placed(pieces, axis):
+    size, me = lax.axis_size(axis), lax.axis_index(axis)
+    out = jnp.zeros((size, *pieces[0].shape), pieces[0].dtype)
+    for by, piece in enumerate(pieces):
+        out = lax.dynamic_update_index_in_dim(out, piece, (me - by) % size, 0)
+    return out
+
+
+def weight_total(part, others, rows):
+    if others:
+        part = part.astype(F32) + placed(others, "y").astype(F32)
     y, height, lanes = part.shape
     part = part.reshape(y, 10, height // 10, lanes).swapaxes(1, 2)
     return part.reshape(-1, 10 * lanes)[:rows].astype(F32)
@@ -673,9 +694,14 @@
     mine, _ = lax.optimization_barrier((mine, out))
     text_grads = unpack_text(core, mine, other_core(mine))
     got = exchange(out, SEQ)
-    got, text_grads = lax.optimization_barrier((got, text_grads))
+    part = mine[:, :WOUT].astype(F32).sum(0).astype(BF)
+    both_sides = lax.axis_size("xl") > 1
+    others = [across(part, by) for by in range(lax.axis_size("y")) if both_sides]
+    part = gathered(part, "y")
+    got, text_grads, part = lax.optimization_barrier((got, text_grads, part))
     grads = unpack(got)
-    weight_grad = weight_total(mine[:, :WOUT], output_grad.shape[2] // N, grads)
+    others, _ = lax.optimization_barrier((others, grads))
+    weight_grad = weight_total(part, others, output_grad.shape[2] // N)
     return (*(g[None] for g in grads), *(g[None] for g in text_grads), weight_grad)
 
 

time: 125 us -> 128 us (1.024)
  starting transfers between devices: 33.6 us -> 36.5 us
  waiting for transfers between devices: 34.6 us -> 32.7 us
    ppermute x0 -> x4, starting transfers between devices: none -> 3.32 us  [across(): return lax.ppermute(x, IMG, pairs)]
    ppermute x10 -> x9, waiting for transfers between devices: 8.61 us -> 5.98 us  [shifted(): return lax.ppermute(x, axis, [(i, (i + by) % size) for i in range(size)])]
    ppermute x0 -> x4, waiting for transfers between devices: none -> 2.56 us  [across(): return lax.ppermute(x, IMG, pairs)]
    all_to_all x3, waiting for transfers between devices: 24 us -> 22.2 us  [exchange(): return lax.all_to_all(x, axes, 0, 0, tiled=True)]
    ppermute x10 -> x9, starting transfers between devices: 13.4 us -> 13 us  [shifted(): return lax.ppermute(x, axis, [(i, (i + by) % size) for i in range(size)])]
  transfers between devices with their start and end apart: 19 -> 22, of which waited for: 11 -> 13; matrix products, arithmetic and copies ran while one was open for 3% -> 3% of each run, Pallas kernels for 30% -> 31%
where the time goes in v7:
time: 128 us; the launch traced here: 126 us
  Pallas kernels  48.8 us (38%)
  starting transfers between devices  36.5 us (29%)
  waiting for transfers between devices  32.7 us (26%)
  local copies, waits for them, and re-layouts  5.06 us (4%)
  other arithmetic  1.99 us (2%)
    all_to_all x3, waiting for transfers between devices, exchange(): return lax.all_to_all(x, axes, 0, 0, tiled=True)  22.2 us
    pallas_call x1, Pallas kernels, image_pairs(): pl.pallas_call(image_pairs_kernel, in_specs=[full] * 5, out_specs=full, o...  18.6 us
    all_to_all x3, starting transfers between devices, exchange(): return lax.all_to_all(x, axes, 0, 0, tiled=True)  17.2 us
    ppermute x9, starting transfers between devices, shifted(): return lax.ppermute(x, axis, [(i, (i + by) % size) for i in range(size)])  13 us
    pallas_call x1, Pallas kernels, text_pairs(): pl.pallas_call(text_pairs_kernel, in_specs=[full] * 7, out_specs=[pl.Bloc...  9.95 us
    pallas_call x1, Pallas kernels, pack(): pl.pallas_call(pack_kernel, in_specs=[pl.BlockSpec(memory_space=pltpu.SME...  6.22 us
    ppermute x9, waiting for transfers between devices, shifted(): return lax.ppermute(x, axis, [(i, (i + by) % size) for i in range(size)])  5.98 us
    pallas_call x1, Pallas kernels, unpack_text(): pl.pallas_call(unpack_text_kernel, in_specs=[pl.BlockSpec(memory_space=pl...  5.11 us
  transfers between devices with their start and end apart: 22, of which 13 were waited for; matrix products, arithmetic and copies ran while one was open for 3% of the time, Pallas kernels for 31%

profile of v7, /device:TPU:1, one launch (start us, length us, event | category | flops | bytes accessed | tf_op | source)
XLA Modules:
  0.0 126.0 jit_solution(2810406021205931247)
XLA Ops:
  0.6 6.2 %pack.1 = bf16[16,400,128]{2,1,0:T(8,128)(2,1)} custom-call(s32[1]{0:T(128)} %bitcast.index, bf16[128,2432]{1,0:T(8,128)(2,1)} %bitcast.77, bf16[2432,1280]{1,0:T(8,128)(2,1)} %w_hbm.1, bf16[128,1280]{1,0:T(8,128)(2,1)} %bitcast.86, bf16[128,1280]{1,0:T(8,128)(2,1)} %bitcast.87, bf16[128,1280]{1,0:T(8,128)(2,1)} %bitcast.88, bf16[128,1280]{1,0:T(8,128)(2,1)} %bitcast.80, ...), custom_call_target="tpu_custom_call" | custom-call | tf_op jit(solution)/shard_map/pack/pallas_call | solution.py:149
  6.9 9.3 %all-to-all-start = ((bf16[16,400,128]{2,1,0:T(8,128)(2,1)}), bf16[16,400,128]{2,1,0:T(8,128)(2,1)S(1)}, u32[]{:S(2)}, u32[]{:S(2)}) async-start(bf16[16,400,128]{2,1,0:T(8,128)(2,1)} %pack.1), calls=%async_computation | async-start | bytes 3276800 | tf_op jit(solution)/shard_map/all_to_all | solution.py:550
  16.2 2.4 %text_prep.1 = (bf16[384,128]{1,0:T(8,128)(2,1)}, bf16[384,128]{1,0:T(8,128)(2,1)}, bf16[16,384]{1,0:T(8,128)(2,1)}, bf16[256,128]{1,0:T(8,128)(2,1)}, bf16[256,...) custom-call(s32[1]{0:T(128)} %bitcast.index, bf16[333,1280]{1,0:T(8,128)(2,1)} %bitcast.63, bf16[333,1280]{1,0:T(8,128)(2,1)} %bitcast.65, ...), custom_call_target="tpu_custom_call" | custom-call | tf_op jit(solution)/shard_map/text_prep/pallas_call | solution.py:219
  18.6 0.3 copy.24
  19.1 0.8 dynamic-slice_bitcast_fusion
  20.0 1.3 %collective-permute-start.4 = (bf16[128,1280]{1,0:T(8,128)(2,1)S(1)}, bf16[128,1280]{1,0:T(8,128)(2,1)S(1)}, u32[]{:S(2)}, u32[]{:S(2)}) collective-permute-start(bf16[128,1280]{1,0:T(8,128)(2,1)S(1)} %bitcast.82), channel_id=1, source_target_pairs={{0,32},{32,64},{64,96},{96,0},{1,33},{33,65},{65,97},{97,1},{2,34}... | collective-permute-start | bytes 983048 | tf_op jit(solution)/shard_map/ppermute | solution.py:559
  21.3 2.6 %collective-permute-start.5 = (bf16[128,1280]{1,0:T(8,128)(2,1)S(1)}, bf16[128,1280]{1,0:T(8,128)(2,1)S(1)}, u32[]{:S(2)}, u32[]{:S(2)}) collective-permute-start(bf16[128,1280]{1,0:T(8,128)(2,1)S(1)} %bitcast.83), channel_id=1, source_target_pairs={{0,64},{32,96},{64,0},{96,32},{1,65},{33,97},{65,1},{97,33},{2,66}... | collective-permute-start | bytes 983048 | tf_op jit(solution)/shard_map/ppermute | solution.py:559
  23.9 1.1 collective-permute-start.6
  25.0 1.8 %fusion.1 = (bf16[320,256]{1,0:T(8,128)(2,1)S(1)}, bf16[320,256]{1,0:T(8,128)(2,1)}, bf16[320,256]{1,0:T(8,128)(2,1)}, bf16[320,256]{1,0:T(8,128)(2,1)}) fusion(s32[]{:T(128)S(6)} %select_n.85, bf16[4,320,128]{2,1,0:T(8,128)(2,1)S(1)} %get-tuple-element.92, bf16[4,320,128]{2,1,0:T(8,128)(2,1)} %collective-permute-done, s32[]{:T(128)S(6)} %select_n.79, ...), kind=kLoop, calls=%fused_computation.14 | loop fusion | flops 1310720 | bytes 1310736 | tf_op jit(solution)/shard_map/jit(dynamic_index_in_dim)/squeeze | solution.py:584
  26.8 0.4 collective-permute-start.1
  27.2 0.8 collective-permute-start.2
  28.0 2.2 %collective-permute-done.4.refs_5_ = bf16[128,1280]{1,0:T(8,128)(2,1)S(1)} collective-permute-done((bf16[128,1280]{1,0:T(8,128)(2,1)S(1)}, bf16[128,1280]{1,0:T(8,128)(2,1)S(1)}, u32[]{:S(2)}, u32[]{:S(2)}) %collective-permute-start.4) | collective-permute-done | bytes 327712 | tf_op jit(solution)/shard_map/ppermute | solution.py:559
  30.2 1.4 %collective-permute-start.3 = (bf16[320,256]{1,0:T(8,128)(2,1)S(1)}, bf16[320,256]{1,0:T(8,128)(2,1)}, u32[]{:S(2)}, u32[]{:S(2)}) collective-permute-start(bf16[320,256]{1,0:T(8,128)(2,1)S(1)} %get-tuple-element.87), channel_id=1, source_target_pairs={{0,96},{32,0},{64,32},{96,64},{1,97},{33,1},{65,33},{97,65},{2,98}... | collective-permute-start | bytes 491528 | tf_op jit(solution)/shard_map/ppermute | solution.py:559
  31.6 8.1 %all-to-all-done.recv = bf16[16,400,128]{2,1,0:T(8,128)(2,1)S(1)} async-done(((bf16[16,400,128]{2,1,0:T(8,128)(2,1)}), bf16[16,400,128]{2,1,0:T(8,128)(2,1)S(1)}, u32[]{:S(2)}, u32[]{:S(2)}) %all-to-all-start) | async-done | bytes 1638432 | tf_op jit(solution)/shard_map/all_to_all | solution.py:550
  39.7 1.2 copy-done
  40.9 10.0 %text_pairs.1 = (bf16[8,1184,128]{2,1,0:T(8,128)(2,1)}, f32[2048,128]{1,0:T(8,128)}, f32[64,2048]{1,0:T(8,128)}, f32[1024,128]{1,0:T(8,128)}, f32[64,1024]{1,0:T(8,128)}) custom-call(bf16[16,400,128]{2,1,0:T(8,128)(2,1)} %copy-done, bf16[384,128]{1,0:T(8,128)(2,1)} %get-tuple-element.48.wqg, bf16[384,128]{1,0:T(8,128)(2,1)} %get-tuple-element.49.wkv, ...), custom_call_target="tpu_custom_call" | custom-call | tf_op jit(solution)/shard_map/text_pairs/pallas_call | solution.py:387
  50.9 1.0 collective-permute-start.7
  51.9 0.3 collective-permute-start.8
  52.2 0.5 collective-permute-start.9
  52.8 0.4 collective-permute-done.7.refs_8_
  53.2 0.7 collective-permute-done.8.refs_9_
  53.8 0.5 collective-permute-done.9.refs_10_
  54.3 0.5 collective-permute-done.10.refs_11_
  54.8 0.2 copy-done.9
  55.0 0.7 copy-done.10
  55.7 3.9 %weight.1 = bf16[8,1184,128]{2,1,0:T(8,128)(2,1)} custom-call(bf16[320,256]{1,0:T(8,128)(2,1)} %get-tuple-element.62.refs_0_, bf16[320,256]{1,0:T(8,128)(2,1)} %collective-permute-done.1.refs_1_, bf16[320,256]{1,0:T(8,128)(2,1)} %collective-permute-done.2.refs_2_, bf16[320,256]{1,0:T(8,128)(2,1)} %collective-permute-done.3.refs_3_, ...), custom_call_target="tpu_custom_call", output_to_operand_aliasing={{}: (12, {})} | custom-call | tf_op jit(solution)/shard_map/weight/pallas_call | solution.py:610
  59.6 3.6 %all-to-all-start.2 = ((bf16[8,1184,128]{2,1,0:T(8,128)(2,1)}), bf16[8,1184,128]{2,1,0:T(8,128)(2,1)S(1)}, u32[]{:S(2)}, u32[]{:S(2)}) async-start(bf16[8,1184,128]{2,1,0:T(8,128)(2,1)} %weight.1), calls=%async_computation.2 | async-start | bytes 4849664 | tf_op jit(solution)/shard_map/all_to_all | solution.py:550
  63.2 18.6 %image_pairs.1 = bf16[16,288,128]{2,1,0:T(8,128)(2,1)} custom-call(bf16[16,400,128]{2,1,0:T(8,128)(2,1)} %copy-done, f32[2048,128]{1,0:T(8,128)} %get-tuple-element.54.a, f32[64,2048]{1,0:T(8,128)} %get-tuple-element.55.b, f32[1024,128]{1,0:T(8,128)} %get-tuple-element.56.c, f32[64,1024]{1,0:T(8,128)} %get-tuple-element.57.d), custom_call_target="tpu_custom_call" | custom-call | tf_op jit(solution)/shard_map/image_pairs/pallas_call | solution.py:429
  81.8 13.3 %all-to-all-done.2.mine = bf16[8,1184,128]{2,1,0:T(8,128)(2,1)S(1)} async-done(((bf16[8,1184,128]{2,1,0:T(8,128)(2,1)}), bf16[8,1184,128]{2,1,0:T(8,128)(2,1)S(1)}, u32[]{:S(2)}, u32[]{:S(2)}) %all-to-all-start.2) | async-done | bytes 2424864 | tf_op jit(solution)/shard_map/all_to_all | solution.py:550
  95.1 1.0 collective-permute-start.11
  96.1 4.3 %all-to-all-start.1 = ((bf16[16,288,128]{2,1,0:T(8,128)(2,1)}), bf16[16,288,128]{2,1,0:T(8,128)(2,1)}, u32[]{:S(2)}, u32[]{:S(2)}) async-start(bf16[16,288,128]{2,1,0:T(8,128)(2,1)} %image_pairs.1), calls=%async_computation.1 | async-start | bytes 2359296 | tf_op jit(solution)/shard_map/all_to_all | solution.py:550
  100.6 1.4 %collective-permute-start.12 = (bf16[400,128]{1,0:T(8,128)(2,1)S(1)}, bf16[400,128]{1,0:T(8,128)(2,1)S(1)}, u32[]{:S(2)}, u32[]{:S(2)}) collective-permute-start(bf16[400,128]{1,0:T(8,128)(2,1)S(1)} %slice_reduce_fusion), channel_id=1, source_target_pairs={{0,32},{32,64},{64,96},{96,0},{1,33},{33,65},{65,97},{97,1},{2,34}... | collective-permute-start | bytes 307208 | tf_op jit(solution)/shard_map/ppermute | solution.py:559
  102.0 3.7 %collective-permute-start.13 = (bf16[400,128]{1,0:T(8,128)(2,1)S(1)}, bf16[400,128]{1,0:T(8,128)(2,1)S(1)}, u32[]{:S(2)}, u32[]{:S(2)}) collective-permute-start(bf16[400,128]{1,0:T(8,128)(2,1)S(1)} %slice_reduce_fusion), channel_id=1, source_target_pairs={{0,64},{32,96},{64,0},{96,32},{1,65},{33,97},{65,1},{97,33},{2,66}... | collective-permute-start | bytes 307208 | tf_op jit(solution)/shard_map/ppermute | solution.py:559
  105.7 0.4 collective-permute-start.14
  106.0 0.3 collective-permute-start.15
  106.4 1.3 %collective-permute-done.12 = bf16[400,128]{1,0:T(8,128)(2,1)S(1)} collective-permute-done((bf16[400,128]{1,0:T(8,128)(2,1)S(1)}, bf16[400,128]{1,0:T(8,128)(2,1)S(1)}, u32[]{:S(2)}, u32[]{:S(2)}) %collective-permute-start.12) | collective-permute-done | bytes 102432 | tf_op jit(solution)/shard_map/ppermute | solution.py:559
  107.7 0.8 collective-permute-start.16
  108.5 2.4 %collective-permute-done.13 = bf16[400,128]{1,0:T(8,128)(2,1)S(1)} collective-permute-done((bf16[400,128]{1,0:T(8,128)(2,1)S(1)}, bf16[400,128]{1,0:T(8,128)(2,1)S(1)}, u32[]{:S(2)}, u32[]{:S(2)}) %collective-permute-start.13) | collective-permute-done | bytes 102432 | tf_op jit(solution)/shard_map/ppermute | solution.py:559
  110.9 0.5 collective-permute-start.17
  111.4 1.8 %collective-permute-start.18 = (bf16[400,128]{1,0:T(8,128)(2,1)S(1)}, bf16[400,128]{1,0:T(8,128)(2,1)S(1)}, u32[]{:S(2)}, u32[]{:S(2)}) collective-permute-start(bf16[400,128]{1,0:T(8,128)(2,1)S(1)} %slice_reduce_fusion), channel_id=1, source_target_pairs={{0,112},{16,96},{32,16},{48,0},{64,48},{80,32},{96,80},{112,64},{1... | collective-permute-start | bytes 307208 | tf_op jit(solution)/shard_map/ppermute | solution.py:629
  113.2 5.1 %unpack_text.1 = (bf16[333,1280]{1,0:T(8,128)(2,1)}, bf16[333,1280]{1,0:T(8,128)(2,1)}, bf16[333,1280]{1,0:T(8,128)(2,1)}) custom-call(s32[1]{0:T(128)} %bitcast.13.core, bf16[8,1184,128]{2,1,0:T(8,128)(2,1)} %copy-done.1, bf16[8,1184,128]{2,1,0:T(8,128)(2,1)} %collective-permute-done.11.other), custom_call_target="tpu_custom_call" | custom-call | tf_op jit(solution)/shard_map/unpack_text/pallas_call | solution.py:539
  118.3 0.7 all-to-all-done.1.recv
  119.1 2.6 %unpack.1 = (bf16[128,1280]{1,0:T(8,128)(2,1)}, bf16[128,1280]{1,0:T(8,128)(2,1)}, bf16[128,1280]{1,0:T(8,128)(2,1)}) custom-call(bf16[16,288,128]{2,1,0:T(8,128)(2,1)} %all-to-all-done.1.recv), custom_call_target="tpu_custom_call" | custom-call | tf_op jit(solution)/shard_map/unpack/pallas_call | solution.py:485
  121.7 0.6 collective-permute-done.16
  122.3 1.9 %collective-permute-done.17 = bf16[400,128]{1,0:T(8,128)(2,1)S(1)} collective-permute-done((bf16[400,128]{1,0:T(8,128)(2,1)S(1)}, bf16[400,128]{1,0:T(8,128)(2,1)S(1)}, u32[]{:S(2)}, u32[]{:S(2)}) %collective-permute-start.17) | collective-permute-done | bytes 102432 | tf_op jit(solution)/shard_map/ppermute | solution.py:629
  124.5 0.2 copy.26
  124.7 0.3 copy.29
  125.0 0.9 slice.8
  (45 shorter events, 0.9 us)
Async XLA Ops:
  6.9 32.9 %all-to-all-start = ((bf16[16,400,128]{2,1,0:T(8,128)(2,1)}), bf16[16,400,128]{2,1,0:T(8,128)(2,1)S(1)}, u32[]{:S(2)}, u32[]{:S(2)}) async-start(bf16[16,400,128]{2,1,0:T(8,128)(2,1)} %pack.1), calls=%async_computation | async-start | bytes 3276800 | tf_op jit(solution)/shard_map/all_to_all | solution.py:550
  16.2 2.4 %copy-start.2 = (bf16[1,128,2432]{2,1,0:T(8,128)(2,1)S(1)}, bf16[1,128,2432]{2,1,0:T(8,128)(2,1)}, u32[]{:S(2)}) copy-start(bf16[1,128,2432]{2,1,0:T(8,128)(2,1)} %param.17) | copy-start | bytes 1867780
  18.6 1.4 %copy-start.3 = (bf16[1,128,1280]{2,1,0:T(8,128)(2,1)S(1)}, bf16[1,128,1280]{2,1,0:T(8,128)(2,1)}, u32[]{:S(2)}) copy-start(bf16[1,128,1280]{2,1,0:T(8,128)(2,1)} %param.16) | copy-start | bytes 983044
  19.9 5.1 %collective-permute-start = (bf16[4,320,128]{2,1,0:T(8,128)(2,1)}, bf16[4,320,128]{2,1,0:T(8,128)(2,1)}, u32[]{:S(2)}, u32[]{:S(2)}) collective-permute-start(bf16[4,320,128]{2,1,0:T(8,128)(2,1)} %get-tuple-element.91), channel_id=1, source_target_pairs={{0,1},{1,0},{2,3},{3,2},{4,5},{5,4},{6,7},{7,6},{8,9},{9,8},{10,11... | collective-permute-start | bytes 983048 | tf_op jit(solution)/shard_map/ppermute | solution.py:554
  20.0 10.2 %collective-permute-start.4 = (bf16[128,1280]{1,0:T(8,128)(2,1)S(1)}, bf16[128,1280]{1,0:T(8,128)(2,1)S(1)}, u32[]{:S(2)}, u32[]{:S(2)}) collective-permute-start(bf16[128,1280]{1,0:T(8,128)(2,1)S(1)} %bitcast.82), channel_id=1, source_target_pairs={{0,32},{32,64},{64,96},{96,0},{1,33},{33,65},{65,97},{97,1},{2,34}... | collective-permute-start | bytes 983048 | tf_op jit(solution)/shard_map/ppermute | solution.py:559
  21.3 29.6 %collective-permute-start.5 = (bf16[128,1280]{1,0:T(8,128)(2,1)S(1)}, bf16[128,1280]{1,0:T(8,128)(2,1)S(1)}, u32[]{:S(2)}, u32[]{:S(2)}) collective-permute-start(bf16[128,1280]{1,0:T(8,128)(2,1)S(1)} %bitcast.83), channel_id=1, source_target_pairs={{0,64},{32,96},{64,0},{96,32},{1,65},{33,97},{65,1},{97,33},{2,66}... | collective-permute-start | bytes 983048 | tf_op jit(solution)/shard_map/ppermute | solution.py:559
  23.9 28.0 %collective-permute-start.6 = (bf16[128,1280]{1,0:T(8,128)(2,1)S(1)}, bf16[128,1280]{1,0:T(8,128)(2,1)S(1)}, u32[]{:S(2)}, u32[]{:S(2)}) collective-permute-start(bf16[128,1280]{1,0:T(8,128)(2,1)S(1)} %bitcast.84), channel_id=1, source_target_pairs={{0,96},{32,0},{64,32},{96,64},{1,97},{33,1},{65,33},{97,65},{2,98}... | collective-permute-start | bytes 983048 | tf_op jit(solution)/shard_map/ppermute | solution.py:559
  26.8 25.1 %collective-permute-start.1 = (bf16[320,256]{1,0:T(8,128)(2,1)}, bf16[320,256]{1,0:T(8,128)(2,1)}, u32[]{:S(2)}, u32[]{:S(2)}) collective-permute-start(bf16[320,256]{1,0:T(8,128)(2,1)} %get-tuple-element.89), channel_id=1, source_target_pairs={{0,32},{32,64},{64,96},{96,0},{1,33},{33,65},{65,97},{97,1},{2,34}... | collective-permute-start | bytes 491528 | tf_op jit(solution)/shard_map/ppermute | solution.py:559
  27.2 24.8 %collective-permute-start.2 = (bf16[320,256]{1,0:T(8,128)(2,1)}, bf16[320,256]{1,0:T(8,128)(2,1)}, u32[]{:S(2)}, u32[]{:S(2)}) collective-permute-start(bf16[320,256]{1,0:T(8,128)(2,1)} %get-tuple-element.90), channel_id=1, source_target_pairs={{0,64},{32,96},{64,0},{96,32},{1,65},{33,97},{65,1},{97,33},{2,66}... | collective-permute-start | bytes 491528 | tf_op jit(solution)/shard_map/ppermute | solution.py:559
  30.2 24.6 %copy-start.4 = (bf16[128,1280]{1,0:T(8,128)(2,1)}, bf16[128,1280]{1,0:T(8,128)(2,1)S(1)}, u32[]{:S(2)}) copy-start(bf16[128,1280]{1,0:T(8,128)(2,1)S(1)} %collective-permute-done.4.refs_5_) | copy-start | bytes 983044
  30.2 21.7 %collective-permute-start.3 = (bf16[320,256]{1,0:T(8,128)(2,1)S(1)}, bf16[320,256]{1,0:T(8,128)(2,1)}, u32[]{:S(2)}, u32[]{:S(2)}) collective-permute-start(bf16[320,256]{1,0:T(8,128)(2,1)S(1)} %get-tuple-element.87), channel_id=1, source_target_pairs={{0,96},{32,0},{64,32},{96,64},{1,97},{33,1},{65,33},{97,65},{2,98}... | collective-permute-start | bytes 491528 | tf_op jit(solution)/shard_map/ppermute | solution.py:559
  39.7 1.2 copy-start
  50.9 3.9 %copy-start.5 = (bf16[128,1280]{1,0:T(8,128)(2,1)}, bf16[128,1280]{1,0:T(8,128)(2,1)S(1)}, u32[]{:S(2)}) copy-start(bf16[128,1280]{1,0:T(8,128)(2,1)S(1)} %collective-permute-done.5.refs_6_) | copy-start | bytes 983044
  50.9 2.3 %collective-permute-start.7 = (bf16[128,1280]{1,0:T(8,128)(2,1)S(1)}, bf16[128,1280]{1,0:T(8,128)(2,1)S(1)}, u32[]{:S(2)}, u32[]{:S(2)}) collective-permute-start(bf16[128,1280]{1,0:T(8,128)(2,1)S(1)} %bitcast.85), channel_id=1, source_target_pairs={{0,1},{1,0},{2,3},{3,2},{4,5},{5,4},{6,7},{7,6},{8,9},{9,8},{10,11... | collective-permute-start | bytes 983048 | tf_op jit(solution)/shard_map/ppermute | solution.py:554
  51.9 2.9 %copy-start.6 = (bf16[128,1280]{1,0:T(8,128)(2,1)}, bf16[128,1280]{1,0:T(8,128)(2,1)S(1)}, u32[]{:S(2)}) copy-start(bf16[128,1280]{1,0:T(8,128)(2,1)S(1)} %collective-permute-done.6.refs_7_) | copy-start | bytes 983044
  51.9 1.9 %collective-permute-start.8 = (bf16[128,1280]{1,0:T(8,128)(2,1)S(1)}, bf16[128,1280]{1,0:T(8,128)(2,1)S(1)}, u32[]{:S(2)}, u32[]{:S(2)}) collective-permute-start(bf16[128,1280]{1,0:T(8,128)(2,1)S(1)} %collective-permute-done.4.refs_5_), channel_id=1, source_target_pairs={{0,1},{1,0},{2,3},{3,2},{4,5},{5,4},{6,7},{7,6},{8,9},{9,8},{10,11... | collective-permute-start | bytes 983048 | tf_op jit(solution)/shard_map/ppermute | solution.py:554
  52.2 2.1 %collective-permute-start.9 = (bf16[128,1280]{1,0:T(8,128)(2,1)S(1)}, bf16[128,1280]{1,0:T(8,128)(2,1)S(1)}, u32[]{:S(2)}, u32[]{:S(2)}) collective-permute-start(bf16[128,1280]{1,0:T(8,128)(2,1)S(1)} %collective-permute-done.5.refs_6_), channel_id=1, source_target_pairs={{0,1},{1,0},{2,3},{3,2},{4,5},{5,4},{6,7},{7,6},{8,9},{9,8},{10,11... | collective-permute-start | bytes 983048 | tf_op jit(solution)/shard_map/ppermute | solution.py:554
  52.7 2.1 %collective-permute-start.10 = (bf16[128,1280]{1,0:T(8,128)(2,1)S(1)}, bf16[128,1280]{1,0:T(8,128)(2,1)S(1)}, u32[]{:S(2)}, u32[]{:S(2)}) collective-permute-start(bf16[128,1280]{1,0:T(8,128)(2,1)S(1)} %collective-permute-done.6.refs_7_), channel_id=1, source_target_pairs={{0,1},{1,0},{2,3},{3,2},{4,5},{5,4},{6,7},{7,6},{8,9},{9,8},{10,11... | collective-permute-start | bytes 983048 | tf_op jit(solution)/shard_map/ppermute | solution.py:554
  53.2 1.6 %copy-start.7 = (bf16[128,1280]{1,0:T(8,128)(2,1)}, bf16[128,1280]{1,0:T(8,128)(2,1)S(1)}, u32[]{:S(2)}) copy-start(bf16[128,1280]{1,0:T(8,128)(2,1)S(1)} %collective-permute-done.7.refs_8_) | copy-start | bytes 983044
  53.8 1.0 copy-start.8
  54.3 0.7 copy-start.9
  55.0 0.7 copy-start.10
  59.6 35.5 %all-to-all-start.2 = ((bf16[8,1184,128]{2,1,0:T(8,128)(2,1)}), bf16[8,1184,128]{2,1,0:T(8,128)(2,1)S(1)}, u32[]{:S(2)}, u32[]{:S(2)}) async-start(bf16[8,1184,128]{2,1,0:T(8,128)(2,1)} %weight.1), calls=%async_computation.2 | async-start | bytes 4849664 | tf_op jit(solution)/shard_map/all_to_all | solution.py:550
  95.1 18.1 %copy-start.1 = (bf16[8,1184,128]{2,1,0:T(8,128)(2,1)}, bf16[8,1184,128]{2,1,0:T(8,128)(2,1)S(1)}, u32[]{:S(2)}) copy-start(bf16[8,1184,128]{2,1,0:T(8,128)(2,1)S(1)} %all-to-all-done.2.mine) | copy-start | bytes 7274500
  95.1 18.1 %collective-permute-start.11 = (bf16[8,1184,128]{2,1,0:T(8,128)(2,1)S(1)}, bf16[8,1184,128]{2,1,0:T(8,128)(2,1)}, u32[]{:S(2)}, u32[]{:S(2)}) collective-permute-start(bf16[8,1184,128]{2,1,0:T(8,128)(2,1)S(1)} %all-to-all-done.2.mine), channel_id=1, source_target_pairs={{0,1},{1,0},{2,3},{3,2},{4,5},{5,4},{6,7},{7,6},{8,9},{9,8},{10,11... | collective-permute-start | bytes 7274504 | tf_op jit(solution)/shard_map/ppermute | solution.py:554
  96.1 23.0 %all-to-all-start.1 = ((bf16[16,288,128]{2,1,0:T(8,128)(2,1)}), bf16[16,288,128]{2,1,0:T(8,128)(2,1)}, u32[]{:S(2)}, u32[]{:S(2)}) async-start(bf16[16,288,128]{2,1,0:T(8,128)(2,1)} %image_pairs.1), calls=%async_computation.1 | async-start | bytes 2359296 | tf_op jit(solution)/shard_map/all_to_all | solution.py:550
  100.6 7.1 %collective-permute-start.12 = (bf16[400,128]{1,0:T(8,128)(2,1)S(1)}, bf16[400,128]{1,0:T(8,128)(2,1)S(1)}, u32[]{:S(2)}, u32[]{:S(2)}) collective-permute-start(bf16[400,128]{1,0:T(8,128)(2,1)S(1)} %slice_reduce_fusion), channel_id=1, source_target_pairs={{0,32},{32,64},{64,96},{96,0},{1,33},{33,65},{65,97},{97,1},{2,34}... | collective-permute-start | bytes 307208 | tf_op jit(solution)/shard_map/ppermute | solution.py:559
  102.0 8.9 %collective-permute-start.13 = (bf16[400,128]{1,0:T(8,128)(2,1)S(1)}, bf16[400,128]{1,0:T(8,128)(2,1)S(1)}, u32[]{:S(2)}, u32[]{:S(2)}) collective-permute-start(bf16[400,128]{1,0:T(8,128)(2,1)S(1)} %slice_reduce_fusion), channel_id=1, source_target_pairs={{0,64},{32,96},{64,0},{96,32},{1,65},{33,97},{65,1},{97,33},{2,66}... | collective-permute-start | bytes 307208 | tf_op jit(solution)/shard_map/ppermute | solution.py:559
  105.7 5.8 %collective-permute-start.14 = (bf16[400,128]{1,0:T(8,128)(2,1)S(1)}, bf16[400,128]{1,0:T(8,128)(2,1)S(1)}, u32[]{:S(2)}, u32[]{:S(2)}) collective-permute-start(bf16[400,128]{1,0:T(8,128)(2,1)S(1)} %slice_reduce_fusion), channel_id=1, source_target_pairs={{0,96},{32,0},{64,32},{96,64},{1,97},{33,1},{65,33},{97,65},{2,98}... | collective-permute-start | bytes 307208 | tf_op jit(solution)/shard_map/ppermute | solution.py:559
  106.0 15.7 %collective-permute-start.15 = (bf16[400,128]{1,0:T(8,128)(2,1)S(1)}, bf16[400,128]{1,0:T(8,128)(2,1)S(1)}, u32[]{:S(2)}, u32[]{:S(2)}) collective-permute-start(bf16[400,128]{1,0:T(8,128)(2,1)S(1)} %slice_reduce_fusion), channel_id=1, source_target_pairs={{0,16},{16,0},{32,48},{48,32},{64,80},{80,64},{96,112},{112,96},{1... | collective-permute-start | bytes 307208 | tf_op jit(solution)/shard_map/ppermute | solution.py:629
  107.7 14.6 %collective-permute-start.16 = (bf16[400,128]{1,0:T(8,128)(2,1)S(1)}, bf16[400,128]{1,0:T(8,128)(2,1)S(1)}, u32[]{:S(2)}, u32[]{:S(2)}) collective-permute-start(bf16[400,128]{1,0:T(8,128)(2,1)S(1)} %slice_reduce_fusion), channel_id=1, source_target_pairs={{0,48},{16,32},{32,80},{48,64},{64,112},{80,96},{96,16},{112,0},{1... | collective-permute-start | bytes 307208 | tf_op jit(solution)/shard_map/ppermute | solution.py:629
  110.9 13.2 %collective-permute-start.17 = (bf16[400,128]{1,0:T(8,128)(2,1)S(1)}, bf16[400,128]{1,0:T(8,128)(2,1)S(1)}, u32[]{:S(2)}, u32[]{:S(2)}) collective-permute-start(bf16[400,128]{1,0:T(8,128)(2,1)S(1)} %slice_reduce_fusion), channel_id=1, source_target_pairs={{0,80},{16,64},{32,112},{48,96},{64,16},{80,0},{96,48},{112,32},{1... | collective-permute-start | bytes 307208 | tf_op jit(solution)/shard_map/ppermute | solution.py:629
  111.4 12.8 %collective-permute-start.18 = (bf16[400,128]{1,0:T(8,128)(2,1)S(1)}, bf16[400,128]{1,0:T(8,128)(2,1)S(1)}, u32[]{:S(2)}, u32[]{:S(2)}) collective-permute-start(bf16[400,128]{1,0:T(8,128)(2,1)S(1)} %slice_reduce_fusion), channel_id=1, source_target_pairs={{0,112},{16,96},{32,16},{48,0},{64,48},{80,32},{96,80},{112,64},{1... | collective-permute-start | bytes 307208 | tf_op jit(solution)/shard_map/ppermute | solution.py:629
